TPU v7x, 32 devices: a whole 2x2x4 slice. The times are simulated.
32 devices in a mesh: ctx: 8 (over z, x), tp: 4 (over y, core).
Axes of the slice: x: 2, y: 2, z: 4, core: 2. Of those that a mesh axis runs over, the one named last changes fastest.
Arguments:
- hidden_states: bfloat16 [768, 8192], P('ctx', 'tp'), may hold values from -6 to 6
- counts: int32 [8], P('ctx'), may hold values from 24 to 72, as said below
- selected: int32 [8, 72], P('ctx'), may hold values from 0 to 95, as said below
- router_weight: float32 [768], P('ctx'), may hold values from 0.25 to 1.5
- norm_gain: float32 [8192], P('tp'), may hold values from 0.25 to 1.75
- w_gate: bfloat16 [8192, 28672], P('tp', 'ctx'), may hold values from -0.0625 to 0.0625
- w_up: bfloat16 [8192, 28672], P('tp', 'ctx'), may hold values from -0.0625 to 0.0625
- w_down: bfloat16 [28672, 8192], P('ctx', 'tp'), may hold values from -0.03125 to 0.03125
Outputs:
- block_out: bfloat16 [768, 8192], P('ctx', 'tp')
Inputs may be any that keep to these rules, and one draw needn't show every extreme that they name: The counts sum to 384; for every shard s the counts of the shards before s sum to between s * 48 - 48 // 4 and s * 48 + 48 // 4. `selected`: the entries of a row are distinct; only the first counts[s] entries of row s are used.
All inputs are finite; a program needn't handle non-finite values.
Results may differ from a plain program's by a relative error of at most 0.014.
Values may be sent and summed in bfloat16 or wider, within the bound.
No kernel may reach another device: no remote copies, remote signals or barrier semaphores. Data moves between devices by JAX's collectives and lax.ppermute only.
A program may use at most 128 MiB of HBM per device.

v0:
```python
import jax
import jax.numpy as jnp
from jax import lax
from jax.sharding import PartitionSpec as P

D = 8192


def body(hidden_states, counts, selected, router_weight, norm_gain, w_gate, w_up, w_down):
    chosen = selected[0]
    how_many = counts[0]
    most_rows = chosen.shape[0]
    tok_local = hidden_states.shape[0]
    active = jnp.arange(most_rows, dtype=jnp.int32) < how_many
    picked_f = hidden_states[chosen].astype(jnp.float32)
    squares = jnp.sum(picked_f * picked_f, axis=-1)
    totals = lax.psum(squares, "tp")
    mean_sq = totals / D
    scaled = picked_f * lax.rsqrt(mean_sq + 1e-05)[:, None] * norm_gain[None, :]
    normed = jnp.where(active[:, None], scaled, 0.0).astype(jnp.bfloat16)
    piece = lax.all_gather(normed, "ctx", axis=0, tiled=True)
    gate_part = jnp.dot(piece, w_gate, preferred_element_type=jnp.float32)
    up_part = jnp.dot(piece, w_up, preferred_element_type=jnp.float32)
    partial_units = jnp.stack([gate_part, up_part], axis=1)
    shares = lax.psum_scatter(
        partial_units.astype(jnp.bfloat16), "tp", scatter_dimension=2, tiled=True
    ).astype(jnp.float32)
    hidden_share = (jax.nn.silu(shares[:, 0]) * shares[:, 1]).astype(jnp.bfloat16)
    hidden = lax.all_gather(hidden_share, "tp", axis=1, tiled=True)
    ffn_block = lax.psum_scatter(
        jnp.dot(hidden, w_down, preferred_element_type=jnp.float32).astype(jnp.bfloat16),
        "ctx",
        scatter_dimension=0,
        tiled=True,
    )
    scale_rows = router_weight[chosen] * active.astype(jnp.float32)
    delta = ffn_block.astype(jnp.float32) * scale_rows[:, None]
    onehot = (jnp.arange(tok_local, dtype=jnp.int32)[:, None] == chosen[None, :]).astype(
        jnp.float32
    )
    added = jnp.dot(
        onehot, delta, precision=lax.Precision.HIGHEST, preferred_element_type=jnp.float32
    )
    return (hidden_states.astype(jnp.float32) + added).astype(jnp.bfloat16)


def solution(mesh):
    placed = (
        P("ctx", "tp"),
        P("ctx"),
        P("ctx", None),
        P("ctx"),
        P("tp"),
        P("tp", "ctx"),
        P("tp", "ctx"),
        P("ctx", "tp"),
    )
    return jax.shard_map(
        body, mesh=mesh, in_specs=placed, out_specs=P("ctx", "tp"), check_vma=False
    )
```

profile of v0, /device:TPU:0, one launch (start us, length us, event | category | flops | bytes accessed | tf_op | source)
XLA Modules:
  0.0 358.7 jit_solution(160952739863638929)
XLA Ops:
  6.5 0.0 copy-start
  6.5 0.0 all-gather.3.cloned.1.call-start
  7.2 0.7 fusion.13
  7.9 2.1 gather_fusion
  10.0 0.2 fusion.5
  10.1 8.4 %psum.7 = f32[72]{0:T(128)S(1)} all-reduce(f32[72]{0:T(128)S(1)} %fusion.5), channel_id=1, replica_groups=mesh['ctx'=8,'tp'=4] {'tp'}, use_global_device_ids=true, to_apply=%region_1.0 | all-reduce | flops 72 | bytes 576 | tf_op jit(solution)/shard_map/psum | solution.py:17
  18.5 1.6 fusion.8
  20.1 0.0 all-gather.3.cloned.1.call-update
  20.1 0.0 reduce-scatter.7.cloned.1.call-start
  20.1 52.5 %all-gather.3.cloned.1.call-done = bf16[576,2048]{1,0:T(8,128)(2,1)} async-done(((bf16[72,2048]{1,0:T(8,128)(2,1)}), bf16[576,2048]{1,0:T(8,128)(2,1)}) %all-gather.3.cloned.1.call-update) | async-done | bytes 2359312 | tf_op jit(solution)/shard_map/all_gather | solution.py:21
  72.6 0.0 copy-start.3
  72.6 14.7 %fusion.1 = bf16[576,1,3584]{2,0,1:T(8,128)(2,1)S(1)} fusion(bf16[576,2048]{1,0:T(8,128)(2,1)} %all-gather.3.cloned.1.call-done, bf16[2048,3584]{1,0:T(8,128)(2,1)} %param.14), kind=kOutput, calls=%fused_computation.6 | convolution fusion | flops 8457781248 | bytes 21168128 | tf_op jit(solution)/shard_map/dot_general | solution.py:23
  87.3 0.0 copy-done.3
  87.3 13.3 %fusion = bf16[576,1,3584]{2,0,1:T(8,128)(2,1)} fusion(bf16[576,2048]{1,0:T(8,128)(2,1)S(1)} %copy-done.3, bf16[2048,3584]{1,0:T(8,128)(2,1)} %param.13), kind=kOutput, calls=%fused_computation.5 | convolution fusion | flops 8457781248 | bytes 21168128 | tf_op jit(solution)/shard_map/dot_general | solution.py:22
  100.7 6.1 %pad_maximum_fusion = bf16[576,2,3584]{2,0,1:T(8,128)(2,1)} fusion(bf16[576,1,3584]{2,0,1:T(8,128)(2,1)S(1)} %fusion.1, bf16[576,1,3584]{2,0,1:T(8,128)(2,1)} %fusion), kind=kLoop, calls=%fused_computation.2 | loop fusion | flops 4128768 | bytes 16515072 | tf_op jit(solution)/shard_map/stack | solution.py:24
  106.8 23.1 %copy.9 = bf16[576,2,3584]{0,1,2:T(2,128)(2,1)} copy(bf16[576,2,3584]{2,0,1:T(8,128)(2,1)} %pad_maximum_fusion) | data formatting | bytes 16515072
  129.9 18.3 %reshape.55 = bf16[3584,1152]{1,0:T(8,128)(2,1)} reshape(bf16[3584,2,576]{2,1,0:T(2,128)(2,1)} %bitcast.31) | data formatting | bytes 16515072
  148.3 0.0 reduce-scatter.7.cloned.1.call-update
  148.3 0.2 all-gather.5.cloned.1.call-start
  148.5 69.4 %reduce-scatter.7.cloned.1.call-done = bf16[896,1152]{1,0:T(8,128)(2,1)} async-done(((bf16[3584,1152]{1,0:T(8,128)(2,1)}), bf16[896,1152]{1,0:T(8,128)(2,1)}) %reduce-scatter.7.cloned.1.call-update) | async-done | bytes 2064400
  217.9 5.1 %reshape.56 = bf16[896,2,576]{2,1,0:T(2,128)(2,1)S(1)} reshape(bf16[896,1152]{1,0:T(8,128)(2,1)} %reduce-scatter.7.cloned.1.call-done) | data formatting | bytes 4128768
  223.0 5.8 %copy.10 = bf16[576,2,896]{2,0,1:T(8,128)(2,1)} copy(bf16[576,2,896]{0,1,2:T(2,128)(2,1)S(1)} %bitcast.32) | data formatting | bytes 4128768
  228.8 1.8 convert_element_type.30
  230.7 1.6 fusion.4
  232.2 0.0 all-gather.5.cloned.1.call-update
  232.3 0.0 copy-start.1
  232.3 0.0 copy-start.2
  232.3 0.0 reduce-scatter.5.cloned.1.call-start
  232.3 34.2 %all-gather.5.cloned.1.call-done = bf16[576,3584]{1,0:T(8,128)(2,1)} async-done(((bf16[576,896]{1,0:T(8,128)(2,1)}), bf16[576,3584]{1,0:T(8,128)(2,1)}) %all-gather.5.cloned.1.call-update) | async-done | bytes 4128784 | tf_op jit(solution)/shard_map/all_gather | solution.py:29
  266.5 14.2 %convolution_convert_fusion.2 = bf16[576,2048]{1,0:T(8,128)(2,1)} fusion(bf16[576,3584]{1,0:T(8,128)(2,1)} %all-gather.5.cloned.1.call-done, bf16[3584,2048]{1,0:T(8,128)(2,1)} %param.15), kind=kOutput, calls=%fused_computation.7 | convolution fusion | flops 8456896512 | bytes 21168128 | tf_op jit(solution)/shard_map/dot_general | solution.py:31
  280.7 0.0 reduce-scatter.5.cloned.1.call-update
  280.7 0.0 copy-done
  280.7 1.2 gather_fusion.1
  282.0 67.8 %reduce-scatter.5.cloned.1.call-done = bf16[72,2048]{1,0:T(8,128)(2,1)} async-done(((bf16[576,2048]{1,0:T(8,128)(2,1)}), bf16[72,2048]{1,0:T(8,128)(2,1)}) %reduce-scatter.5.cloned.1.call-update) | async-done | bytes 294928 | tf_op jit(solution)/shard_map/reduce_scatter | solution.py:30
  349.8 0.0 copy-done.1
  349.8 0.0 copy-done.2
  349.8 2.3 fusion.2
  (4 shorter events, 0.0 us)
Async XLA Ops:
  6.5 274.2 %copy-start = (f32[96]{0:T(128)S(1)}, f32[96]{0:T(128)}, u32[]{:S(2)}) copy-start(f32[96]{0:T(128)} %param.11) | copy-start | bytes 1156
  6.5 66.1 %all-gather.3.cloned.1.call-start = ((), (), s32[]{:S(2)}) async-start(), calls=%async_computation.2 | async-start | bytes 2654208 | tf_op jit(solution)/shard_map/all_gather | solution.py:21
  20.1 197.8 %reduce-scatter.7.cloned.1.call-start = ((), (), s32[]{:S(2)}) async-start(), calls=%async_computation.5 | async-start | bytes 10321920
  72.6 14.7 %copy-start.3 = (bf16[576,2048]{1,0:T(8,128)(2,1)S(1)}, bf16[576,2048]{1,0:T(8,128)(2,1)}, u32[]{:S(2)}) copy-start(bf16[576,2048]{1,0:T(8,128)(2,1)} %all-gather.3.cloned.1.call-done) | copy-start | bytes 7077892
  148.3 118.2 %all-gather.5.cloned.1.call-start = ((), (), s32[]{:S(2)}) async-start(), calls=%async_computation.3 | async-start | bytes 5160960 | tf_op jit(solution)/shard_map/all_gather | solution.py:29
  232.3 117.6 %copy-start.1 = (bf16[96,2048]{1,0:T(8,128)(2,1)S(1)}, bf16[96,2048]{1,0:T(8,128)(2,1)}, u32[]{:S(2)}) copy-start(bf16[96,2048]{1,0:T(8,128)(2,1)} %param.8) | copy-start | bytes 1179652
  232.3 117.6 %copy-start.2 = (s32[1,72]{1,0:T(1,128)S(1)}, s32[1,72]{1,0:T(1,128)}, u32[]{:S(2)}) copy-start(s32[1,72]{1,0:T(1,128)} %param.10) | copy-start | bytes 868
  232.3 117.5 %reduce-scatter.5.cloned.1.call-start = ((), (), s32[]{:S(2)}) async-start(), calls=%async_computation.4 | async-start | bytes 2654208 | tf_op jit(solution)/shard_map/reduce_scatter | solution.py:30
Sparse Core Ops, SparseCore 0:
  20.2 52.3 all-gather.2
  148.4 69.4 reduce-scatter.6
  232.4 34.0 all-gather.4
  280.8 68.9 reduce-scatter.4
where the time goes:
time: 360 us; the launch traced here: 359 us
  waiting for transfers between devices  224 us (62%)
  local copies, waits for them, and re-layouts  55.7 us (15%)
  matrix products  44.6 us (12%)
  between operations  13.9 us (4%)
  other arithmetic  12 us (3%)
  blocking collectives  8.36 us (2%)
    unnamed x5, waiting for transfers between devices  69.5 us
    reduce_scatter x1, waiting for transfers between devices, body(): lax.psum_scatter(jnp.dot(hidden, w_down, preferred_element_type=jnp.float...  67.8 us
    all_gather x1, waiting for transfers between devices, body(): piece = lax.all_gather(normed, 'ctx', axis=0, tiled=True)  52.5 us
    unnamed x12, local copies, waits for them, and re-layouts  52.4 us
    all_gather x1, waiting for transfers between devices, body(): hidden = lax.all_gather(hidden_share, 'tp', axis=1, tiled=True)  34.2 us
    dot_general x1, matrix products, body(): up_part = jnp.dot(piece, w_up, preferred_element_type=jnp.float32)  14.7 us
    dot_general x1, matrix products, body(): jnp.dot(hidden, w_down, preferred_element_type=jnp.float32)  14.2 us
    dot_general x1, matrix products, body(): gate_part = jnp.dot(piece, w_gate, preferred_element_type=jnp.float32)  13.3 us
  transfers between devices with their start and end apart: 4, of which 4 were waited for; matrix products, arithmetic and copies ran while one was open for 0% of the time, Pallas kernels for 0%

commit v1 on v0

v1 whole, which is shorter than its diff:
```python
import functools

import jax
import jax.numpy as jnp
from jax import lax
from jax.experimental import pallas as pl
from jax.experimental.pallas import tpu as pltpu
from jax.sharding import PartitionSpec as P

D = 8192
SEL = 48
SURE = SEL // 2
SLACK = SEL // 4
GROUP = 4
EPS = 1e-05
MIB = 1 << 20
F32 = jnp.float32
BF16 = jnp.bfloat16


def swap(value, axis, size, bit):
    return lax.ppermute(value, axis, [(i, i ^ bit) for i in range(size)])


def gate_up_kernel(me_ref, x_ref, g_ref, u_ref, send_ref, keep_ref):
    width = g_ref.shape[1]

    def fill(out):
        x = x_ref[...]
        out[0, :, :width] = jnp.dot(x, g_ref[...], preferred_element_type=F32).astype(BF16)
        out[0, :, width:] = jnp.dot(x, u_ref[...], preferred_element_type=F32).astype(BF16)

    @pl.when(pl.program_id(0) == 0)
    def _():
        fill(send_ref)

    @pl.when(pl.program_id(0) == 1)
    def _():
        fill(keep_ref)


def gate_up(me, x, w_gate, w_up, tp):
    rows, feats = x.shape
    units = w_gate.shape[1]
    width = units // tp
    if width % 128:
        sums = [
            jnp.dot(x, w, preferred_element_type=F32).astype(BF16).reshape(rows, tp, width)
            for w in (w_gate, w_up)
        ]
        shares = jnp.concatenate(sums, axis=2).transpose(1, 0, 2)
        send, keep = (shares[(me[0] ^ k) ^ jnp.array([2, 0])] for k in (1, 0))
        return send, keep
    weight = pl.BlockSpec(
        (feats, width), lambda k, h, me: (0, me[0] ^ (1 - k) ^ (2 * (1 - h)))
    )
    half = jax.ShapeDtypeStruct((2, rows, 2 * width), BF16)
    return pl.pallas_call(
        gate_up_kernel,
        out_shape=(half, half),
        grid_spec=pltpu.PrefetchScalarGridSpec(
            num_scalar_prefetch=1,
            grid=(2, 2),
            in_specs=[pl.BlockSpec((rows, feats), lambda k, h, me: (0, 0)), weight, weight],
            out_specs=[
                pl.BlockSpec((1, rows, 2 * width), lambda k, h, me: (jnp.where(k == 0, h, 1), 0, 0)),
                pl.BlockSpec((1, rows, 2 * width), lambda k, h, me: (jnp.where(k == 0, 0, h), 0, 0)),
            ],
        ),
        compiler_params=pltpu.CompilerParams(vmem_limit_bytes=28 * MIB),
        cost_estimate=pl.CostEstimate(
            flops=4 * rows * feats * units, bytes_accessed=4 * feats * units, transcendentals=0
        ),
        name=f"gate_up_{rows}",
    )(me, x, w_gate, w_up)


def down_kernel(me_ref, h0, h1, h2, h3, w_ref, out_ref, acc):
    step = pl.program_id(0)
    for position, hidden in enumerate((h0, h1, h2, h3)):

        @pl.when(step == position)
        def _():
            term = jnp.dot(hidden[...], w_ref[...], preferred_element_type=F32)
            if position == 0:
                acc[...] = term
            elif position < 3:
                acc[...] += term
            else:
                out_ref[...] = (acc[...] + term).astype(BF16)


def down(me, hiddens, w_down):
    rows, width = hiddens[0].shape
    units, feats = w_down.shape
    whole = pl.BlockSpec((rows, width), lambda j, me: (0, 0))
    return pl.pallas_call(
        down_kernel,
        out_shape=jax.ShapeDtypeStruct((rows, feats), BF16),
        grid_spec=pltpu.PrefetchScalarGridSpec(
            num_scalar_prefetch=1,
            grid=(4,),
            in_specs=[whole] * 4
            + [pl.BlockSpec((width, feats), lambda j, me: (me[0] ^ (j // 2) ^ (2 * (j % 2)), 0))],
            out_specs=pl.BlockSpec((rows, feats), lambda j, me: (0, 0)),
            scratch_shapes=[pltpu.VMEM((rows, feats), F32)],
        ),
        compiler_params=pltpu.CompilerParams(vmem_limit_bytes=20 * MIB),
        cost_estimate=pl.CostEstimate(
            flops=2 * rows * feats * units, bytes_accessed=2 * feats * units, transcendentals=0
        ),
        name=f"down_{rows}",
    )(me, *hiddens, w_down)


def feed_forward(me, tp, x, gain, w_gate, w_up, w_down):
    xf = x.astype(F32)
    squares = jnp.sum(xf * xf, axis=-1)
    scaled = (xf * gain[None, :]).astype(BF16)
    send, keep = gate_up(me, scaled, w_gate, w_up, tp)
    squares = squares + swap(squares, "tp", tp, 1)
    got = swap(send, "tp", tp, 1)
    squares = squares + swap(squares, "tp", tp, 2)
    outgoing = (keep[0].astype(F32) + got[0].astype(F32)).astype(BF16)
    across = swap(outgoing, "tp", tp, 2)
    total = keep[1].astype(F32) + got[1].astype(F32) + across.astype(F32)
    total = total * lax.rsqrt(squares / D + EPS)[:, None]
    width = total.shape[1] // 2
    gate, up = total[:, :width], total[:, width:]
    own = (jax.nn.silu(gate) * up).astype(BF16)
    other_y = swap(own, "tp", tp, 2)
    other_core = swap(own, "tp", tp, 1)
    both = swap(other_y, "tp", tp, 1)
    return down(me, (own, other_y, other_core, both), w_down)


def gather_group(rows, n_ctx):
    return [rows] + [swap(rows, "ctx", n_ctx, j) for j in range(1, GROUP)]


def reduce_group(blocks, n_ctx):
    total = blocks[0].astype(F32)
    for j in range(1, GROUP):
        total = total + swap(blocks[j], "ctx", n_ctx, j).astype(F32)
    return total


def packing(extras, slots, window):
    starts = jnp.cumsum(extras) - extras
    slot = jnp.arange(slots, dtype=jnp.int32)[:, None, None]
    row = jnp.arange(window, dtype=jnp.int32)[None, None, :]
    hit = (slot == starts[None, :, None] + row) & (row < extras[None, :, None])
    return hit.astype(BF16).reshape(slots, GROUP * window)


def body(hidden_states, counts, selected, router_weight, norm_gain, w_gate, w_up, w_down, *, n_ctx, tp):
    me = lax.axis_index("tp").astype(jnp.int32).reshape(1)
    chosen = selected[0]
    count = counts[0]
    most = chosen.shape[0]
    tokens, feats = hidden_states.shape
    window = most - SURE
    payload = most + 8
    inner = min(2, n_ctx // GROUP - 1)
    slots = -(-(GROUP * (SEL - SURE) + SLACK * inner) // 16) * 16

    index = jnp.arange(payload, dtype=jnp.int32)
    listed = jnp.concatenate([chosen, jnp.zeros((payload - most,), jnp.int32)])
    active = (index < most) & (index < count)
    place = jnp.arange(tokens, dtype=jnp.int32)
    pick = ((listed[:, None] == place[None, :]) & active[:, None]).astype(BF16)
    rows = jnp.dot(pick, hidden_states, preferred_element_type=F32)
    rows = jnp.where((index == most)[:, None], count.astype(F32), rows).astype(BF16)
    sure, rest = rows[:SURE], rows[SURE:]

    def unpack(members):
        extras = jnp.stack([m[most - SURE, 0] for m in members]).astype(jnp.int32) - SURE
        map_ = packing(extras, slots, window)
        stacked = jnp.concatenate([m[:window] for m in members])
        return jnp.dot(map_, stacked, preferred_element_type=F32).astype(BF16), map_

    def spread(map_, partial):
        wide = jnp.dot(map_.T, partial, preferred_element_type=F32).astype(BF16)
        return [wide[j * window : (j + 1) * window] for j in range(GROUP)]

    def split(partial):
        return [partial[j * SURE : (j + 1) * SURE] for j in range(GROUP)]

    run = functools.partial(
        feed_forward, me, tp, gain=norm_gain, w_gate=w_gate, w_up=w_up, w_down=w_down
    )
    near_sure = jnp.concatenate(gather_group(sure, n_ctx))
    far_rows = [swap(rows, "ctx", n_ctx, d) for d in range(GROUP, n_ctx, GROUP)]
    near_rest, near_map = unpack(gather_group(rest, n_ctx))

    total_sure = reduce_group(split(run(near_sure)), n_ctx)
    total_rest = 0.0
    for number, mine in enumerate(far_rows):
        members = gather_group(mine, n_ctx)
        far_sure = jnp.concatenate([m[:SURE] for m in members])
        far_rest, far_map = unpack([m[SURE:] for m in members])
        partial = run(jnp.concatenate([far_sure, far_rest]))
        blocks = [
            jnp.concatenate(pair)
            for pair in zip(split(partial[: GROUP * SURE]), spread(far_map, partial[GROUP * SURE :]))
        ]
        summed = reduce_group(blocks, n_ctx).astype(BF16)
        back = swap(summed, "ctx", n_ctx, GROUP * (number + 1)).astype(F32)
        total_sure = total_sure + back[:SURE]
        total_rest = total_rest + back[SURE:]
    total_rest = total_rest + reduce_group(spread(near_map, run(near_rest)), n_ctx)

    ffn = jnp.concatenate([total_sure, total_rest]).astype(BF16)
    put = ((chosen[None, :] == place[:, None]) & active[None, :most]).astype(BF16)
    added = jnp.dot(put, ffn, preferred_element_type=F32) * router_weight[:, None]
    return (hidden_states.astype(F32) + added).astype(BF16)


def solution(mesh):
    placed = (
        P("ctx", "tp"),
        P("ctx"),
        P("ctx", None),
        P("ctx"),
        P("tp"),
        P("tp", "ctx"),
        P("tp", "ctx"),
        P("ctx", "tp"),
    )
    return jax.shard_map(
        functools.partial(body, n_ctx=mesh.shape["ctx"], tp=mesh.shape["tp"]),
        mesh=mesh,
        in_specs=placed,
        out_specs=P("ctx", "tp"),
        check_vma=False,
    )
```

time: 360 us -> 223 us (0.62)
  waiting for transfers between devices: 224 us -> 77 us
  Pallas kernels: 0 us -> 40.9 us
  matrix products: 44.6 us -> 6.41 us
  starting transfers between devices: 0.31 us -> 38.1 us
  local copies, waits for them, and re-layouts: 55.7 us -> 41.8 us
  between operations: 13.9 us -> 1.16 us
  blocking collectives: 8.36 us -> 0 us
  other arithmetic: 12 us -> 16.9 us
    all_gather x2 -> x0, waiting for transfers between devices: 86.6 us -> none  [the longest x1 52.5 us: body(): piece = lax.all_gather(normed, 'ctx', axis=0, tiled=True)]
    ppermute x0 -> x41, waiting for transfers between devices: none -> 77 us  [swap(): return lax.ppermute(value, axis, [(i, i ^ bit) for i in range(size)])]
    unnamed x5 -> x0, waiting for transfers between devices: 69.5 us -> none
    reduce_scatter x1 -> x0, waiting for transfers between devices: 67.8 us -> none  [body(): lax.psum_scatter(jnp.dot(hidden, w_down, preferred_element_type=jnp.float...]
    pallas_call x0 -> x6, Pallas kernels: none -> 40.9 us  [the longest x3 30.1 us: gate_up(): pl.pallas_call(gate_up_kernel, out_shape=(half, half), grid_spec=pltpu.Pr...]
    dot_general x4 -> x6, matrix products: 44.6 us -> 6.41 us  [the longest x2 2.57 us: unpack(): jnp.dot(map_, stacked, preferred_element_type=F32).astype(BF16)]
    ppermute x0 -> x41, starting transfers between devices: none -> 38.1 us  [swap(): return lax.ppermute(value, axis, [(i, i ^ bit) for i in range(size)])]
    unnamed x12 -> x44, local copies, waits for them, and re-layouts: 52.4 us -> 21.8 us
  transfers between devices with their start and end apart: 4 -> 41, of which waited for: 4 -> 12; matrix products, arithmetic and copies ran while one was open for 0% -> 20% of each run, Pallas kernels for 0% -> 16%
where the time goes in v1:
time: 223 us; the launch traced here: 222 us
  waiting for transfers between devices  77 us (35%)
  local copies, waits for them, and re-layouts  41.8 us (19%)
  Pallas kernels  40.9 us (18%)
  starting transfers between devices  38.1 us (17%)
  other arithmetic  16.9 us (8%)
  matrix products  6.41 us (3%)
    ppermute x41, waiting for transfers between devices, swap(): return lax.ppermute(value, axis, [(i, i ^ bit) for i in range(size)])  77 us
    ppermute x41, starting transfers between devices, swap(): return lax.ppermute(value, axis, [(i, i ^ bit) for i in range(size)])  38.1 us
    pallas_call x3, Pallas kernels, gate_up(): pl.pallas_call(gate_up_kernel, out_shape=(half, half), grid_spec=pltpu.Pr...  30.1 us
    unnamed x44, local copies, waits for them, and re-layouts  21.8 us
    pallas_call x3, Pallas kernels, down(): pl.pallas_call(down_kernel, out_shape=jax.ShapeDtypeStruct((rows, feats),...  10.8 us
    slice x10, local copies, waits for them, and re-layouts, unpack(): stacked = jnp.concatenate([m[:window] for m in members])  8.85 us
    slice x8, local copies, waits for them, and re-layouts, unpack(): m[most - SURE, 0]  7.84 us
    sub x2, other arithmetic, packing(): starts = jnp.cumsum(extras) - extras  5.24 us
  transfers between devices with their start and end apart: 41, of which 12 were waited for; matrix products, arithmetic and copies ran while one was open for 20% of the time, Pallas kernels for 16%

profile of v1, /device:TPU:0, one launch (start us, length us, event | category | flops | bytes accessed | tf_op | source)
XLA Modules:
  0.0 222.3 jit_solution(1355996575764270605)
XLA Ops:
  1.3 2.0 fusion.4
  4.2 4.0 %collective-permute-start.2 = (bf16[24,2048]{1,0:T(8,128)(2,1)S(1)}, bf16[24,2048]{1,0:T(8,128)(2,1)S(1)}, u32[]{:S(2)}, u32[]{:S(2)}) collective-permute-start(bf16[24,2048]{1,0:T(8,128)(2,1)S(1)} %slice.259), channel_id=1, source_target_pairs={{0,12},{4,8},{8,4},{12,0},{16,28},{20,24},{24,20},{28,16},{1,13},{... | collective-permute-start | bytes 294920 | tf_op jit(solution)/shard_map/ppermute | solution.py:22
  8.8 2.9 %collective-permute-start.13 = (bf16[80,2048]{1,0:T(8,128)(2,1)}, bf16[80,2048]{1,0:T(8,128)(2,1)}, u32[]{:S(2)}, u32[]{:S(2)}) collective-permute-start(bf16[80,2048]{1,0:T(8,128)(2,1)} %fusion.4), channel_id=1, source_target_pairs={{0,16},{4,20},{8,24},{12,28},{16,0},{20,4},{24,8},{28,12},{1,17},{... | collective-permute-start | bytes 983048 | tf_op jit(solution)/shard_map/ppermute | solution.py:22
  12.8 2.6 %collective-permute-start.30 = (bf16[56,2048]{1,0:T(8,128)(2,1)S(1)}, bf16[56,2048]{1,0:T(8,128)(2,1)S(1)}, u32[]{:S(2)}, u32[]{:S(2)}) collective-permute-start(bf16[56,2048]{1,0:T(8,128)(2,1)S(1)} %slice.296), channel_id=1, source_target_pairs={{0,12},{4,8},{8,4},{12,0},{16,28},{20,24},{24,20},{28,16},{1,13},{... | collective-permute-start | bytes 688136 | tf_op jit(solution)/shard_map/ppermute | solution.py:22
  15.8 2.0 collective-permute-done.1
  20.0 1.6 slice.300
  21.7 1.5 collective-permute-start.6
  23.2 5.2 %copy-done = bf16[2048,3584]{1,0:T(8,128)(2,1)S(1)} copy-done((bf16[2048,3584]{1,0:T(8,128)(2,1)S(1)}, bf16[2048,3584]{1,0:T(8,128)(2,1)}, u32[]{:S(2)}) %copy-start) | copy-done | bytes 14680088
  28.4 9.1 %gate_up_96.1 = (bf16[2,96,1792]{2,1,0:T(8,128)(2,1)S(1)}, bf16[2,96,1792]{2,1,0:T(8,128)(2,1)S(1)}) custom-call(s32[1]{0:T(128)} %bitcast.2.me_ref, bf16[96,2048]{1,0:T(8,128)(2,1)S(1)} %get-tuple-element.40.x_ref, bf16[2048,3584]{1,0:T(8,128)(2,1)S(1)} %copy-done, bf16[2048,3584]{1,0:T(8,128)(2,1)} %u_ref.5), custom_call_target="tpu_custom_call" | custom-call | flops 2818572288 | bytes 29360128 | tf_op jit(solution)/shard_map/gate_up_96/pallas_call | solution.py:58
  39.6 2.4 %convert_add_fusion = s32[4,1]{1,0:T(4,128)S(1)} fusion(bf16[1,1]{1,0:T(2,128)(2,1)} %slice.299, bf16[1,1]{1,0:T(2,128)(2,1)} %slice.298, bf16[1,1]{1,0:T(2,128)(2,1)} %slice.297, bf16[1,1]{1,0:T(2,128)(2,1)} %slice.295), kind=kLoop, calls=%fused_computation.90 | loop fusion | flops 36 | bytes 24 | tf_op jit(solution)/shard_map/sub | solution.py:177
  42.2 2.5 %fusion.65 = (s32[4]{0:T(128)S(1)}, s32[4]{0:T(128)S(1)}) fusion(s32[4]{0:T(128)S(1)} %reduce.3, bf16[1]{0:T(256)(128)(2,1)} %bitcast.14, bf16[1]{0:T(256)(128)(2,1)} %bitcast.13, bf16[1]{0:T(256)(128)(2,1)} %bitcast.12, bf16[1]{0:T(256)(128)(2,1)} %bitcast.11), kind=kLoop, calls=%fused_computation.108 | loop fusion | flops 40 | bytes 56 | tf_op jit(solution)/shard_map/sub | solution.py:149
  45.6 2.0 collective-permute-start.14
  47.7 1.5 collective-permute-start.16
  49.2 1.7 slice.276
  52.1 1.5 slice_dynamic-update-slice_fusion.3
  53.7 10.8 %collective-permute-done.16 = bf16[80,2048]{1,0:T(8,128)(2,1)} collective-permute-done((bf16[80,2048]{1,0:T(8,128)(2,1)}, bf16[80,2048]{1,0:T(8,128)(2,1)}, u32[]{:S(2)}, u32[]{:S(2)}) %collective-permute-start.16) | collective-permute-done | bytes 327712 | tf_op jit(solution)/shard_map/ppermute | solution.py:22
  68.1 2.7 %convert_add_fusion.1 = s32[4,1]{1,0:T(4,128)S(1)} fusion(bf16[1,1]{1,0:T(2,128)(2,1)} %slice.275, bf16[1,1]{1,0:T(2,128)(2,1)} %slice.274, bf16[1,1]{1,0:T(2,128)(2,1)} %slice.273, bf16[1,1]{1,0:T(2,128)(2,1)} %slice.272), kind=kLoop, calls=%fused_computation.91 | loop fusion | flops 36 | bytes 24 | tf_op jit(solution)/shard_map/sub | solution.py:177
  71.0 2.7 %fusion.67 = (s32[4]{0:T(128)S(1)}, s32[4]{0:T(128)S(1)}) fusion(s32[4]{0:T(128)S(1)} %reduce, bf16[1]{0:T(256)(128)(2,1)} %bitcast.8, bf16[1]{0:T(256)(128)(2,1)} %bitcast.7, bf16[1]{0:T(256)(128)(2,1)} %bitcast.6, bf16[1]{0:T(256)(128)(2,1)} %bitcast.5), kind=kLoop, calls=%fused_computation.109 | loop fusion | flops 40 | bytes 56 | tf_op jit(solution)/shard_map/sub | solution.py:149
  74.0 1.7 slice.279
  75.6 1.6 slice.278
  77.2 1.6 slice.277
  78.9 1.5 slice_dynamic-update-slice_fusion.2
  80.4 1.5 slice_dynamic-update-slice_fusion.1
  81.9 1.6 slice_dynamic-update-slice_fusion
  83.5 2.2 fusion.2
  85.7 1.5 fusion.6
  87.2 5.2 %copy-done.1 = bf16[2048,3584]{1,0:T(8,128)(2,1)S(1)} copy-done((bf16[2048,3584]{1,0:T(8,128)(2,1)S(1)}, bf16[2048,3584]{1,0:T(8,128)(2,1)}, u32[]{:S(2)}) %copy-start.1) | copy-done | bytes 14680088
  92.4 11.8 %gate_up_208.1 = (bf16[2,208,1792]{2,1,0:T(8,128)(2,1)S(1)}, bf16[2,208,1792]{2,1,0:T(8,128)(2,1)S(1)}) custom-call(s32[1]{0:T(128)} %bitcast.2.me_ref, bf16[208,2048]{1,0:T(8,128)(2,1)S(1)} %get-tuple-element.28.x_ref, bf16[2048,3584]{1,0:T(8,128)(2,1)S(1)} %copy-done.1, bf16[2048,3584]{1,0:T(8,128)(2,1)} %u_ref.5), custom_call_target="tpu_custom_call" | custom-call | flops 6106906624 | bytes 29360128 | tf_op jit(solution)/shard_map/gate_up_208/pallas_call | solution.py:58
  105.3 9.2 %gate_up_112.1 = (bf16[2,112,1792]{2,1,0:T(8,128)(2,1)S(1)}, bf16[2,112,1792]{2,1,0:T(8,128)(2,1)S(1)}) custom-call(s32[1]{0:T(128)} %bitcast.2.me_ref, bf16[112,2048]{1,0:T(8,128)(2,1)S(1)} %get-tuple-element.22.x_ref, bf16[2048,3584]{1,0:T(8,128)(2,1)S(1)} %bitcast.35, bf16[2048,3584]{1,0:T(8,128)(2,1)} %u_ref.5), custom_call_target="tpu_custom_call" | custom-call | flops 3288334336 | bytes 29360128 | tf_op jit(solution)/shard_map/gate_up_112/pallas_call | solution.py:58
  115.6 1.5 collective-permute-start.20
  119.2 8.5 %collective-permute-done.4 = bf16[96,1792]{1,0:T(8,128)(2,1)S(1)} collective-permute-done((bf16[96,1792]{1,0:T(8,128)(2,1)S(1)}, bf16[96,1792]{1,0:T(8,128)(2,1)S(1)}, u32[]{:S(2)}, u32[]{:S(2)}) %collective-permute-start.4) | collective-permute-done | bytes 344096 | tf_op jit(solution)/shard_map/ppermute | solution.py:22
  129.7 1.5 collective-permute-start.32
  132.0 12.9 %collective-permute-done.32 = bf16[112,1792]{1,0:T(8,128)(2,1)S(1)} collective-permute-done((bf16[112,1792]{1,0:T(8,128)(2,1)S(1)}, bf16[112,1792]{1,0:T(8,128)(2,1)S(1)}, u32[]{:S(2)}, u32[]{:S(2)}) %collective-permute-start.32) | collective-permute-done | bytes 401440 | tf_op jit(solution)/shard_map/ppermute | solution.py:22
  145.9 15.1 %collective-permute-done.18 = bf16[208,1792]{1,0:T(8,128)(2,1)S(1)} collective-permute-done((bf16[208,1792]{1,0:T(8,128)(2,1)S(1)}, bf16[208,1792]{1,0:T(8,128)(2,1)S(1)}, u32[]{:S(2)}, u32[]{:S(2)}) %collective-permute-start.18) | collective-permute-done | bytes 745504 | tf_op jit(solution)/shard_map/ppermute | solution.py:22
  162.6 2.6 %collective-permute-done.35.h1 = bf16[112,896]{1,0:T(8,128)(2,1)S(1)} collective-permute-done((bf16[112,896]{1,0:T(8,128)(2,1)S(1)}, bf16[112,896]{1,0:T(8,128)(2,1)S(1)}, u32[]{:S(2)}, u32[]{:S(2)}) %collective-permute-start.35) | collective-permute-done | bytes 200736 | tf_op jit(solution)/shard_map/ppermute | solution.py:22
  165.3 5.2 %copy-done.2 = bf16[3584,2048]{1,0:T(8,128)(2,1)S(1)} copy-done((bf16[3584,2048]{1,0:T(8,128)(2,1)S(1)}, bf16[3584,2048]{1,0:T(8,128)(2,1)}, u32[]{:S(2)}) %copy-start.2) | copy-done | bytes 14680088
  170.4 3.2 %down_96.1 = bf16[96,2048]{1,0:T(8,128)(2,1)S(1)} custom-call(s32[1]{0:T(128)} %bitcast.2.me_ref, bf16[96,896]{1,0:T(8,128)(2,1)S(1)} %fusion.33.h0, bf16[96,896]{1,0:T(8,128)(2,1)S(1)} %collective-permute-done.7.h1, bf16[96,896]{1,0:T(8,128)(2,1)S(1)} %collective-permute-done.8.h2, bf16[96,896]{1,0:T(8,128)(2,1)S(1)} %collective-permute-done.9.h3, ...), custom_call_target="tpu_custom_call" | custom-call | flops 1409286144 | bytes 14680064 | tf_op jit(solution)/shard_map/down_96/pallas_call | solution.py:97
  174.3 3.1 %down_112.1 = bf16[112,2048]{1,0:T(8,128)(2,1)S(1)} custom-call(s32[1]{0:T(128)} %bitcast.2.me_ref, bf16[112,896]{1,0:T(8,128)(2,1)S(1)} %fusion.30.h0, bf16[112,896]{1,0:T(8,128)(2,1)S(1)} %collective-permute-done.35.h1, bf16[112,896]{1,0:T(8,128)(2,1)S(1)} %collective-permute-done.36.h2, bf16[112,896]{1,0:T(8,128)(2,1)S(1)} %collective-permute-done.37.h3, ...), custom_call_target="tpu_custom_call" | custom-call | flops 1644167168 | bytes 14680064 | tf_op jit(solution)/shard_map/down_112/pallas_call | solution.py:97
  177.9 4.5 %down_208.1 = bf16[208,2048]{1,0:T(8,128)(2,1)S(1)} custom-call(s32[1]{0:T(128)} %bitcast.2.me_ref, bf16[208,896]{1,0:T(8,128)(2,1)S(1)} %fusion.26.h0, bf16[208,896]{1,0:T(8,128)(2,1)S(1)} %collective-permute-done.21.h1, bf16[208,896]{1,0:T(8,128)(2,1)S(1)} %collective-permute-done.22.h2, bf16[208,896]{1,0:T(8,128)(2,1)S(1)} %collective-permute-done.23.h3, ...), custom_call_target="tpu_custom_call" | custom-call | flops 3053453312 | bytes 14680064 | tf_op jit(solution)/shard_map/down_208/pallas_call | solution.py:97
  184.5 1.8 collective-permute-start.25
  188.3 1.7 collective-permute-start.39
  190.0 3.8 %collective-permute-done.26 = bf16[72,2048]{1,0:T(8,128)(2,1)S(1)} collective-permute-done((bf16[72,2048]{1,0:T(8,128)(2,1)S(1)}, bf16[72,2048]{1,0:T(8,128)(2,1)S(1)}, u32[]{:S(2)}, u32[]{:S(2)}) %collective-permute-start.26) | collective-permute-done | bytes 294944 | tf_op jit(solution)/shard_map/ppermute | solution.py:22
  193.8 1.7 collective-permute-start.38
  195.5 4.9 %collective-permute-done.25 = bf16[72,2048]{1,0:T(8,128)(2,1)S(1)} collective-permute-done((bf16[72,2048]{1,0:T(8,128)(2,1)S(1)}, bf16[72,2048]{1,0:T(8,128)(2,1)S(1)}, u32[]{:S(2)}, u32[]{:S(2)}) %collective-permute-start.25) | collective-permute-done | bytes 294944 | tf_op jit(solution)/shard_map/ppermute | solution.py:22
  200.7 2.7 %collective-permute-start.12 = (bf16[24,2048]{1,0:T(8,128)(2,1)S(1)}, bf16[24,2048]{1,0:T(8,128)(2,1)S(1)}, u32[]{:S(2)}, u32[]{:S(2)}) collective-permute-start(bf16[24,2048]{1,0:T(8,128)(2,1)S(1)} %get-tuple-element.37), channel_id=1, source_target_pairs={{0,12},{4,8},{8,4},{12,0},{16,28},{20,24},{24,20},{28,16},{1,13},{... | collective-permute-start | bytes 294920 | tf_op jit(solution)/shard_map/ppermute | solution.py:22
  203.4 13.1 %collective-permute-done.27 = bf16[72,2048]{1,0:T(8,128)(2,1)S(1)} collective-permute-done((bf16[72,2048]{1,0:T(8,128)(2,1)S(1)}, bf16[72,2048]{1,0:T(8,128)(2,1)S(1)}, u32[]{:S(2)}, u32[]{:S(2)}) %collective-permute-start.27) | collective-permute-done | bytes 294944 | tf_op jit(solution)/shard_map/ppermute | solution.py:22
  216.5 1.6 collective-permute-start.10
  218.3 2.8 %collective-permute-done.11 = bf16[24,2048]{1,0:T(8,128)(2,1)S(1)} collective-permute-done((bf16[24,2048]{1,0:T(8,128)(2,1)S(1)}, bf16[24,2048]{1,0:T(8,128)(2,1)S(1)}, u32[]{:S(2)}, u32[]{:S(2)}) %collective-permute-start.11) | collective-permute-done | bytes 98336 | tf_op jit(solution)/shard_map/ppermute | solution.py:22
  (161 shorter events, 30.8 us)
Async XLA Ops:
  4.2 11.1 %collective-permute-start.2 = (bf16[24,2048]{1,0:T(8,128)(2,1)S(1)}, bf16[24,2048]{1,0:T(8,128)(2,1)S(1)}, u32[]{:S(2)}, u32[]{:S(2)}) collective-permute-start(bf16[24,2048]{1,0:T(8,128)(2,1)S(1)} %slice.259), channel_id=1, source_target_pairs={{0,12},{4,8},{8,4},{12,0},{16,28},{20,24},{24,20},{28,16},{1,13},{... | collective-permute-start | bytes 294920 | tf_op jit(solution)/shard_map/ppermute | solution.py:22
  8.2 9.6 %collective-permute-start.1 = (bf16[24,2048]{1,0:T(8,128)(2,1)S(1)}, bf16[24,2048]{1,0:T(8,128)(2,1)S(1)}, u32[]{:S(2)}, u32[]{:S(2)}) collective-permute-start(bf16[24,2048]{1,0:T(8,128)(2,1)S(1)} %slice.259), channel_id=1, source_target_pairs={{0,8},{4,12},{8,0},{12,4},{16,24},{20,28},{24,16},{28,20},{1,9},{5... | collective-permute-start | bytes 294920 | tf_op jit(solution)/shard_map/ppermute | solution.py:22
  8.6 9.2 %collective-permute-start = (bf16[24,2048]{1,0:T(8,128)(2,1)S(1)}, bf16[24,2048]{1,0:T(8,128)(2,1)S(1)}, u32[]{:S(2)}, u32[]{:S(2)}) collective-permute-start(bf16[24,2048]{1,0:T(8,128)(2,1)S(1)} %slice.259), channel_id=1, source_target_pairs={{0,4},{4,0},{8,12},{12,8},{16,20},{20,16},{24,28},{28,24},{1,5},{5... | collective-permute-start | bytes 294920 | tf_op jit(solution)/shard_map/ppermute | solution.py:22
  8.8 36.8 %collective-permute-start.13 = (bf16[80,2048]{1,0:T(8,128)(2,1)}, bf16[80,2048]{1,0:T(8,128)(2,1)}, u32[]{:S(2)}, u32[]{:S(2)}) collective-permute-start(bf16[80,2048]{1,0:T(8,128)(2,1)} %fusion.4), channel_id=1, source_target_pairs={{0,16},{4,20},{8,24},{12,28},{16,0},{20,4},{24,8},{28,12},{1,17},{... | collective-permute-start | bytes 983048 | tf_op jit(solution)/shard_map/ppermute | solution.py:22
  12.8 25.1 %collective-permute-start.30 = (bf16[56,2048]{1,0:T(8,128)(2,1)S(1)}, bf16[56,2048]{1,0:T(8,128)(2,1)S(1)}, u32[]{:S(2)}, u32[]{:S(2)}) collective-permute-start(bf16[56,2048]{1,0:T(8,128)(2,1)S(1)} %slice.296), channel_id=1, source_target_pairs={{0,12},{4,8},{8,4},{12,0},{16,28},{20,24},{24,20},{28,16},{1,13},{... | collective-permute-start | bytes 688136 | tf_op jit(solution)/shard_map/ppermute | solution.py:22
  15.3 23.1 %collective-permute-start.29 = (bf16[56,2048]{1,0:T(8,128)(2,1)S(1)}, bf16[56,2048]{1,0:T(8,128)(2,1)S(1)}, u32[]{:S(2)}, u32[]{:S(2)}) collective-permute-start(bf16[56,2048]{1,0:T(8,128)(2,1)S(1)} %slice.296), channel_id=1, source_target_pairs={{0,8},{4,12},{8,0},{12,4},{16,24},{20,28},{24,16},{28,20},{1,9},{5... | collective-permute-start | bytes 688136 | tf_op jit(solution)/shard_map/ppermute | solution.py:22
  17.8 21.2 %collective-permute-start.28 = (bf16[56,2048]{1,0:T(8,128)(2,1)S(1)}, bf16[56,2048]{1,0:T(8,128)(2,1)S(1)}, u32[]{:S(2)}, u32[]{:S(2)}) collective-permute-start(bf16[56,2048]{1,0:T(8,128)(2,1)S(1)} %slice.296), channel_id=1, source_target_pairs={{0,4},{4,0},{8,12},{12,8},{16,20},{20,16},{24,28},{28,24},{1,5},{5... | collective-permute-start | bytes 688136 | tf_op jit(solution)/shard_map/ppermute | solution.py:22
  18.8 2.9 %collective-permute-start.5 = (f32[96]{0:T(128)S(1)}, f32[96]{0:T(128)S(1)}, u32[]{:S(2)}, u32[]{:S(2)}) collective-permute-start(f32[96]{0:T(128)S(1)} %get-tuple-element.39), channel_id=1, source_target_pairs={{0,1},{1,0},{2,3},{3,2},{4,5},{5,4},{6,7},{7,6},{8,9},{9,8},{10,11... | collective-permute-start | bytes 1160 | tf_op jit(solution)/shard_map/ppermute | solution.py:22
  21.7 15.8 %collective-permute-start.6 = (f32[96]{0:T(128)S(1)}, f32[96]{0:T(128)S(1)}, u32[]{:S(2)}, u32[]{:S(2)}) collective-permute-start(f32[96]{0:T(128)S(1)} %add.215), channel_id=1, source_target_pairs={{0,2},{1,3},{2,0},{3,1},{4,6},{5,7},{6,4},{7,5},{8,10},{9,11},{10,... | collective-permute-start | bytes 1160 | tf_op jit(solution)/shard_map/ppermute | solution.py:22
  37.5 79.6 %collective-permute-start.3 = (bf16[2,96,1792]{2,1,0:T(8,128)(2,1)S(1)}, bf16[2,96,1792]{2,1,0:T(8,128)(2,1)}, u32[]{:S(2)}, u32[]{:S(2)}) collective-permute-start(bf16[2,96,1792]{2,1,0:T(8,128)(2,1)S(1)} %get-tuple-element.12), channel_id=1, source_target_pairs={{0,1},{1,0},{2,3},{3,2},{4,5},{5,4},{6,7},{7,6},{8,9},{9,8},{10,11... | collective-permute-start | bytes 2064392 | tf_op jit(solution)/shard_map/ppermute | solution.py:22
  45.6 59.6 %slice-start = ((s8[14680064]{0:T(1024)(128)(4,1)}), s8[2097152]{0:T(1024)(128)(4,1)S(1)}, s32[]{:S(2)}) async-start(s8[14680064]{0:T(1024)(128)(4,1)} %bitcast.34), calls=%async_computation | async-start | bytes 4194304
  45.6 21.2 %collective-permute-start.14 = (bf16[80,2048]{1,0:T(8,128)(2,1)}, bf16[80,2048]{1,0:T(8,128)(2,1)}, u32[]{:S(2)}, u32[]{:S(2)}) collective-permute-start(bf16[80,2048]{1,0:T(8,128)(2,1)} %collective-permute-done.13), channel_id=1, source_target_pairs={{0,4},{4,0},{8,12},{12,8},{16,20},{20,16},{24,28},{28,24},{1,5},{5... | collective-permute-start | bytes 983048 | tf_op jit(solution)/shard_map/ppermute | solution.py:22
  47.7 17.9 %collective-permute-start.15 = (bf16[80,2048]{1,0:T(8,128)(2,1)}, bf16[80,2048]{1,0:T(8,128)(2,1)}, u32[]{:S(2)}, u32[]{:S(2)}) collective-permute-start(bf16[80,2048]{1,0:T(8,128)(2,1)} %collective-permute-done.13), channel_id=1, source_target_pairs={{0,8},{4,12},{8,0},{12,4},{16,24},{20,28},{24,16},{28,20},{1,9},{5... | collective-permute-start | bytes 983048 | tf_op jit(solution)/shard_map/ppermute | solution.py:22
  47.7 16.8 %collective-permute-start.16 = (bf16[80,2048]{1,0:T(8,128)(2,1)}, bf16[80,2048]{1,0:T(8,128)(2,1)}, u32[]{:S(2)}, u32[]{:S(2)}) collective-permute-start(bf16[80,2048]{1,0:T(8,128)(2,1)} %collective-permute-done.13), channel_id=1, source_target_pairs={{0,12},{4,8},{8,4},{12,0},{16,28},{20,24},{24,20},{28,16},{1,13},{... | collective-permute-start | bytes 983048 | tf_op jit(solution)/shard_map/ppermute | solution.py:22
  92.4 12.9 %slice-start.1 = ((s8[14680064]{0:T(1024)(128)(4,1)}), s8[4194304]{0:T(1024)(128)(4,1)S(1)}, s32[]{:S(2)}) async-start(s8[14680064]{0:T(1024)(128)(4,1)} %bitcast.34), calls=%async_computation.1 | async-start | bytes 8388608
  92.4 12.9 %slice-start.2 = ((s8[14680064]{0:T(1024)(128)(4,1)}), s8[4194304]{0:T(1024)(128)(4,1)S(1)}, s32[]{:S(2)}) async-start(s8[14680064]{0:T(1024)(128)(4,1)} %bitcast.34), calls=%async_computation.2 | async-start | bytes 8388608
  92.4 12.9 %slice-start.3 = ((s8[14680064]{0:T(1024)(128)(4,1)}), s8[4194304]{0:T(1024)(128)(4,1)S(1)}, s32[]{:S(2)}) async-start(s8[14680064]{0:T(1024)(128)(4,1)} %bitcast.34), calls=%async_computation.3 | async-start | bytes 8388608
  104.2 27.1 %collective-permute-start.17 = (bf16[2,208,1792]{2,1,0:T(8,128)(2,1)S(1)}, bf16[2,208,1792]{2,1,0:T(8,128)(2,1)S(1)}, u32[]{:S(2)}, u32[]{:S(2)}) collective-permute-start(bf16[2,208,1792]{2,1,0:T(8,128)(2,1)S(1)} %get-tuple-element.14), channel_id=1, source_target_pairs={{0,1},{1,0},{2,3},{3,2},{4,5},{5,4},{6,7},{7,6},{8,9},{9,8},{10,11... | collective-permute-start | bytes 4472840 | tf_op jit(solution)/shard_map/ppermute | solution.py:22
  104.3 11.4 %collective-permute-start.19 = (f32[208]{0:T(256)S(1)}, f32[208]{0:T(256)S(1)}, u32[]{:S(2)}, u32[]{:S(2)}) collective-permute-start(f32[208]{0:T(256)S(1)} %get-tuple-element.27), channel_id=1, source_target_pairs={{0,1},{1,0},{2,3},{3,2},{4,5},{5,4},{6,7},{7,6},{8,9},{9,8},{10,11... | collective-permute-start | bytes 2504 | tf_op jit(solution)/shard_map/ppermute | solution.py:22
  105.1 9.9 %collective-permute-start.33 = (f32[112]{0:T(128)S(1)}, f32[112]{0:T(128)S(1)}, u32[]{:S(2)}, u32[]{:S(2)}) collective-permute-start(f32[112]{0:T(128)S(1)} %get-tuple-element.21), channel_id=1, source_target_pairs={{0,1},{1,0},{2,3},{3,2},{4,5},{5,4},{6,7},{7,6},{8,9},{9,8},{10,11... | collective-permute-start | bytes 1352 | tf_op jit(solution)/shard_map/ppermute | solution.py:22
  114.5 15.1 %collective-permute-start.31 = (bf16[2,112,1792]{2,1,0:T(8,128)(2,1)S(1)}, bf16[2,112,1792]{2,1,0:T(8,128)(2,1)S(1)}, u32[]{:S(2)}, u32[]{:S(2)}) collective-permute-start(bf16[2,112,1792]{2,1,0:T(8,128)(2,1)S(1)} %get-tuple-element.16), channel_id=1, source_target_pairs={{0,1},{1,0},{2,3},{3,2},{4,5},{5,4},{6,7},{7,6},{8,9},{9,8},{10,11... | collective-permute-start | bytes 2408456 | tf_op jit(solution)/shard_map/ppermute | solution.py:22
  115.1 3.7 %collective-permute-start.34 = (f32[112]{0:T(128)S(1)}, f32[112]{0:T(128)S(1)}, u32[]{:S(2)}, u32[]{:S(2)}) collective-permute-start(f32[112]{0:T(128)S(1)} %add.248), channel_id=1, source_target_pairs={{0,2},{1,3},{2,0},{3,1},{4,6},{5,7},{6,4},{7,5},{8,10},{9,11},{10,... | collective-permute-start | bytes 1352 | tf_op jit(solution)/shard_map/ppermute | solution.py:22
  115.6 3.6 %collective-permute-start.20 = (f32[208]{0:T(256)S(1)}, f32[208]{0:T(256)S(1)}, u32[]{:S(2)}, u32[]{:S(2)}) collective-permute-start(f32[208]{0:T(256)S(1)} %add.232), channel_id=1, source_target_pairs={{0,2},{1,3},{2,0},{3,1},{4,6},{5,7},{6,4},{7,5},{8,10},{9,11},{10,... | collective-permute-start | bytes 2504 | tf_op jit(solution)/shard_map/ppermute | solution.py:22
  118.2 9.5 %collective-permute-start.4 = (bf16[96,1792]{1,0:T(8,128)(2,1)S(1)}, bf16[96,1792]{1,0:T(8,128)(2,1)S(1)}, u32[]{:S(2)}, u32[]{:S(2)}) collective-permute-start(bf16[96,1792]{1,0:T(8,128)(2,1)S(1)} %fusion.32), channel_id=1, source_target_pairs={{0,2},{1,3},{2,0},{3,1},{4,6},{5,7},{6,4},{7,5},{8,10},{9,11},{10,... | collective-permute-start | bytes 1032200 | tf_op jit(solution)/shard_map/ppermute | solution.py:22
  129.0 33.1 %collective-permute-start.7 = (bf16[96,896]{1,0:T(8,128)(2,1)S(1)}, bf16[96,896]{1,0:T(8,128)(2,1)S(1)}, u32[]{:S(2)}, u32[]{:S(2)}) collective-permute-start(bf16[96,896]{1,0:T(8,128)(2,1)S(1)} %fusion.33.h0), channel_id=1, source_target_pairs={{0,2},{1,3},{2,0},{3,1},{4,6},{5,7},{6,4},{7,5},{8,10},{9,11},{10,... | collective-permute-start | bytes 516104 | tf_op jit(solution)/shard_map/ppermute | solution.py:22
  129.7 15.3 %collective-permute-start.32 = (bf16[112,1792]{1,0:T(8,128)(2,1)S(1)}, bf16[112,1792]{1,0:T(8,128)(2,1)S(1)}, u32[]{:S(2)}, u32[]{:S(2)}) collective-permute-start(bf16[112,1792]{1,0:T(8,128)(2,1)S(1)} %fusion.29), channel_id=1, source_target_pairs={{0,2},{1,3},{2,0},{3,1},{4,6},{5,7},{6,4},{7,5},{8,10},{9,11},{10,... | collective-permute-start | bytes 1204232 | tf_op jit(solution)/shard_map/ppermute | solution.py:22
  131.4 29.5 %collective-permute-start.18 = (bf16[208,1792]{1,0:T(8,128)(2,1)S(1)}, bf16[208,1792]{1,0:T(8,128)(2,1)S(1)}, u32[]{:S(2)}, u32[]{:S(2)}) collective-permute-start(bf16[208,1792]{1,0:T(8,128)(2,1)S(1)} %fusion.25), channel_id=1, source_target_pairs={{0,2},{1,3},{2,0},{3,1},{4,6},{5,7},{6,4},{7,5},{8,10},{9,11},{10,... | collective-permute-start | bytes 2236424 | tf_op jit(solution)/shard_map/ppermute | solution.py:22
  145.3 20.0 %collective-permute-start.35 = (bf16[112,896]{1,0:T(8,128)(2,1)S(1)}, bf16[112,896]{1,0:T(8,128)(2,1)S(1)}, u32[]{:S(2)}, u32[]{:S(2)}) collective-permute-start(bf16[112,896]{1,0:T(8,128)(2,1)S(1)} %fusion.30.h0), channel_id=1, source_target_pairs={{0,2},{1,3},{2,0},{3,1},{4,6},{5,7},{6,4},{7,5},{8,10},{9,11},{10,... | collective-permute-start | bytes 602120 | tf_op jit(solution)/shard_map/ppermute | solution.py:22
  161.5 12.8 %collective-permute-start.21 = (bf16[208,896]{1,0:T(8,128)(2,1)S(1)}, bf16[208,896]{1,0:T(8,128)(2,1)S(1)}, u32[]{:S(2)}, u32[]{:S(2)}) collective-permute-start(bf16[208,896]{1,0:T(8,128)(2,1)S(1)} %fusion.26.h0), channel_id=1, source_target_pairs={{0,2},{1,3},{2,0},{3,1},{4,6},{5,7},{6,4},{7,5},{8,10},{9,11},{10,... | collective-permute-start | bytes 1118216 | tf_op jit(solution)/shard_map/ppermute | solution.py:22
  162.1 3.2 %collective-permute-start.8 = (bf16[96,896]{1,0:T(8,128)(2,1)S(1)}, bf16[96,896]{1,0:T(8,128)(2,1)S(1)}, u32[]{:S(2)}, u32[]{:S(2)}) collective-permute-start(bf16[96,896]{1,0:T(8,128)(2,1)S(1)} %fusion.33.h0), channel_id=1, source_target_pairs={{0,1},{1,0},{2,3},{3,2},{4,5},{5,4},{6,7},{7,6},{8,9},{9,8},{10,11... | collective-permute-start | bytes 516104 | tf_op jit(solution)/shard_map/ppermute | solution.py:22
  162.1 3.2 %collective-permute-start.9 = (bf16[96,896]{1,0:T(8,128)(2,1)S(1)}, bf16[96,896]{1,0:T(8,128)(2,1)S(1)}, u32[]{:S(2)}, u32[]{:S(2)}) collective-permute-start(bf16[96,896]{1,0:T(8,128)(2,1)S(1)} %collective-permute-done.7.h1), channel_id=1, source_target_pairs={{0,1},{1,0},{2,3},{3,2},{4,5},{5,4},{6,7},{7,6},{8,9},{9,8},{10,11... | collective-permute-start | bytes 516104 | tf_op jit(solution)/shard_map/ppermute | solution.py:22
  162.6 11.7 %collective-permute-start.36 = (bf16[112,896]{1,0:T(8,128)(2,1)S(1)}, bf16[112,896]{1,0:T(8,128)(2,1)S(1)}, u32[]{:S(2)}, u32[]{:S(2)}) collective-permute-start(bf16[112,896]{1,0:T(8,128)(2,1)S(1)} %fusion.30.h0), channel_id=1, source_target_pairs={{0,1},{1,0},{2,3},{3,2},{4,5},{5,4},{6,7},{7,6},{8,9},{9,8},{10,11... | collective-permute-start | bytes 602120 | tf_op jit(solution)/shard_map/ppermute | solution.py:22
  165.2 9.1 %collective-permute-start.37 = (bf16[112,896]{1,0:T(8,128)(2,1)S(1)}, bf16[112,896]{1,0:T(8,128)(2,1)S(1)}, u32[]{:S(2)}, u32[]{:S(2)}) collective-permute-start(bf16[112,896]{1,0:T(8,128)(2,1)S(1)} %collective-permute-done.35.h1), channel_id=1, source_target_pairs={{0,1},{1,0},{2,3},{3,2},{4,5},{5,4},{6,7},{7,6},{8,9},{9,8},{10,11... | collective-permute-start | bytes 602120 | tf_op jit(solution)/shard_map/ppermute | solution.py:22
  173.7 4.2 %collective-permute-start.22 = (bf16[208,896]{1,0:T(8,128)(2,1)S(1)}, bf16[208,896]{1,0:T(8,128)(2,1)S(1)}, u32[]{:S(2)}, u32[]{:S(2)}) collective-permute-start(bf16[208,896]{1,0:T(8,128)(2,1)S(1)} %fusion.26.h0), channel_id=1, source_target_pairs={{0,1},{1,0},{2,3},{3,2},{4,5},{5,4},{6,7},{7,6},{8,9},{9,8},{10,11... | collective-permute-start | bytes 1118216 | tf_op jit(solution)/shard_map/ppermute | solution.py:22
  174.2 3.7 %collective-permute-start.23 = (bf16[208,896]{1,0:T(8,128)(2,1)S(1)}, bf16[208,896]{1,0:T(8,128)(2,1)S(1)}, u32[]{:S(2)}, u32[]{:S(2)}) collective-permute-start(bf16[208,896]{1,0:T(8,128)(2,1)S(1)} %collective-permute-done.21.h1), channel_id=1, source_target_pairs={{0,1},{1,0},{2,3},{3,2},{4,5},{5,4},{6,7},{7,6},{8,9},{9,8},{10,11... | collective-permute-start | bytes 1118216 | tf_op jit(solution)/shard_map/ppermute | solution.py:22
  183.0 10.8 %collective-permute-start.26 = (bf16[72,2048]{1,0:T(8,128)(2,1)S(1)}, bf16[72,2048]{1,0:T(8,128)(2,1)S(1)}, u32[]{:S(2)}, u32[]{:S(2)}) collective-permute-start(bf16[72,2048]{1,0:T(8,128)(2,1)S(1)} %pad_maximum_fusion.3), channel_id=1, source_target_pairs={{0,12},{4,8},{8,4},{12,0},{16,28},{20,24},{24,20},{28,16},{1,13},{... | collective-permute-start | bytes 884744 | tf_op jit(solution)/shard_map/ppermute | solution.py:22
  184.5 15.8 %collective-permute-start.25 = (bf16[72,2048]{1,0:T(8,128)(2,1)S(1)}, bf16[72,2048]{1,0:T(8,128)(2,1)S(1)}, u32[]{:S(2)}, u32[]{:S(2)}) collective-permute-start(bf16[72,2048]{1,0:T(8,128)(2,1)S(1)} %pad_maximum_fusion.2), channel_id=1, source_target_pairs={{0,8},{4,12},{8,0},{12,4},{16,24},{20,28},{24,16},{28,20},{1,9},{5... | collective-permute-start | bytes 884744 | tf_op jit(solution)/shard_map/ppermute | solution.py:22
  186.3 14.0 %collective-permute-start.24 = (bf16[72,2048]{1,0:T(8,128)(2,1)S(1)}, bf16[72,2048]{1,0:T(8,128)(2,1)S(1)}, u32[]{:S(2)}, u32[]{:S(2)}) collective-permute-start(bf16[72,2048]{1,0:T(8,128)(2,1)S(1)} %pad_maximum_fusion.1), channel_id=1, source_target_pairs={{0,4},{4,0},{8,12},{12,8},{16,20},{20,16},{24,28},{28,24},{1,5},{5... | collective-permute-start | bytes 884744 | tf_op jit(solution)/shard_map/ppermute | solution.py:22
  186.8 29.7 %collective-permute-start.40 = (bf16[48,2048]{1,0:T(8,128)(2,1)S(1)}, bf16[48,2048]{1,0:T(8,128)(2,1)S(1)}, u32[]{:S(2)}, u32[]{:S(2)}) collective-permute-start(bf16[48,2048]{1,0:T(8,128)(2,1)S(1)} %get-tuple-element.30), channel_id=1, source_target_pairs={{0,12},{4,8},{8,4},{12,0},{16,28},{20,24},{24,20},{28,16},{1,13},{... | collective-permute-start | bytes 589832 | tf_op jit(solution)/shard_map/ppermute | solution.py:22
  188.3 29.9 %collective-permute-start.39 = (bf16[48,2048]{1,0:T(8,128)(2,1)S(1)}, bf16[48,2048]{1,0:T(8,128)(2,1)S(1)}, u32[]{:S(2)}, u32[]{:S(2)}) collective-permute-start(bf16[48,2048]{1,0:T(8,128)(2,1)S(1)} %get-tuple-element.31), channel_id=1, source_target_pairs={{0,8},{4,12},{8,0},{12,4},{16,24},{20,28},{24,16},{28,20},{1,9},{5... | collective-permute-start | bytes 589832 | tf_op jit(solution)/shard_map/ppermute | solution.py:22
  193.8 24.4 %collective-permute-start.38 = (bf16[48,2048]{1,0:T(8,128)(2,1)S(1)}, bf16[48,2048]{1,0:T(8,128)(2,1)S(1)}, u32[]{:S(2)}, u32[]{:S(2)}) collective-permute-start(bf16[48,2048]{1,0:T(8,128)(2,1)S(1)} %get-tuple-element.29), channel_id=1, source_target_pairs={{0,4},{4,0},{8,12},{12,8},{16,20},{20,16},{24,28},{28,24},{1,5},{5... | collective-permute-start | bytes 589832 | tf_op jit(solution)/shard_map/ppermute | solution.py:22
  200.5 16.0 %collective-permute-start.27 = (bf16[72,2048]{1,0:T(8,128)(2,1)S(1)}, bf16[72,2048]{1,0:T(8,128)(2,1)S(1)}, u32[]{:S(2)}, u32[]{:S(2)}) collective-permute-start(bf16[72,2048]{1,0:T(8,128)(2,1)S(1)} %add_convert_fusion.3), channel_id=1, source_target_pairs={{0,16},{4,20},{8,24},{12,28},{16,0},{20,4},{24,8},{28,12},{1,17},{... | collective-permute-start | bytes 884744 | tf_op jit(solution)/shard_map/ppermute | solution.py:22
  200.6 20.6 %copy-start.3 = (bf16[96,2048]{1,0:T(8,128)(2,1)S(1)}, bf16[96,2048]{1,0:T(8,128)(2,1)}, u32[]{:S(2)}) copy-start(bf16[96,2048]{1,0:T(8,128)(2,1)} %param.8) | copy-start | bytes 1179652
  200.7 20.6 %copy-start.10 = (f32[96]{0:T(128)S(1)}, f32[96]{0:T(128)}, u32[]{:S(2)}) copy-start(f32[96]{0:T(128)} %param.11) | copy-start | bytes 1156
  200.7 20.6 %copy-start.11 = (s32[1,72]{1,0:T(1,128)S(1)}, s32[1,72]{1,0:T(1,128)}, u32[]{:S(2)}) copy-start(s32[1,72]{1,0:T(1,128)} %param.10) | copy-start | bytes 868
  200.7 17.6 %collective-permute-start.12 = (bf16[24,2048]{1,0:T(8,128)(2,1)S(1)}, bf16[24,2048]{1,0:T(8,128)(2,1)S(1)}, u32[]{:S(2)}, u32[]{:S(2)}) collective-permute-start(bf16[24,2048]{1,0:T(8,128)(2,1)S(1)} %get-tuple-element.37), channel_id=1, source_target_pairs={{0,12},{4,8},{8,4},{12,0},{16,28},{20,24},{24,20},{28,16},{1,13},{... | collective-permute-start | bytes 294920 | tf_op jit(solution)/shard_map/ppermute | solution.py:22
  216.5 4.6 %collective-permute-start.11 = (bf16[24,2048]{1,0:T(8,128)(2,1)S(1)}, bf16[24,2048]{1,0:T(8,128)(2,1)S(1)}, u32[]{:S(2)}, u32[]{:S(2)}) collective-permute-start(bf16[24,2048]{1,0:T(8,128)(2,1)S(1)} %get-tuple-element.38), channel_id=1, source_target_pairs={{0,8},{4,12},{8,0},{12,4},{16,24},{20,28},{24,16},{28,20},{1,9},{5... | collective-permute-start | bytes 294920 | tf_op jit(solution)/shard_map/ppermute | solution.py:22
  216.5 4.7 %collective-permute-start.10 = (bf16[24,2048]{1,0:T(8,128)(2,1)S(1)}, bf16[24,2048]{1,0:T(8,128)(2,1)S(1)}, u32[]{:S(2)}, u32[]{:S(2)}) collective-permute-start(bf16[24,2048]{1,0:T(8,128)(2,1)S(1)} %get-tuple-element.36), channel_id=1, source_target_pairs={{0,4},{4,0},{8,12},{12,8},{16,20},{20,16},{24,28},{28,24},{1,5},{5... | collective-permute-start | bytes 294920 | tf_op jit(solution)/shard_map/ppermute | solution.py:22
  (15 other events, 113.5 us)

commit v2 on v0

v2 whole, which is shorter than its diff:
```python
import functools

import jax
import jax.numpy as jnp
from jax import lax
from jax.experimental import pallas as pl
from jax.experimental.pallas import tpu as pltpu
from jax.sharding import PartitionSpec as P

D = 8192
SEL = 48
SURE = SEL // 2
SLACK = SEL // 4
GROUP = 4
EPS = 1e-05
NONE = 1024.0
MIB = 1 << 20
LANES = 256
SPARE = 3
F32 = jnp.float32
BF16 = jnp.bfloat16
VMEM = pl.BlockSpec(memory_space=pltpu.VMEM)
SMEM = pl.BlockSpec(memory_space=pltpu.SMEM)
HBM = pl.BlockSpec(memory_space=pltpu.HBM)
ANY = pl.BlockSpec(memory_space=pl.ANY)


def swap(value, axis, size, bit):
    return lax.ppermute(value, axis, [(i, i ^ bit) for i in range(size)])


def call(kernel, outs, operands, specs, name, limit, scratch=(), after=()):
    made = pl.pallas_call(
        kernel,
        out_shape=[jax.ShapeDtypeStruct(shape, dtype) for shape, dtype in outs],
        in_specs=list(specs) + [ANY] * len(after),
        out_specs=[VMEM] * len(outs),
        scratch_shapes=list(scratch),
        compiler_params=pltpu.CompilerParams(vmem_limit_bytes=limit * MIB),
        name=name,
    )(*operands, *after)
    return list(made)


def pick_kernel(count_ref, chosen_ref, tokens_ref, out_ref):
    tokens, most = tokens_ref.shape[0], out_ref.shape[0]
    place = lax.broadcasted_iota(jnp.int32, (tokens, most), 0)
    rows = lax.dot_general(
        jnp.where(chosen_ref[...] == place, 1.0, 0.0).astype(BF16),
        tokens_ref[...],
        (((0,), (0,)), ((), ())),
        preferred_element_type=F32,
    )
    index = lax.broadcasted_iota(jnp.int32, rows.shape, 0)
    out_ref[...] = jnp.where(index < count_ref[0], rows, NONE).astype(BF16)


def slots_of(index, extras, start, member, window):
    index = index.astype(F32)
    in_rest = index - SURE
    slot = jnp.where(index < SURE, index + member * SURE, in_rest + start + GROUP * SURE)
    valid = (index < SURE) | ((in_rest < extras) & (in_rest < window))
    return jnp.where(valid, slot, -1.0)


def assemble_kernel(gain_ref, *refs, window):
    sources, (x_ref, squares_ref, extras_ref) = refs[:GROUP], refs[-3:]
    rows, feats = x_ref.shape
    payload = sources[0].shape[0]
    lanes = extras_ref.shape[1]
    total = jnp.zeros((rows, feats), F32)
    start = jnp.zeros((1, lanes), F32)
    extras_ref[...] = jnp.zeros_like(extras_ref)
    for member, source in enumerate(sources):
        marks = source[:, :lanes].astype(F32)
        extras = jnp.sum(jnp.where(marks < NONE, 1.0, 0.0), axis=0, keepdims=True) - SURE
        extras_ref[member : member + 1, :] = extras
        index = lax.broadcasted_iota(jnp.int32, (rows, payload), 1)
        slot = slots_of(index, extras[:, :payload], start[:, :payload], member, window)
        here = lax.broadcasted_iota(jnp.int32, (rows, payload), 0).astype(F32)
        hit = jnp.where(slot == here, 1.0, 0.0).astype(BF16)
        total += jnp.dot(hit, source[...], preferred_element_type=F32)
        start = start + extras
    x_ref[...] = (total * gain_ref[...]).astype(BF16)
    sums = jnp.sum(total * total, axis=1, keepdims=True)
    row = lax.broadcasted_iota(jnp.int32, (rows, lanes), 0)
    lane = lax.broadcasted_iota(jnp.int32, (rows, lanes), 1)
    spread = jnp.sum(jnp.where(row == lane, sums, 0.0), axis=0, keepdims=True)
    squares_ref[...] = jnp.broadcast_to(spread, squares_ref.shape)


def assemble(gain, sources, rows, window, after=()):
    feats = sources[0].shape[1]
    return call(
        functools.partial(assemble_kernel, window=window),
        [((rows, feats), BF16), ((8, LANES), F32), ((8, LANES), F32)],
        (gain, *sources),
        [VMEM] * (1 + GROUP),
        f"assemble_{rows}",
        24,
        after=after,
    )


def coded(squares, block):
    high = squares.astype(BF16).astype(F32)
    middle = (squares - high).astype(BF16).astype(F32)
    width = block.shape[1]
    terms = []
    for term in (high, middle, squares - high - middle):
        if width > LANES:
            term = jnp.concatenate([term, jnp.zeros((1, width - LANES), F32)], axis=1)
        terms.append(term[:, :width])
    row = lax.broadcasted_iota(jnp.int32, block.shape, 0) - (block.shape[0] - SPARE)
    block = block.astype(F32)
    for number, term in enumerate(terms):
        block = jnp.where(row == number, term, block)
    return block.astype(BF16)


def decoded(block):
    block = block.astype(F32)
    total = block[13:14] + block[14:15] + block[15:16]
    if total.shape[1] < LANES:
        total = jnp.concatenate([total, jnp.zeros((1, LANES - total.shape[1]), F32)], axis=1)
    return total[:, :LANES]


def gate_up_kernel(me_ref, x_ref, s_ref, g_ref, u_ref, *refs, share_width, cuts, shares, count):
    outs, (buffer, sems) = refs[-2 - count : -2], refs[-2:]
    me = me_ref[0]
    rows = x_ref.shape[0]
    slots = buffer.shape[0]
    tiles = [(step, array, cut) for step in range(2) for array in range(2) for cut in range(len(cuts))]

    def copy(tile):
        step, array, cut = tiles[tile]
        offset, width = cuts[cut]
        begin = pl.multiple_of((me ^ shares[step]) * share_width + offset, 128)
        source = (g_ref, u_ref)[array].at[:, pl.ds(begin, width)]
        slot = tile % slots
        return pltpu.make_async_copy(source, buffer.at[slot, :, pl.ds(0, width)], sems.at[slot])

    for tile in range(min(slots, len(tiles))):
        copy(tile).start()
    for tile, (step, array, cut) in enumerate(tiles):
        offset, width = cuts[cut]
        copy(tile).wait()
        term = jnp.dot(x_ref[...], buffer[tile % slots, :, :width], preferred_element_type=F32)
        if tile + slots < len(tiles):
            copy(tile + slots).start()
        if step == 1 or count == 2:
            place = pl.ds(array * share_width + offset, width)
            outs[step - 2][:, place] = term.astype(BF16)
        elif tile == 0:
            outs[0][: rows - 16, :] = term[: rows - 16].astype(BF16)
            outs[0][rows - 16 :, :] = coded(s_ref[0:1, :], term[rows - 16 :])
        else:
            outs[tile][...] = term.astype(BF16)


def gate_up(me, x, squares, w_gate, w_up, tp, cuts, mine, after):
    rows, feats = x.shape
    width = w_gate.shape[1] // tp
    shares = (1, 0) if mine else (3, 2)
    if width % 128:
        sums = [
            jnp.dot(x, w, preferred_element_type=F32).astype(BF16).reshape(rows, tp, width)
            for w in (w_gate, w_up)
        ]
        out = [
            [lax.dynamic_index_in_dim(p, me[0] ^ share, 1, False) for p in sums] for share in shares
        ]
        joined = [jnp.concatenate(pair, axis=1) for pair in out]
        if mine:
            return joined
        return [coded(squares[0:1], out[0][0]), out[0][1], joined[1]]
    whole = ((rows, 2 * width), BF16)
    pieces = [((rows, w), BF16) for _ in range(2) for _, w in cuts]
    outs = [whole] * 2 if mine else pieces + [whole]
    return call(
        functools.partial(
            gate_up_kernel, share_width=width, cuts=cuts, shares=shares, count=len(outs)
        ),
        outs,
        (me, x, squares, w_gate, w_up),
        [SMEM, VMEM, VMEM, HBM, HBM],
        f"gate_up_{rows}_{int(mine)}",
        50,
        scratch=[
            pltpu.VMEM((4, feats, max(w for _, w in cuts)), BF16),
            pltpu.SemaphoreType.DMA((4,)),
        ],
        after=after,
    )


def add_kernel(own_ref, s_ref, *refs, cuts, count):
    gots, (out_ref, sum_ref) = refs[:count], refs[-2:]
    rows, width = own_ref.shape
    for number, got in enumerate(gots):
        array, cut = divmod(number, len(cuts))
        offset, part = cuts[cut]
        place = pl.ds(array * (width // 2) + offset, part)
        total = own_ref[:, place].astype(F32) + got[...].astype(F32)
        out_ref[:, place] = total.astype(BF16)
    squares = s_ref[0:1, :] + decoded(gots[0][rows - 16 :, :])
    out_ref[rows - 16 :, :] = coded(squares, out_ref[rows - 16 :, :])
    sum_ref[...] = jnp.broadcast_to(squares, sum_ref.shape)


def add(own, gots, squares, cuts, after):
    return call(
        functools.partial(add_kernel, cuts=cuts, count=len(gots)),
        [(own.shape, BF16), ((8, LANES), F32)],
        (own, squares, *gots),
        [VMEM] * (2 + len(gots)),
        "add",
        16,
        after=after,
    )


def silu_kernel(a_ref, b_ref, c_ref, s_ref, *refs):
    out_ref = refs[-1]
    rows, width = out_ref.shape
    squares = s_ref[0:1, :] + decoded(c_ref[rows - 16 :, :])
    row = lax.broadcasted_iota(jnp.int32, (rows, LANES), 0)
    lane = lax.broadcasted_iota(jnp.int32, (rows, LANES), 1)
    column = jnp.sum(jnp.where(row == lane, squares, 0.0), axis=1, keepdims=True)
    scale = jnp.where(row[:, :1] < rows - SPARE, lax.rsqrt(column / D + EPS), 0.0)

    def total(part):
        return (
            a_ref[:, part].astype(F32) + b_ref[:, part].astype(F32) + c_ref[:, part].astype(F32)
        ) * scale

    gate, up = total(slice(0, width)), total(slice(width, 2 * width))
    out_ref[...] = (gate / (1.0 + jnp.exp(-gate)) * up).astype(BF16)


def silu(a, b, c, squares, after):
    rows, width = a.shape
    return call(
        silu_kernel,
        [((rows, width // 2), BF16)],
        (a, b, c, squares),
        [VMEM] * 4,
        "silu",
        16,
        after=after,
    )[0]


def relay_kernel(in_ref, *refs):
    refs[-1][...] = in_ref[...]


def relay(value, after):
    return call(relay_kernel, [(value.shape, value.dtype)], (value,), [VMEM], "relay", 16, after=after)[0]


def down_kernel(me_ref, extras_ref, h0, h1, w_ref, *refs, shares, parts, window, last):
    outs, (acc, buffer, sems) = refs[-GROUP - 3 if last else -4 : -3], refs[-3:]
    me = me_ref[0]
    width = h0.shape[1]
    depth = width // parts
    tiles = [(number, part) for number in range(2) for part in range(parts)]

    def copy(tile):
        number, part = tiles[tile]
        begin = pl.multiple_of((me ^ shares[number]) * width + part * depth, 16)
        return pltpu.make_async_copy(w_ref.at[pl.ds(begin, depth), :], buffer.at[tile], sems.at[tile])

    for tile in range(len(tiles)):
        copy(tile).start()
    for tile, (number, part) in enumerate(tiles):
        copy(tile).wait()
        hidden = (h0, h1)[number][:, part * depth : (part + 1) * depth]
        term = jnp.dot(hidden, buffer[tile], preferred_element_type=F32)
        if tile == 0:
            acc[...] = refs[0][...] + term if last else term
        else:
            acc[...] += term
    if not last:
        outs[0][...] = acc[...]
        return

    partial = acc[...].astype(BF16)
    rows = partial.shape[0]
    start = jnp.zeros((1, extras_ref.shape[1]), F32)
    for member, out in enumerate(outs):
        extras = extras_ref[member : member + 1, :]
        index = lax.broadcasted_iota(jnp.int32, (out.shape[0], rows), 0)
        slot = slots_of(index, extras[:, :rows], start[:, :rows], member, window)
        here = lax.broadcasted_iota(jnp.int32, (out.shape[0], rows), 1).astype(F32)
        hit = jnp.where(slot == here, 1.0, 0.0).astype(BF16)
        out[...] = jnp.dot(hit, partial, preferred_element_type=F32).astype(BF16)
        start = start + extras


def down(me, extras, w_down, hiddens, before, window, after):
    rows, width = hiddens[0].shape
    feats = w_down.shape[1]
    last = before is not None
    parts = 2 if width % 32 == 0 else 1
    return call(
        functools.partial(
            down_kernel, shares=(2, 3) if last else (0, 1), parts=parts, window=window, last=last
        ),
        [((SURE + window, feats), BF16)] * GROUP if last else [((rows, feats), F32)],
        (me, extras, *hiddens, w_down) + ((before,) if last else ()),
        [SMEM, VMEM, VMEM, VMEM, HBM] + [VMEM] * last,
        f"down_{rows}_{int(last)}",
        50,
        scratch=[
            pltpu.VMEM((rows, feats), F32),
            pltpu.VMEM((2 * parts, width // parts, feats), BF16),
            pltpu.SemaphoreType.DMA((2 * parts,)),
        ],
        after=after,
    )


def gather_group(rows, n_ctx):
    return [rows] + [swap(rows, "ctx", n_ctx, j) for j in range(1, GROUP)]


def sum_kernel(a_ref, b_ref, c_ref, d_ref, *refs):
    total = a_ref[...].astype(F32) + b_ref[...].astype(F32)
    refs[-1][...] = (total + c_ref[...].astype(F32) + d_ref[...].astype(F32)).astype(BF16)


def reduce_group(blocks, n_ctx, after):
    got = [blocks[0]] + [swap(blocks[j], "ctx", n_ctx, j) for j in range(1, GROUP)]
    return call(
        sum_kernel, [(blocks[0].shape, BF16)], got, [VMEM] * GROUP, "sum", 16, after=after
    )[0]


def body(hidden_states, counts, selected, router_weight, norm_gain, w_gate, w_up, w_down, *, n_ctx, tp):
    me = lax.axis_index("tp").astype(jnp.int32).reshape(1)
    chosen = selected[0]
    most = chosen.shape[0]
    tokens, feats = hidden_states.shape
    window = most - SURE
    inner = min(2, n_ctx // GROUP - 1)
    slots = -(-(GROUP * (SEL - SURE) + SLACK * inner + SPARE) // 16) * 16
    height = GROUP * SURE + slots
    gain = norm_gain[None, :]
    share_width = w_gate.shape[1] // tp
    first = -(-share_width // 256) * 128
    cuts = [(0, share_width)]
    if share_width % 128 == 0 and first < share_width:
        cuts = [(0, first), (first, share_width - first)]

    rows = call(
        pick_kernel,
        [((most, feats), BF16)],
        (counts, selected, hidden_states),
        [SMEM, VMEM, VMEM],
        "pick",
        16,
    )[0]
    sources = [gather_group(rows, n_ctx)]
    for d in range(GROUP, n_ctx, GROUP):
        sources.append(gather_group(swap(rows, "ctx", n_ctx, d), n_ctx))
    weights = (w_gate, w_up, tp, cuts)

    chunks = [assemble(gain, members, height, window) for members in sources]
    begun, after = [], []
    for number, (x, squares, _) in enumerate(chunks):
        *sends, keep = gate_up(me, x, squares, *weights, False, after)
        gots = [swap(piece, "tp", tp, 1) for piece in sends]
        outgoing, two = add(keep, gots, squares, cuts, [] if number else chunks[1][:1])
        begun.append((swap(outgoing, "tp", tp, 2), two))
        after = [outgoing]
    owns, cores, parts = [], [], []
    for (x, squares, extras), (across, two) in zip(chunks, begun):
        send, keep = gate_up(me, x, squares, *weights, True, after)
        own = silu(keep, swap(send, "tp", tp, 1), across, two, parts[:1])
        after = [own]
        owns.append(own)
        cores.append(swap(own, "tp", tp, 1))
        if not parts:
            parts.append(down(me, extras, w_down, (own, cores[0]), None, window, [])[0])

    blocks, behind = [], []
    for number in [*range(1, len(chunks)), 0]:
        extras = chunks[number][2]
        other_y = swap(owns[number], "tp", tp, 2)
        if number:
            hidden = (owns[number], cores[number])
            part = down(me, extras, w_down, hidden, None, window, behind)[0]
        else:
            part = parts[0]
        other_y = relay(other_y, [part] + behind)
        both = swap(other_y, "tp", tp, 1)
        blocks.append(down(me, extras, w_down, (other_y, both), part, window, []))
        behind = blocks[-1][:1]

    total = 0.0
    for number, parts in enumerate(blocks[:-1]):
        summed = reduce_group(parts, n_ctx, blocks[-1][:1])
        total = total + swap(summed, "ctx", n_ctx, GROUP * (number + 1)).astype(F32)
    for number, part in enumerate(blocks[-1]):
        total = total + (swap(part, "ctx", n_ctx, number) if number else part).astype(F32)

    ffn = total.astype(BF16)
    active = jnp.arange(most, dtype=jnp.int32) < counts[0]
    place = jnp.arange(tokens, dtype=jnp.int32)
    put = ((chosen[None, :] == place[:, None]) & active[None, :]).astype(BF16)
    added = jnp.dot(put, ffn, preferred_element_type=F32) * router_weight[:, None]
    return (hidden_states.astype(F32) + added).astype(BF16)


def solution(mesh):
    placed = (
        P("ctx", "tp"),
        P("ctx"),
        P("ctx", None),
        P("ctx"),
        P("tp"),
        P("tp", "ctx"),
        P("tp", "ctx"),
        P("ctx", "tp"),
    )
    return jax.shard_map(
        functools.partial(body, n_ctx=mesh.shape["ctx"], tp=mesh.shape["tp"]),
        mesh=mesh,
        in_specs=placed,
        out_specs=P("ctx", "tp"),
        check_vma=False,
    )
```

time: 360 us -> 145 us (0.40)
  waiting for transfers between devices: 224 us -> 63.1 us
  local copies, waits for them, and re-layouts: 55.7 us -> 2.37 us
  Pallas kernels: 0 us -> 48.7 us
  matrix products: 44.6 us -> 1.13 us
  starting transfers between devices: 0.31 us -> 28.8 us
  between operations: 13.9 us -> 0.9 us
  other arithmetic: 12 us -> 0.01 us
  blocking collectives: 8.36 us -> 0 us
    all_gather x2 -> x0, waiting for transfers between devices: 86.6 us -> none  [the longest x1 52.5 us: body(): piece = lax.all_gather(normed, 'ctx', axis=0, tiled=True)]
    unnamed x5 -> x0, waiting for transfers between devices: 69.5 us -> none
    reduce_scatter x1 -> x0, waiting for transfers between devices: 67.8 us -> none  [body(): lax.psum_scatter(jnp.dot(hidden, w_down, preferred_element_type=jnp.float...]
    ppermute x0 -> x32, waiting for transfers between devices: none -> 63.1 us  [swap(): return lax.ppermute(value, axis, [(i, i ^ bit) for i in range(size)])]
    unnamed x12 -> x14, local copies, waits for them, and re-layouts: 52.4 us -> 2.37 us
    pallas_call x0 -> x18, Pallas kernels: none -> 48.7 us  [call(): pl.pallas_call(kernel, out_shape=[jax.ShapeDtypeStruct(shape, dtype) for...]
    dot_general x4 -> x1, matrix products: 44.6 us -> 1.13 us  [body(): jnp.dot(put, ffn, preferred_element_type=F32) * router_weight[:, None]]
    ppermute x0 -> x32, starting transfers between devices: none -> 28.8 us  [swap(): return lax.ppermute(value, axis, [(i, i ^ bit) for i in range(size)])]
  transfers between devices with their start and end apart: 4 -> 32, of which waited for: 4 -> 13; matrix products, arithmetic and copies ran while one was open for 0% -> 0% of each run, Pallas kernels for 0% -> 28%
where the time goes in v2:
time: 145 us
  waiting for transfers between devices  63.1 us (44%)
  Pallas kernels  48.7 us (34%)
  starting transfers between devices  28.8 us (20%)
  local copies, waits for them, and re-layouts  2.37 us (2%)
    ppermute x32, waiting for transfers between devices, swap(): return lax.ppermute(value, axis, [(i, i ^ bit) for i in range(size)])  63.1 us
    pallas_call x18, Pallas kernels, call(): pl.pallas_call(kernel, out_shape=[jax.ShapeDtypeStruct(shape, dtype) for...  48.7 us
    ppermute x32, starting transfers between devices, swap(): return lax.ppermute(value, axis, [(i, i ^ bit) for i in range(size)])  28.8 us
  transfers between devices with their start and end apart: 32, of which 13 were waited for; matrix products, arithmetic and copies ran while one was open for 0% of the time, Pallas kernels for 28%

profile of v2, /device:TPU:0, one launch (start us, length us, event | category | flops | bytes accessed | tf_op | source)
XLA Modules:
  0.0 145.0 jit_solution(5790660453079920666)
XLA Ops:
  0.7 1.0 copy-done
  1.7 0.7 copy-done.4
  2.6 4.1 %collective-permute-start = (bf16[72,2048]{1,0:T(8,128)(2,1)S(1)}, bf16[72,2048]{1,0:T(8,128)(2,1)S(1)}, u32[]{:S(2)}, u32[]{:S(2)}) collective-permute-start(bf16[72,2048]{1,0:T(8,128)(2,1)S(1)} %pick.1.refs_0_), channel_id=1, source_target_pairs={{0,16},{4,20},{8,24},{12,28},{16,0},{20,4},{24,8},{28,12},{1,17},{... | collective-permute-start | bytes 884744 | tf_op jit(solution)/shard_map/ppermute | solution.py:29
  6.7 2.5 %collective-permute-start.6 = (bf16[72,2048]{1,0:T(8,128)(2,1)S(1)}, bf16[72,2048]{1,0:T(8,128)(2,1)S(1)}, u32[]{:S(2)}, u32[]{:S(2)}) collective-permute-start(bf16[72,2048]{1,0:T(8,128)(2,1)S(1)} %pick.1.refs_0_), channel_id=1, source_target_pairs={{0,12},{4,8},{8,4},{12,0},{16,28},{20,24},{24,20},{28,16},{1,13},{... | collective-permute-start | bytes 884744 | tf_op jit(solution)/shard_map/ppermute | solution.py:29
  9.2 0.4 collective-permute-start.5
  9.6 0.5 collective-permute-start.4
  10.2 9.9 %collective-permute-done.refs_0_ = bf16[72,2048]{1,0:T(8,128)(2,1)S(1)} collective-permute-done((bf16[72,2048]{1,0:T(8,128)(2,1)S(1)}, bf16[72,2048]{1,0:T(8,128)(2,1)S(1)}, u32[]{:S(2)}, u32[]{:S(2)}) %collective-permute-start) | collective-permute-done | bytes 294944 | tf_op jit(solution)/shard_map/ppermute | solution.py:29
  20.1 1.6 %collective-permute-start.3 = (bf16[72,2048]{1,0:T(8,128)(2,1)S(1)}, bf16[72,2048]{1,0:T(8,128)(2,1)S(1)}, u32[]{:S(2)}, u32[]{:S(2)}) collective-permute-start(bf16[72,2048]{1,0:T(8,128)(2,1)S(1)} %collective-permute-done.refs_0_), channel_id=1, source_target_pairs={{0,12},{4,8},{8,4},{12,0},{16,28},{20,24},{24,20},{28,16},{1,13},{... | collective-permute-start | bytes 884744 | tf_op jit(solution)/shard_map/ppermute | solution.py:29
  21.7 1.4 collective-permute-start.2
  23.1 1.1 collective-permute-start.1
  24.2 4.9 %collective-permute-done.5.refs_2_ = bf16[72,2048]{1,0:T(8,128)(2,1)S(1)} collective-permute-done((bf16[72,2048]{1,0:T(8,128)(2,1)S(1)}, bf16[72,2048]{1,0:T(8,128)(2,1)S(1)}, u32[]{:S(2)}, u32[]{:S(2)}) %collective-permute-start.5) | collective-permute-done | bytes 294944 | tf_op jit(solution)/shard_map/ppermute | solution.py:29
  29.1 0.7 copy-done.2
  29.8 1.1 assemble_208.3
  30.9 6.7 %gate_up_208_0.2 = (bf16[208,512]{1,0:T(8,128)(2,1)S(1)}, bf16[208,384]{1,0:T(8,128)(2,1)S(1)}, bf16[208,512]{1,0:T(8,128)(2,1)S(1)}, bf16[208,384]{1,0:T(8,128)(2,1)S(1)}, bf16[208,1792]{1,0:T(8,128)(2,1)S(1)}) custom-call(s32[1]{0:T(128)} %bitcast.2.me_ref, bf16[208,2048]{1,0:T(8,128)(2,1)S(1)} %get-tuple-element.40.x_ref, ...), custom_call_target="tpu_custom_call" | custom-call | tf_op jit(solution)/shard_map/gate_up_208_0/pallas_call | solution.py:33
  37.7 0.5 collective-permute-start.9
  38.3 2.0 %collective-permute-done.2.refs_2_ = bf16[72,2048]{1,0:T(8,128)(2,1)S(1)} collective-permute-done((bf16[72,2048]{1,0:T(8,128)(2,1)S(1)}, bf16[72,2048]{1,0:T(8,128)(2,1)S(1)}, u32[]{:S(2)}, u32[]{:S(2)}) %collective-permute-start.2) | collective-permute-done | bytes 294944 | tf_op jit(solution)/shard_map/ppermute | solution.py:29
  40.3 1.1 assemble_208.2
  42.0 6.7 %gate_up_208_0.3 = (bf16[208,512]{1,0:T(8,128)(2,1)S(1)}, bf16[208,384]{1,0:T(8,128)(2,1)S(1)}, bf16[208,512]{1,0:T(8,128)(2,1)S(1)}, bf16[208,384]{1,0:T(8,128)(2,1)S(1)}, bf16[208,1792]{1,0:T(8,128)(2,1)S(1)}) custom-call(s32[1]{0:T(128)} %bitcast.2.me_ref, bf16[208,2048]{1,0:T(8,128)(2,1)S(1)} %get-tuple-element.38.refs_4_.x_ref, ...), custom_call_target="tpu_custom_call" | custom-call | tf_op jit(solution)/shard_map/gate_up_208_0/pallas_call | solution.py:33
  49.8 1.6 %collective-permute-start.16 = (bf16[208,1792]{1,0:T(8,128)(2,1)S(1)}, bf16[208,1792]{1,0:T(8,128)(2,1)S(1)}, u32[]{:S(2)}, u32[]{:S(2)}) collective-permute-start(bf16[208,1792]{1,0:T(8,128)(2,1)S(1)} %get-tuple-element.47.refs_0_), channel_id=1, source_target_pairs={{0,2},{1,3},{2,0},{3,1},{4,6},{5,7},{6,4},{7,5},{8,10},{9,11},{10,... | collective-permute-start | bytes 2236424 | tf_op jit(solution)/shard_map/ppermute | solution.py:29
  51.7 6.8 %gate_up_208_1.2 = (bf16[208,1792]{1,0:T(8,128)(2,1)S(1)}, bf16[208,1792]{1,0:T(8,128)(2,1)S(1)}) custom-call(s32[1]{0:T(128)} %bitcast.2.me_ref, bf16[208,2048]{1,0:T(8,128)(2,1)S(1)} %get-tuple-element.40.x_ref, f32[8,256]{1,0:T(8,128)S(1)} %get-tuple-element.41.s_ref, bf16[2048,3584]{1,0:T(8,128)(2,1)} %g_ref.7, bf16[2048,3584]{1,0:T(8,128)(2,1)} %u_ref.7, ...), custom_call_target="tpu_custom_call" | custom-call | tf_op jit(solution)/shard_map/gate_up_208_1/pallas_call | solution.py:33
  58.6 1.5 %collective-permute-start.18 = (bf16[208,1792]{1,0:T(8,128)(2,1)S(1)}, bf16[208,1792]{1,0:T(8,128)(2,1)S(1)}, u32[]{:S(2)}, u32[]{:S(2)}) collective-permute-start(bf16[208,1792]{1,0:T(8,128)(2,1)S(1)} %get-tuple-element.53.refs_0_), channel_id=1, source_target_pairs={{0,2},{1,3},{2,0},{3,1},{4,6},{5,7},{6,4},{7,5},{8,10},{9,11},{10,... | collective-permute-start | bytes 2236424 | tf_op jit(solution)/shard_map/ppermute | solution.py:29
  60.1 9.1 %collective-permute-done.16.c_ref = bf16[208,1792]{1,0:T(8,128)(2,1)S(1)} collective-permute-done((bf16[208,1792]{1,0:T(8,128)(2,1)S(1)}, bf16[208,1792]{1,0:T(8,128)(2,1)S(1)}, u32[]{:S(2)}, u32[]{:S(2)}) %collective-permute-start.16) | collective-permute-done | bytes 745504 | tf_op jit(solution)/shard_map/ppermute | solution.py:29
  69.3 0.8 silu.2.refs_0_.h0
  70.1 6.7 %gate_up_208_1.3 = (bf16[208,1792]{1,0:T(8,128)(2,1)S(1)}, bf16[208,1792]{1,0:T(8,128)(2,1)S(1)}) custom-call(s32[1]{0:T(128)} %bitcast.2.me_ref, bf16[208,2048]{1,0:T(8,128)(2,1)S(1)} %get-tuple-element.38.refs_4_.x_ref, f32[8,256]{1,0:T(8,128)S(1)} %get-tuple-element.39.s_ref, bf16[2048,3584]{1,0:T(8,128)(2,1)} %g_ref.7, bf16[2048,3584]{1,0:T(8,128)(2,1)} %u_ref.7, ...), custom_call_target="tpu_custom_call" | custom-call | tf_op jit(solution)/shard_map/gate_up_208_1/pallas_call | solution.py:33
  76.8 0.5 collective-permute-start.19
  77.3 2.2 %collective-permute-done.19.h1 = bf16[208,896]{1,0:T(8,128)(2,1)S(1)} collective-permute-done((bf16[208,896]{1,0:T(8,128)(2,1)S(1)}, bf16[208,896]{1,0:T(8,128)(2,1)S(1)}, u32[]{:S(2)}, u32[]{:S(2)}) %collective-permute-start.19) | collective-permute-done | bytes 372768 | tf_op jit(solution)/shard_map/ppermute | solution.py:29
  79.6 3.8 %down_208_0.2.refs_0_ = f32[208,2048]{1,0:T(8,128)S(1)} custom-call(s32[1]{0:T(128)} %bitcast.2.me_ref, f32[8,256]{1,0:T(8,128)S(1)} %get-tuple-element.60.extras_ref, bf16[208,896]{1,0:T(8,128)(2,1)S(1)} %silu.2.refs_0_.h0, bf16[208,896]{1,0:T(8,128)(2,1)S(1)} %collective-permute-done.19.h1, bf16[3584,2048]{1,0:T(8,128)(2,1)} %w_ref.7), custom_call_target="tpu_custom_call" | custom-call | tf_op jit(solution)/shard_map/down_208_0/pallas_call | solution.py:33
  83.4 1.2 collective-permute-done.18.c_ref
  84.6 0.8 silu.3.h0
  85.5 1.6 %collective-permute-start.20 = (bf16[208,896]{1,0:T(8,128)(2,1)S(1)}, bf16[208,896]{1,0:T(8,128)(2,1)S(1)}, u32[]{:S(2)}, u32[]{:S(2)}) collective-permute-start(bf16[208,896]{1,0:T(8,128)(2,1)S(1)} %silu.3.h0), channel_id=1, source_target_pairs={{0,2},{1,3},{2,0},{3,1},{4,6},{5,7},{6,4},{7,5},{8,10},{9,11},{10,... | collective-permute-start | bytes 1118216 | tf_op jit(solution)/shard_map/ppermute | solution.py:29
  87.2 3.8 %down_208_0.3.refs_0_ = f32[208,2048]{1,0:T(8,128)S(1)} custom-call(s32[1]{0:T(128)} %bitcast.2.me_ref, f32[8,256]{1,0:T(8,128)S(1)} %get-tuple-element.37.extras_ref, bf16[208,896]{1,0:T(8,128)(2,1)S(1)} %silu.3.h0, bf16[208,896]{1,0:T(8,128)(2,1)S(1)} %collective-permute-done.21.h1, bf16[3584,2048]{1,0:T(8,128)(2,1)} %w_ref.7), custom_call_target="tpu_custom_call" | custom-call | tf_op jit(solution)/shard_map/down_208_0/pallas_call | solution.py:33
  91.0 5.6 %collective-permute-done.20.in_ref = bf16[208,896]{1,0:T(8,128)(2,1)S(1)} collective-permute-done((bf16[208,896]{1,0:T(8,128)(2,1)S(1)}, bf16[208,896]{1,0:T(8,128)(2,1)S(1)}, u32[]{:S(2)}, u32[]{:S(2)}) %collective-permute-start.20) | collective-permute-done | bytes 372768 | tf_op jit(solution)/shard_map/ppermute | solution.py:29
  96.7 1.6 %collective-permute-start.26 = (bf16[208,896]{1,0:T(8,128)(2,1)S(1)}, bf16[208,896]{1,0:T(8,128)(2,1)S(1)}, u32[]{:S(2)}, u32[]{:S(2)}) collective-permute-start(bf16[208,896]{1,0:T(8,128)(2,1)S(1)} %silu.2.refs_0_.h0), channel_id=1, source_target_pairs={{0,2},{1,3},{2,0},{3,1},{4,6},{5,7},{6,4},{7,5},{8,10},{9,11},{10,... | collective-permute-start | bytes 1118216 | tf_op jit(solution)/shard_map/ppermute | solution.py:29
  98.4 4.7 %down_208_1.2 = (bf16[72,2048]{1,0:T(8,128)(2,1)S(1)}, bf16[72,2048]{1,0:T(8,128)(2,1)S(1)}, bf16[72,2048]{1,0:T(8,128)(2,1)S(1)}, bf16[72,2048]{1,0:T(8,128)(2,1)S(1)}) custom-call(s32[1]{0:T(128)} %bitcast.2.me_ref, f32[8,256]{1,0:T(8,128)S(1)} %get-tuple-element.37.extras_ref, bf16[208,896]{1,0:T(8,128)(2,1)S(1)} %relay.2.h0, ...), custom_call_target="tpu_custom_call" | custom-call | tf_op jit(solution)/shard_map/down_208_1/pallas_call | solution.py:33
  103.1 4.7 %collective-permute-done.26.in_ref = bf16[208,896]{1,0:T(8,128)(2,1)S(1)} collective-permute-done((bf16[208,896]{1,0:T(8,128)(2,1)S(1)}, bf16[208,896]{1,0:T(8,128)(2,1)S(1)}, u32[]{:S(2)}, u32[]{:S(2)}) %collective-permute-start.26) | collective-permute-done | bytes 372768 | tf_op jit(solution)/shard_map/ppermute | solution.py:29
  107.9 0.7 collective-permute-start.23
  108.6 1.5 %collective-permute-start.24 = (bf16[72,2048]{1,0:T(8,128)(2,1)S(1)}, bf16[72,2048]{1,0:T(8,128)(2,1)S(1)}, u32[]{:S(2)}, u32[]{:S(2)}) collective-permute-start(bf16[72,2048]{1,0:T(8,128)(2,1)S(1)} %get-tuple-element.63), channel_id=1, source_target_pairs={{0,8},{4,12},{8,0},{12,4},{16,24},{20,28},{24,16},{28,20},{1,9},{5... | collective-permute-start | bytes 884744 | tf_op jit(solution)/shard_map/ppermute | solution.py:29
  110.0 1.4 collective-permute-start.25
  111.5 4.4 %down_208_1.3 = (bf16[72,2048]{1,0:T(8,128)(2,1)S(1)}, bf16[72,2048]{1,0:T(8,128)(2,1)S(1)}, bf16[72,2048]{1,0:T(8,128)(2,1)S(1)}, bf16[72,2048]{1,0:T(8,128)(2,1)S(1)}) custom-call(s32[1]{0:T(128)} %bitcast.2.me_ref, f32[8,256]{1,0:T(8,128)S(1)} %get-tuple-element.60.extras_ref, bf16[208,896]{1,0:T(8,128)(2,1)S(1)} %relay.3.h0, ...), custom_call_target="tpu_custom_call" | custom-call | tf_op jit(solution)/shard_map/down_208_1/pallas_call | solution.py:33
  115.9 0.7 collective-permute-start.29
  116.6 1.5 %collective-permute-start.30 = (bf16[72,2048]{1,0:T(8,128)(2,1)S(1)}, bf16[72,2048]{1,0:T(8,128)(2,1)S(1)}, u32[]{:S(2)}, u32[]{:S(2)}) collective-permute-start(bf16[72,2048]{1,0:T(8,128)(2,1)S(1)} %get-tuple-element.67), channel_id=1, source_target_pairs={{0,8},{4,12},{8,0},{12,4},{16,24},{20,28},{24,16},{28,20},{1,9},{5... | collective-permute-start | bytes 884744 | tf_op jit(solution)/shard_map/ppermute | solution.py:29
  118.0 1.4 collective-permute-start.31
  119.5 6.2 %collective-permute-done.25.d_ref = bf16[72,2048]{1,0:T(8,128)(2,1)S(1)} collective-permute-done((bf16[72,2048]{1,0:T(8,128)(2,1)S(1)}, bf16[72,2048]{1,0:T(8,128)(2,1)S(1)}, u32[]{:S(2)}, u32[]{:S(2)}) %collective-permute-start.25) | collective-permute-done | bytes 294944 | tf_op jit(solution)/shard_map/ppermute | solution.py:29
  125.8 1.1 collective-permute-start.28
  126.9 3.7 %collective-permute-done.29 = bf16[72,2048]{1,0:T(8,128)(2,1)S(1)} collective-permute-done((bf16[72,2048]{1,0:T(8,128)(2,1)S(1)}, bf16[72,2048]{1,0:T(8,128)(2,1)S(1)}, u32[]{:S(2)}, u32[]{:S(2)}) %collective-permute-start.29) | collective-permute-done | bytes 294944 | tf_op jit(solution)/shard_map/ppermute | solution.py:29
  130.6 6.8 %collective-permute-done.30 = bf16[72,2048]{1,0:T(8,128)(2,1)S(1)} collective-permute-done((bf16[72,2048]{1,0:T(8,128)(2,1)S(1)}, bf16[72,2048]{1,0:T(8,128)(2,1)S(1)}, u32[]{:S(2)}, u32[]{:S(2)}) %collective-permute-start.30) | collective-permute-done | bytes 294944 | tf_op jit(solution)/shard_map/ppermute | solution.py:29
  137.4 6.4 %collective-permute-done.31 = bf16[72,2048]{1,0:T(8,128)(2,1)S(1)} collective-permute-done((bf16[72,2048]{1,0:T(8,128)(2,1)S(1)}, bf16[72,2048]{1,0:T(8,128)(2,1)S(1)}, u32[]{:S(2)}, u32[]{:S(2)}) %collective-permute-start.31) | collective-permute-done | bytes 294944 | tf_op jit(solution)/shard_map/ppermute | solution.py:29
  143.9 1.1 fusion.1
  (50 shorter events, 3.1 us)
Async XLA Ops:
  0.7 1.0 copy-start
  1.7 0.7 copy-start.4
  2.6 17.5 %collective-permute-start = (bf16[72,2048]{1,0:T(8,128)(2,1)S(1)}, bf16[72,2048]{1,0:T(8,128)(2,1)S(1)}, u32[]{:S(2)}, u32[]{:S(2)}) collective-permute-start(bf16[72,2048]{1,0:T(8,128)(2,1)S(1)} %pick.1.refs_0_), channel_id=1, source_target_pairs={{0,16},{4,20},{8,24},{12,28},{16,0},{20,4},{24,8},{28,12},{1,17},{... | collective-permute-start | bytes 884744 | tf_op jit(solution)/shard_map/ppermute | solution.py:29
  6.7 16.4 %collective-permute-start.6 = (bf16[72,2048]{1,0:T(8,128)(2,1)S(1)}, bf16[72,2048]{1,0:T(8,128)(2,1)S(1)}, u32[]{:S(2)}, u32[]{:S(2)}) collective-permute-start(bf16[72,2048]{1,0:T(8,128)(2,1)S(1)} %pick.1.refs_0_), channel_id=1, source_target_pairs={{0,12},{4,8},{8,4},{12,0},{16,28},{20,24},{24,20},{28,16},{1,13},{... | collective-permute-start | bytes 884744 | tf_op jit(solution)/shard_map/ppermute | solution.py:29
  9.2 19.9 %collective-permute-start.5 = (bf16[72,2048]{1,0:T(8,128)(2,1)S(1)}, bf16[72,2048]{1,0:T(8,128)(2,1)S(1)}, u32[]{:S(2)}, u32[]{:S(2)}) collective-permute-start(bf16[72,2048]{1,0:T(8,128)(2,1)S(1)} %pick.1.refs_0_), channel_id=1, source_target_pairs={{0,8},{4,12},{8,0},{12,4},{16,24},{20,28},{24,16},{28,20},{1,9},{5... | collective-permute-start | bytes 884744 | tf_op jit(solution)/shard_map/ppermute | solution.py:29
  9.6 19.4 %collective-permute-start.4 = (bf16[72,2048]{1,0:T(8,128)(2,1)S(1)}, bf16[72,2048]{1,0:T(8,128)(2,1)S(1)}, u32[]{:S(2)}, u32[]{:S(2)}) collective-permute-start(bf16[72,2048]{1,0:T(8,128)(2,1)S(1)} %pick.1.refs_0_), channel_id=1, source_target_pairs={{0,4},{4,0},{8,12},{12,8},{16,20},{20,16},{24,28},{28,24},{1,5},{5... | collective-permute-start | bytes 884744 | tf_op jit(solution)/shard_map/ppermute | solution.py:29
  20.1 18.1 %collective-permute-start.3 = (bf16[72,2048]{1,0:T(8,128)(2,1)S(1)}, bf16[72,2048]{1,0:T(8,128)(2,1)S(1)}, u32[]{:S(2)}, u32[]{:S(2)}) collective-permute-start(bf16[72,2048]{1,0:T(8,128)(2,1)S(1)} %collective-permute-done.refs_0_), channel_id=1, source_target_pairs={{0,12},{4,8},{8,4},{12,0},{16,28},{20,24},{24,20},{28,16},{1,13},{... | collective-permute-start | bytes 884744 | tf_op jit(solution)/shard_map/ppermute | solution.py:29
  21.7 18.6 %collective-permute-start.2 = (bf16[72,2048]{1,0:T(8,128)(2,1)S(1)}, bf16[72,2048]{1,0:T(8,128)(2,1)S(1)}, u32[]{:S(2)}, u32[]{:S(2)}) collective-permute-start(bf16[72,2048]{1,0:T(8,128)(2,1)S(1)} %collective-permute-done.refs_0_), channel_id=1, source_target_pairs={{0,8},{4,12},{8,0},{12,4},{16,24},{20,28},{24,16},{28,20},{1,9},{5... | collective-permute-start | bytes 884744 | tf_op jit(solution)/shard_map/ppermute | solution.py:29
  23.1 17.2 %collective-permute-start.1 = (bf16[72,2048]{1,0:T(8,128)(2,1)S(1)}, bf16[72,2048]{1,0:T(8,128)(2,1)S(1)}, u32[]{:S(2)}, u32[]{:S(2)}) collective-permute-start(bf16[72,2048]{1,0:T(8,128)(2,1)S(1)} %collective-permute-done.refs_0_), channel_id=1, source_target_pairs={{0,4},{4,0},{8,12},{12,8},{16,20},{20,16},{24,28},{28,24},{1,5},{5... | collective-permute-start | bytes 884744 | tf_op jit(solution)/shard_map/ppermute | solution.py:29
  29.1 0.7 copy-start.2
  30.9 9.4 %copy-start.3 = (f32[2048]{0:T(1024)S(1)}, f32[2048]{0:T(1024)}, u32[]{:S(2)}) copy-start(f32[2048]{0:T(1024)} %param.12) | copy-start | bytes 24580
  37.6 4.1 %collective-permute-start.7 = (bf16[208,512]{1,0:T(8,128)(2,1)S(1)}, bf16[208,512]{1,0:T(8,128)(2,1)S(1)}, u32[]{:S(2)}, u32[]{:S(2)}) collective-permute-start(bf16[208,512]{1,0:T(8,128)(2,1)S(1)} %get-tuple-element.43), channel_id=1, source_target_pairs={{0,1},{1,0},{2,3},{3,2},{4,5},{5,4},{6,7},{7,6},{8,9},{9,8},{10,11... | collective-permute-start | bytes 638984 | tf_op jit(solution)/shard_map/ppermute | solution.py:29
  37.7 4.0 %collective-permute-start.9 = (bf16[208,512]{1,0:T(8,128)(2,1)S(1)}, bf16[208,512]{1,0:T(8,128)(2,1)S(1)}, u32[]{:S(2)}, u32[]{:S(2)}) collective-permute-start(bf16[208,512]{1,0:T(8,128)(2,1)S(1)} %get-tuple-element.45), channel_id=1, source_target_pairs={{0,1},{1,0},{2,3},{3,2},{4,5},{5,4},{6,7},{7,6},{8,9},{9,8},{10,11... | collective-permute-start | bytes 638984 | tf_op jit(solution)/shard_map/ppermute | solution.py:29
  38.2 3.2 %collective-permute-start.8 = (bf16[208,384]{1,0:T(8,128)(2,1)S(1)}, bf16[208,384]{1,0:T(8,128)(2,1)S(1)}, u32[]{:S(2)}, u32[]{:S(2)}) collective-permute-start(bf16[208,384]{1,0:T(8,128)(2,1)S(1)} %get-tuple-element.44), channel_id=1, source_target_pairs={{0,1},{1,0},{2,3},{3,2},{4,5},{5,4},{6,7},{7,6},{8,9},{9,8},{10,11... | collective-permute-start | bytes 479240 | tf_op jit(solution)/shard_map/ppermute | solution.py:29
  40.3 1.4 collective-permute-start.10
  48.7 2.7 %collective-permute-start.11 = (bf16[208,512]{1,0:T(8,128)(2,1)S(1)}, bf16[208,512]{1,0:T(8,128)(2,1)S(1)}, u32[]{:S(2)}, u32[]{:S(2)}) collective-permute-start(bf16[208,512]{1,0:T(8,128)(2,1)S(1)} %get-tuple-element.49), channel_id=1, source_target_pairs={{0,1},{1,0},{2,3},{3,2},{4,5},{5,4},{6,7},{7,6},{8,9},{9,8},{10,11... | collective-permute-start | bytes 638984 | tf_op jit(solution)/shard_map/ppermute | solution.py:29
  49.0 2.3 %collective-permute-start.13 = (bf16[208,512]{1,0:T(8,128)(2,1)S(1)}, bf16[208,512]{1,0:T(8,128)(2,1)S(1)}, u32[]{:S(2)}, u32[]{:S(2)}) collective-permute-start(bf16[208,512]{1,0:T(8,128)(2,1)S(1)} %get-tuple-element.51), channel_id=1, source_target_pairs={{0,1},{1,0},{2,3},{3,2},{4,5},{5,4},{6,7},{7,6},{8,9},{9,8},{10,11... | collective-permute-start | bytes 638984 | tf_op jit(solution)/shard_map/ppermute | solution.py:29
  49.2 2.1 %collective-permute-start.12 = (bf16[208,384]{1,0:T(8,128)(2,1)S(1)}, bf16[208,384]{1,0:T(8,128)(2,1)S(1)}, u32[]{:S(2)}, u32[]{:S(2)}) collective-permute-start(bf16[208,384]{1,0:T(8,128)(2,1)S(1)} %get-tuple-element.50), channel_id=1, source_target_pairs={{0,1},{1,0},{2,3},{3,2},{4,5},{5,4},{6,7},{7,6},{8,9},{9,8},{10,11... | collective-permute-start | bytes 479240 | tf_op jit(solution)/shard_map/ppermute | solution.py:29
  49.5 1.8 %collective-permute-start.14 = (bf16[208,384]{1,0:T(8,128)(2,1)S(1)}, bf16[208,384]{1,0:T(8,128)(2,1)S(1)}, u32[]{:S(2)}, u32[]{:S(2)}) collective-permute-start(bf16[208,384]{1,0:T(8,128)(2,1)S(1)} %get-tuple-element.52), channel_id=1, source_target_pairs={{0,1},{1,0},{2,3},{3,2},{4,5},{5,4},{6,7},{7,6},{8,9},{9,8},{10,11... | collective-permute-start | bytes 479240 | tf_op jit(solution)/shard_map/ppermute | solution.py:29
  49.8 19.5 %collective-permute-start.16 = (bf16[208,1792]{1,0:T(8,128)(2,1)S(1)}, bf16[208,1792]{1,0:T(8,128)(2,1)S(1)}, u32[]{:S(2)}, u32[]{:S(2)}) collective-permute-start(bf16[208,1792]{1,0:T(8,128)(2,1)S(1)} %get-tuple-element.47.refs_0_), channel_id=1, source_target_pairs={{0,2},{1,3},{2,0},{3,1},{4,6},{5,7},{6,4},{7,5},{8,10},{9,11},{10,... | collective-permute-start | bytes 2236424 | tf_op jit(solution)/shard_map/ppermute | solution.py:29
  58.5 10.7 %collective-permute-start.15 = (bf16[208,1792]{1,0:T(8,128)(2,1)S(1)}, bf16[208,1792]{1,0:T(8,128)(2,1)S(1)}, u32[]{:S(2)}, u32[]{:S(2)}) collective-permute-start(bf16[208,1792]{1,0:T(8,128)(2,1)S(1)} %get-tuple-element.55), channel_id=1, source_target_pairs={{0,1},{1,0},{2,3},{3,2},{4,5},{5,4},{6,7},{7,6},{8,9},{9,8},{10,11... | collective-permute-start | bytes 2236424 | tf_op jit(solution)/shard_map/ppermute | solution.py:29
  58.6 26.0 %collective-permute-start.18 = (bf16[208,1792]{1,0:T(8,128)(2,1)S(1)}, bf16[208,1792]{1,0:T(8,128)(2,1)S(1)}, u32[]{:S(2)}, u32[]{:S(2)}) collective-permute-start(bf16[208,1792]{1,0:T(8,128)(2,1)S(1)} %get-tuple-element.53.refs_0_), channel_id=1, source_target_pairs={{0,2},{1,3},{2,0},{3,1},{4,6},{5,7},{6,4},{7,5},{8,10},{9,11},{10,... | collective-permute-start | bytes 2236424 | tf_op jit(solution)/shard_map/ppermute | solution.py:29
  76.7 7.9 %collective-permute-start.17 = (bf16[208,1792]{1,0:T(8,128)(2,1)S(1)}, bf16[208,1792]{1,0:T(8,128)(2,1)S(1)}, u32[]{:S(2)}, u32[]{:S(2)}) collective-permute-start(bf16[208,1792]{1,0:T(8,128)(2,1)S(1)} %get-tuple-element.58), channel_id=1, source_target_pairs={{0,1},{1,0},{2,3},{3,2},{4,5},{5,4},{6,7},{7,6},{8,9},{9,8},{10,11... | collective-permute-start | bytes 2236424 | tf_op jit(solution)/shard_map/ppermute | solution.py:29
  76.8 2.7 %collective-permute-start.19 = (bf16[208,896]{1,0:T(8,128)(2,1)S(1)}, bf16[208,896]{1,0:T(8,128)(2,1)S(1)}, u32[]{:S(2)}, u32[]{:S(2)}) collective-permute-start(bf16[208,896]{1,0:T(8,128)(2,1)S(1)} %silu.2.refs_0_.h0), channel_id=1, source_target_pairs={{0,1},{1,0},{2,3},{3,2},{4,5},{5,4},{6,7},{7,6},{8,9},{9,8},{10,11... | collective-permute-start | bytes 1118216 | tf_op jit(solution)/shard_map/ppermute | solution.py:29
  85.4 1.8 %collective-permute-start.21 = (bf16[208,896]{1,0:T(8,128)(2,1)S(1)}, bf16[208,896]{1,0:T(8,128)(2,1)S(1)}, u32[]{:S(2)}, u32[]{:S(2)}) collective-permute-start(bf16[208,896]{1,0:T(8,128)(2,1)S(1)} %silu.3.h0), channel_id=1, source_target_pairs={{0,1},{1,0},{2,3},{3,2},{4,5},{5,4},{6,7},{7,6},{8,9},{9,8},{10,11... | collective-permute-start | bytes 1118216 | tf_op jit(solution)/shard_map/ppermute | solution.py:29
  85.5 11.1 %collective-permute-start.20 = (bf16[208,896]{1,0:T(8,128)(2,1)S(1)}, bf16[208,896]{1,0:T(8,128)(2,1)S(1)}, u32[]{:S(2)}, u32[]{:S(2)}) collective-permute-start(bf16[208,896]{1,0:T(8,128)(2,1)S(1)} %silu.3.h0), channel_id=1, source_target_pairs={{0,2},{1,3},{2,0},{3,1},{4,6},{5,7},{6,4},{7,5},{8,10},{9,11},{10,... | collective-permute-start | bytes 1118216 | tf_op jit(solution)/shard_map/ppermute | solution.py:29
  96.6 1.8 %collective-permute-start.22 = (bf16[208,896]{1,0:T(8,128)(2,1)S(1)}, bf16[208,896]{1,0:T(8,128)(2,1)S(1)}, u32[]{:S(2)}, u32[]{:S(2)}) collective-permute-start(bf16[208,896]{1,0:T(8,128)(2,1)S(1)} %relay.2.h0), channel_id=1, source_target_pairs={{0,1},{1,0},{2,3},{3,2},{4,5},{5,4},{6,7},{7,6},{8,9},{9,8},{10,11... | collective-permute-start | bytes 1118216 | tf_op jit(solution)/shard_map/ppermute | solution.py:29
  96.7 11.1 %collective-permute-start.26 = (bf16[208,896]{1,0:T(8,128)(2,1)S(1)}, bf16[208,896]{1,0:T(8,128)(2,1)S(1)}, u32[]{:S(2)}, u32[]{:S(2)}) collective-permute-start(bf16[208,896]{1,0:T(8,128)(2,1)S(1)} %silu.2.refs_0_.h0), channel_id=1, source_target_pairs={{0,2},{1,3},{2,0},{3,1},{4,6},{5,7},{6,4},{7,5},{8,10},{9,11},{10,... | collective-permute-start | bytes 1118216 | tf_op jit(solution)/shard_map/ppermute | solution.py:29
  103.1 40.8 %copy-start.1 = (bf16[96,2048]{1,0:T(8,128)(2,1)S(1)}, bf16[96,2048]{1,0:T(8,128)(2,1)}, u32[]{:S(2)}) copy-start(bf16[96,2048]{1,0:T(8,128)(2,1)} %tokens_ref.1) | copy-start | bytes 1179652
  103.1 40.8 %copy-start.5 = (s32[1,72]{1,0:T(1,128)S(1)}, s32[1,72]{1,0:T(1,128)}, u32[]{:S(2)}) copy-start(s32[1,72]{1,0:T(1,128)} %chosen_ref.1) | copy-start | bytes 868
  103.1 40.8 %copy-start.6 = (f32[96]{0:T(128)S(1)}, f32[96]{0:T(128)}, u32[]{:S(2)}) copy-start(f32[96]{0:T(128)} %param.11) | copy-start | bytes 1156
  107.8 3.6 %collective-permute-start.27 = (bf16[208,896]{1,0:T(8,128)(2,1)S(1)}, bf16[208,896]{1,0:T(8,128)(2,1)S(1)}, u32[]{:S(2)}, u32[]{:S(2)}) collective-permute-start(bf16[208,896]{1,0:T(8,128)(2,1)S(1)} %relay.3.h0), channel_id=1, source_target_pairs={{0,1},{1,0},{2,3},{3,2},{4,5},{5,4},{6,7},{7,6},{8,9},{9,8},{10,11... | collective-permute-start | bytes 1118216 | tf_op jit(solution)/shard_map/ppermute | solution.py:29
  107.9 10.1 %collective-permute-start.23 = (bf16[72,2048]{1,0:T(8,128)(2,1)S(1)}, bf16[72,2048]{1,0:T(8,128)(2,1)S(1)}, u32[]{:S(2)}, u32[]{:S(2)}) collective-permute-start(bf16[72,2048]{1,0:T(8,128)(2,1)S(1)} %get-tuple-element.62), channel_id=1, source_target_pairs={{0,4},{4,0},{8,12},{12,8},{16,20},{20,16},{24,28},{28,24},{1,5},{5... | collective-permute-start | bytes 884744 | tf_op jit(solution)/shard_map/ppermute | solution.py:29
  108.6 10.9 %collective-permute-start.24 = (bf16[72,2048]{1,0:T(8,128)(2,1)S(1)}, bf16[72,2048]{1,0:T(8,128)(2,1)S(1)}, u32[]{:S(2)}, u32[]{:S(2)}) collective-permute-start(bf16[72,2048]{1,0:T(8,128)(2,1)S(1)} %get-tuple-element.63), channel_id=1, source_target_pairs={{0,8},{4,12},{8,0},{12,4},{16,24},{20,28},{24,16},{28,20},{1,9},{5... | collective-permute-start | bytes 884744 | tf_op jit(solution)/shard_map/ppermute | solution.py:29
  110.0 15.6 %collective-permute-start.25 = (bf16[72,2048]{1,0:T(8,128)(2,1)S(1)}, bf16[72,2048]{1,0:T(8,128)(2,1)S(1)}, u32[]{:S(2)}, u32[]{:S(2)}) collective-permute-start(bf16[72,2048]{1,0:T(8,128)(2,1)S(1)} %get-tuple-element.64), channel_id=1, source_target_pairs={{0,12},{4,8},{8,4},{12,0},{16,28},{20,24},{24,20},{28,16},{1,13},{... | collective-permute-start | bytes 884744 | tf_op jit(solution)/shard_map/ppermute | solution.py:29
  115.9 14.7 %collective-permute-start.29 = (bf16[72,2048]{1,0:T(8,128)(2,1)S(1)}, bf16[72,2048]{1,0:T(8,128)(2,1)S(1)}, u32[]{:S(2)}, u32[]{:S(2)}) collective-permute-start(bf16[72,2048]{1,0:T(8,128)(2,1)S(1)} %get-tuple-element.66), channel_id=1, source_target_pairs={{0,4},{4,0},{8,12},{12,8},{16,20},{20,16},{24,28},{28,24},{1,5},{5... | collective-permute-start | bytes 884744 | tf_op jit(solution)/shard_map/ppermute | solution.py:29
  116.6 20.9 %collective-permute-start.30 = (bf16[72,2048]{1,0:T(8,128)(2,1)S(1)}, bf16[72,2048]{1,0:T(8,128)(2,1)S(1)}, u32[]{:S(2)}, u32[]{:S(2)}) collective-permute-start(bf16[72,2048]{1,0:T(8,128)(2,1)S(1)} %get-tuple-element.67), channel_id=1, source_target_pairs={{0,8},{4,12},{8,0},{12,4},{16,24},{20,28},{24,16},{28,20},{1,9},{5... | collective-permute-start | bytes 884744 | tf_op jit(solution)/shard_map/ppermute | solution.py:29
  118.0 25.8 %collective-permute-start.31 = (bf16[72,2048]{1,0:T(8,128)(2,1)S(1)}, bf16[72,2048]{1,0:T(8,128)(2,1)S(1)}, u32[]{:S(2)}, u32[]{:S(2)}) collective-permute-start(bf16[72,2048]{1,0:T(8,128)(2,1)S(1)} %get-tuple-element.68), channel_id=1, source_target_pairs={{0,12},{4,8},{8,4},{12,0},{16,28},{20,24},{24,20},{28,16},{1,13},{... | collective-permute-start | bytes 884744 | tf_op jit(solution)/shard_map/ppermute | solution.py:29
  125.8 18.0 %collective-permute-start.28 = (bf16[72,2048]{1,0:T(8,128)(2,1)S(1)}, bf16[72,2048]{1,0:T(8,128)(2,1)S(1)}, u32[]{:S(2)}, u32[]{:S(2)}) collective-permute-start(bf16[72,2048]{1,0:T(8,128)(2,1)S(1)} %sum.1), channel_id=1, source_target_pairs={{0,16},{4,20},{8,24},{12,28},{16,0},{20,4},{24,8},{28,12},{1,17},{... | collective-permute-start | bytes 884744 | tf_op jit(solution)/shard_map/ppermute | solution.py:29

commit v3 on v2

--- a/solution.py
+++ b/solution.py
@@ -32,7 +32,9 @@
 def call(kernel, outs, operands, specs, name, limit, scratch=(), after=()):
     made = pl.pallas_call(
         kernel,
-        out_shape=[jax.ShapeDtypeStruct(shape, dtype) for shape, dtype in outs],
+        out_shape=[
+            jax.ShapeDtypeStruct(*out) if isinstance(out, tuple) else out for out in outs
+        ],
         in_specs=list(specs) + [ANY] * len(after),
         out_specs=[VMEM] * len(outs),
         scratch_shapes=list(scratch),
@@ -149,9 +151,11 @@
         term = jnp.dot(x_ref[...], buffer[tile % slots, :, :width], preferred_element_type=F32)
         if tile + slots < len(tiles):
             copy(tile + slots).start()
-        if step == 1 or count == 2:
+        if step == 1:
             place = pl.ds(array * share_width + offset, width)
-            outs[step - 2][:, place] = term.astype(BF16)
+            outs[-1][:, place] = term.astype(BF16)
+        elif count == 3:
+            outs[array][:, pl.ds(offset, width)] = term.astype(BF16)
         elif tile == 0:
             outs[0][: rows - 16, :] = term[: rows - 16].astype(BF16)
             outs[0][rows - 16 :, :] = coded(s_ref[0:1, :], term[rows - 16 :])
@@ -173,11 +177,12 @@
         ]
         joined = [jnp.concatenate(pair, axis=1) for pair in out]
         if mine:
-            return joined
+            return out[0] + joined[1:]
         return [coded(squares[0:1], out[0][0]), out[0][1], joined[1]]
     whole = ((rows, 2 * width), BF16)
     pieces = [((rows, w), BF16) for _ in range(2) for _, w in cuts]
-    outs = [whole] * 2 if mine else pieces + [whole]
+    outs = [((rows, width), BF16)] * 2 if mine else pieces
+    outs = outs + [whole]
     return call(
         functools.partial(
             gate_up_kernel, share_width=width, cuts=cuts, shares=shares, count=len(outs)
@@ -221,8 +226,8 @@
     )
 
 
-def silu_kernel(a_ref, b_ref, c_ref, s_ref, *refs):
-    out_ref = refs[-1]
+def silu_kernel(a_ref, g_ref, u_ref, c_ref, s_ref, *refs, cuts):
+    out_ref, pieces = refs[-1 - len(cuts)], refs[-len(cuts) :]
     rows, width = out_ref.shape
     squares = s_ref[0:1, :] + decoded(c_ref[rows - 16 :, :])
     row = lax.broadcasted_iota(jnp.int32, (rows, LANES), 0)
@@ -230,60 +235,80 @@
     column = jnp.sum(jnp.where(row == lane, squares, 0.0), axis=1, keepdims=True)
     scale = jnp.where(row[:, :1] < rows - SPARE, lax.rsqrt(column / D + EPS), 0.0)
 
-    def total(part):
-        return (
-            a_ref[:, part].astype(F32) + b_ref[:, part].astype(F32) + c_ref[:, part].astype(F32)
-        ) * scale
-
-    gate, up = total(slice(0, width)), total(slice(width, 2 * width))
-    out_ref[...] = (gate / (1.0 + jnp.exp(-gate)) * up).astype(BF16)
-
-
-def silu(a, b, c, squares, after):
+    def total(got, part):
+        return (a_ref[:, part].astype(F32) + got[...].astype(F32) + c_ref[:, part].astype(F32)) * scale
+
+    gate, up = total(g_ref, slice(0, width)), total(u_ref, slice(width, 2 * width))
+    hidden = (gate / (1.0 + jnp.exp(-gate)) * up).astype(BF16)
+    out_ref[...] = hidden
+    for piece, (offset, part) in zip(pieces, cuts):
+        piece[...] = hidden[:, offset : offset + part]
+
+
+def silu(a, gate, up, c, squares, cuts, after):
     rows, width = a.shape
     return call(
-        silu_kernel,
-        [((rows, width // 2), BF16)],
-        (a, b, c, squares),
-        [VMEM] * 4,
+        functools.partial(silu_kernel, cuts=cuts),
+        [((rows, width // 2), BF16)] + [((rows, part), BF16) for _, part in cuts],
+        (a, gate, up, c, squares),
+        [VMEM] * 5,
         "silu",
         16,
         after=after,
-    )[0]
-
-
-def relay_kernel(in_ref, *refs):
-    refs[-1][...] = in_ref[...]
-
-
-def relay(value, after):
-    return call(relay_kernel, [(value.shape, value.dtype)], (value,), [VMEM], "relay", 16, after=after)[0]
-
-
-def down_kernel(me_ref, extras_ref, h0, h1, w_ref, *refs, shares, parts, window, last):
-    outs, (acc, buffer, sems) = refs[-GROUP - 3 if last else -4 : -3], refs[-3:]
+    )
+
+
+def relay_kernel(in_ref, *refs, cuts):
+    whole, pieces = refs[-1 - len(cuts)], refs[-len(cuts) :]
+    whole[...] = in_ref[...]
+    for piece, (offset, width) in zip(pieces, cuts):
+        piece[...] = in_ref[:, offset : offset + width]
+
+
+def relay(value, cuts, after):
+    rows, _ = value.shape
+    return call(
+        functools.partial(relay_kernel, cuts=cuts),
+        [(value.shape, BF16)] + [((rows, width), BF16) for _, width in cuts],
+        (value,),
+        [VMEM],
+        "relay",
+        16,
+        after=after,
+    )
+
+
+def down_kernel(me_ref, extras_ref, w_ref, *refs, tiles, sources, share_width, window, last):
     me = me_ref[0]
-    width = h0.shape[1]
-    depth = width // parts
-    tiles = [(number, part) for number in range(2) for part in range(parts)]
-
-    def copy(tile):
-        number, part = tiles[tile]
-        begin = pl.multiple_of((me ^ shares[number]) * width + part * depth, 16)
-        return pltpu.make_async_copy(w_ref.at[pl.ds(begin, depth), :], buffer.at[tile], sems.at[tile])
-
-    for tile in range(len(tiles)):
-        copy(tile).start()
-    for tile, (number, part) in enumerate(tiles):
-        copy(tile).wait()
-        hidden = (h0, h1)[number][:, part * depth : (part + 1) * depth]
-        term = jnp.dot(hidden, buffer[tile], preferred_element_type=F32)
+    if last:
+        outs, acc, buffer = refs[-GROUP - 1 : -1], refs[-1], w_ref
+    else:
+        (out, ahead), (acc, buffer, sems) = refs[-5:-3], refs[-3:]
+
+    def copy(tile, later):
+        share, offset, depth, _, _ = tiles[tile]
+        begin = pl.multiple_of((me ^ share ^ (2 * later)) * share_width + offset, 16)
+        target = (ahead if later else buffer).at[tile, pl.ds(0, depth), :]
+        sem = sems.at[later * len(tiles) + tile]
+        return pltpu.make_async_copy(w_ref.at[pl.ds(begin, depth), :], target, sem)
+
+    if not last:
+        for later in range(2):
+            for tile in range(len(tiles)):
+                copy(tile, later).start()
+    for tile, (_, _, depth, source, begin) in enumerate(tiles):
+        if not last:
+            copy(tile, 0).wait()
+        hidden = refs[source][:, begin : begin + depth]
+        term = jnp.dot(hidden, buffer[tile, :depth, :], preferred_element_type=F32)
         if tile == 0:
-            acc[...] = refs[0][...] + term if last else term
+            acc[...] = refs[sources][...] + term if last else term
         else:
             acc[...] += term
     if not last:
-        outs[0][...] = acc[...]
+        out[...] = acc[...]
+        for tile in range(len(tiles)):
+            copy(tile, 1).wait()
         return
 
     partial = acc[...].astype(BF16)
@@ -299,25 +324,31 @@
         start = start + extras
 
 
-def down(me, extras, w_down, hiddens, before, window, after):
+def down(me, extras, w_down, hiddens, cuts, before, window, after):
     rows, width = hiddens[0].shape
     feats = w_down.shape[1]
     last = before is not None
-    parts = 2 if width % 32 == 0 else 1
+    tiles = [(0, offset, depth, 0, offset) for offset, depth in cuts]
+    for number, (offset, depth) in enumerate(cuts):
+        source, begin = (number + 1, 0) if len(hiddens) > 2 else (1, offset)
+        tiles.append((1, offset, depth, source, begin))
+    held = pltpu.VMEM((len(tiles), max(depth for _, depth in cuts), feats), BF16)
     return call(
         functools.partial(
-            down_kernel, shares=(2, 3) if last else (0, 1), parts=parts, window=window, last=last
+            down_kernel,
+            tiles=tiles,
+            sources=len(hiddens),
+            share_width=width,
+            window=window,
+            last=last,
         ),
-        [((SURE + window, feats), BF16)] * GROUP if last else [((rows, feats), F32)],
-        (me, extras, *hiddens, w_down) + ((before,) if last else ()),
-        [SMEM, VMEM, VMEM, VMEM, HBM] + [VMEM] * last,
+        [((SURE + window, feats), BF16)] * GROUP if last else [((rows, feats), F32), held],
+        (me, extras, before[1] if last else w_down, *hiddens) + ((before[0],) if last else ()),
+        [SMEM, VMEM, VMEM if last else HBM] + [VMEM] * (len(hiddens) + last),
         f"down_{rows}_{int(last)}",
-        50,
-        scratch=[
-            pltpu.VMEM((rows, feats), F32),
-            pltpu.VMEM((2 * parts, width // parts, feats), BF16),
-            pltpu.SemaphoreType.DMA((2 * parts,)),
-        ],
+        32,
+        scratch=[pltpu.VMEM((rows, feats), F32)]
+        + ([] if last else [held, pltpu.SemaphoreType.DMA((2 * len(tiles),))]),
         after=after,
     )
 
@@ -377,26 +408,27 @@
         after = [outgoing]
     owns, cores, parts = [], [], []
     for (x, squares, extras), (across, two) in zip(chunks, begun):
-        send, keep = gate_up(me, x, squares, *weights, True, after)
-        own = silu(keep, swap(send, "tp", tp, 1), across, two, parts[:1])
+        *sends, keep = gate_up(me, x, squares, *weights, True, after)
+        gots = [swap(piece, "tp", tp, 1) for piece in sends]
+        own, *pieces = silu(keep, *gots, across, two, cuts, parts[0][:1] if parts else [])
         after = [own]
         owns.append(own)
-        cores.append(swap(own, "tp", tp, 1))
+        cores.append([swap(piece, "tp", tp, 1) for piece in pieces])
         if not parts:
-            parts.append(down(me, extras, w_down, (own, cores[0]), None, window, [])[0])
+            parts.append(down(me, extras, w_down, (own, *cores[0]), cuts, None, window, []))
 
     blocks, behind = [], []
     for number in [*range(1, len(chunks)), 0]:
         extras = chunks[number][2]
         other_y = swap(owns[number], "tp", tp, 2)
         if number:
-            hidden = (owns[number], cores[number])
-            part = down(me, extras, w_down, hidden, None, window, behind)[0]
+            hidden = (owns[number], *cores[number])
+            part = down(me, extras, w_down, hidden, cuts, None, window, behind)
         else:
             part = parts[0]
-        other_y = relay(other_y, [part] + behind)
-        both = swap(other_y, "tp", tp, 1)
-        blocks.append(down(me, extras, w_down, (other_y, both), part, window, []))
+        other_y, *pieces = relay(other_y, cuts, part[:1] + behind)
+        both = [swap(piece, "tp", tp, 1) for piece in pieces]
+        blocks.append(down(me, extras, w_down, (other_y, *both), cuts, part, window, []))
         behind = blocks[-1][:1]
 
     total = 0.0

time: 145 us -> 133 us (0.917)
  waiting for transfers between devices: 63.1 us -> 51.9 us
    ppermute x32 -> x38, waiting for transfers between devices: 63.1 us -> 51.9 us  [swap(): return lax.ppermute(value, axis, [(i, i ^ bit) for i in range(size)])]
    ppermute x32 -> x38, starting transfers between devices: 28.8 us -> 29 us  [swap(): return lax.ppermute(value, axis, [(i, i ^ bit) for i in range(size)])]
  transfers between devices with their start and end apart: 32 -> 38, of which waited for: 13 -> 17; matrix products, arithmetic and copies ran while one was open for 0% -> 0% of each run, Pallas kernels for 28% -> 35%
where the time goes in v3:
time: 133 us
  waiting for transfers between devices  51.9 us (39%)
  Pallas kernels  47.9 us (36%)
  starting transfers between devices  29 us (22%)
  local copies, waits for them, and re-layouts  2.37 us (2%)
    ppermute x38, waiting for transfers between devices, swap(): return lax.ppermute(value, axis, [(i, i ^ bit) for i in range(size)])  51.9 us
    pallas_call x18, Pallas kernels, call(): pl.pallas_call(kernel, out_shape=[jax.ShapeDtypeStruct(*out) if isinstanc...  47.9 us
    ppermute x38, starting transfers between devices, swap(): return lax.ppermute(value, axis, [(i, i ^ bit) for i in range(size)])  29 us
  transfers between devices with their start and end apart: 38, of which 17 were waited for; matrix products, arithmetic and copies ran while one was open for 0% of the time, Pallas kernels for 35%

profile of v3, /device:TPU:0, one launch (start us, length us, event | category | flops | bytes accessed | tf_op | source)
XLA Modules:
  0.0 133.2 jit_solution(8775755717730130512)
XLA Ops:
  0.7 1.0 copy-done
  1.7 0.7 copy-done.4
  2.6 4.1 %collective-permute-start = (bf16[72,2048]{1,0:T(8,128)(2,1)S(1)}, bf16[72,2048]{1,0:T(8,128)(2,1)S(1)}, u32[]{:S(2)}, u32[]{:S(2)}) collective-permute-start(bf16[72,2048]{1,0:T(8,128)(2,1)S(1)} %pick.1.refs_0_), channel_id=1, source_target_pairs={{0,16},{4,20},{8,24},{12,28},{16,0},{20,4},{24,8},{28,12},{1,17},{... | collective-permute-start | bytes 884744 | tf_op jit(solution)/shard_map/ppermute | solution.py:29
  6.7 2.5 %collective-permute-start.6 = (bf16[72,2048]{1,0:T(8,128)(2,1)S(1)}, bf16[72,2048]{1,0:T(8,128)(2,1)S(1)}, u32[]{:S(2)}, u32[]{:S(2)}) collective-permute-start(bf16[72,2048]{1,0:T(8,128)(2,1)S(1)} %pick.1.refs_0_), channel_id=1, source_target_pairs={{0,12},{4,8},{8,4},{12,0},{16,28},{20,24},{24,20},{28,16},{1,13},{... | collective-permute-start | bytes 884744 | tf_op jit(solution)/shard_map/ppermute | solution.py:29
  9.6 0.5 collective-permute-start.4
  10.2 9.9 %collective-permute-done.refs_0_ = bf16[72,2048]{1,0:T(8,128)(2,1)S(1)} collective-permute-done((bf16[72,2048]{1,0:T(8,128)(2,1)S(1)}, bf16[72,2048]{1,0:T(8,128)(2,1)S(1)}, u32[]{:S(2)}, u32[]{:S(2)}) %collective-permute-start) | collective-permute-done | bytes 294944 | tf_op jit(solution)/shard_map/ppermute | solution.py:29
  20.1 1.6 %collective-permute-start.3 = (bf16[72,2048]{1,0:T(8,128)(2,1)S(1)}, bf16[72,2048]{1,0:T(8,128)(2,1)S(1)}, u32[]{:S(2)}, u32[]{:S(2)}) collective-permute-start(bf16[72,2048]{1,0:T(8,128)(2,1)S(1)} %collective-permute-done.refs_0_), channel_id=1, source_target_pairs={{0,12},{4,8},{8,4},{12,0},{16,28},{20,24},{24,20},{28,16},{1,13},{... | collective-permute-start | bytes 884744 | tf_op jit(solution)/shard_map/ppermute | solution.py:29
  21.7 1.4 %collective-permute-start.2 = (bf16[72,2048]{1,0:T(8,128)(2,1)S(1)}, bf16[72,2048]{1,0:T(8,128)(2,1)S(1)}, u32[]{:S(2)}, u32[]{:S(2)}) collective-permute-start(bf16[72,2048]{1,0:T(8,128)(2,1)S(1)} %collective-permute-done.refs_0_), channel_id=1, source_target_pairs={{0,8},{4,12},{8,0},{12,4},{16,24},{20,28},{24,16},{28,20},{1,9},{5... | collective-permute-start | bytes 884744 | tf_op jit(solution)/shard_map/ppermute | solution.py:29
  23.1 1.1 collective-permute-start.1
  24.2 4.9 %collective-permute-done.5.refs_2_ = bf16[72,2048]{1,0:T(8,128)(2,1)S(1)} collective-permute-done((bf16[72,2048]{1,0:T(8,128)(2,1)S(1)}, bf16[72,2048]{1,0:T(8,128)(2,1)S(1)}, u32[]{:S(2)}, u32[]{:S(2)}) %collective-permute-start.5) | collective-permute-done | bytes 294944 | tf_op jit(solution)/shard_map/ppermute | solution.py:29
  29.1 0.7 copy-done.2
  29.8 1.1 assemble_208.3
  30.9 6.7 %gate_up_208_0.2 = (bf16[208,512]{1,0:T(8,128)(2,1)S(1)}, bf16[208,384]{1,0:T(8,128)(2,1)S(1)}, bf16[208,512]{1,0:T(8,128)(2,1)S(1)}, bf16[208,384]{1,0:T(8,128)(2,1)S(1)}, bf16[208,1792]{1,0:T(8,128)(2,1)S(1)}) custom-call(s32[1]{0:T(128)} %bitcast.2.me_ref, bf16[208,2048]{1,0:T(8,128)(2,1)S(1)} %get-tuple-element.58.x_ref, ...), custom_call_target="tpu_custom_call" | custom-call | tf_op jit(solution)/shard_map/gate_up_208_0/pallas_call | solution.py:33
  38.3 2.0 %collective-permute-done.2.refs_2_ = bf16[72,2048]{1,0:T(8,128)(2,1)S(1)} collective-permute-done((bf16[72,2048]{1,0:T(8,128)(2,1)S(1)}, bf16[72,2048]{1,0:T(8,128)(2,1)S(1)}, u32[]{:S(2)}, u32[]{:S(2)}) %collective-permute-start.2) | collective-permute-done | bytes 294944 | tf_op jit(solution)/shard_map/ppermute | solution.py:29
  40.3 1.1 assemble_208.2
  42.0 1.6 %collective-permute-start.17 = (bf16[208,1792]{1,0:T(8,128)(2,1)S(1)}, bf16[208,1792]{1,0:T(8,128)(2,1)S(1)}, u32[]{:S(2)}, u32[]{:S(2)}) collective-permute-start(bf16[208,1792]{1,0:T(8,128)(2,1)S(1)} %get-tuple-element.65.refs_0_), channel_id=1, source_target_pairs={{0,2},{1,3},{2,0},{3,1},{4,6},{5,7},{6,4},{7,5},{8,10},{9,11},{10,... | collective-permute-start | bytes 2236424 | tf_op jit(solution)/shard_map/ppermute | solution.py:29
  43.6 6.7 %gate_up_208_0.3 = (bf16[208,512]{1,0:T(8,128)(2,1)S(1)}, bf16[208,384]{1,0:T(8,128)(2,1)S(1)}, bf16[208,512]{1,0:T(8,128)(2,1)S(1)}, bf16[208,384]{1,0:T(8,128)(2,1)S(1)}, bf16[208,1792]{1,0:T(8,128)(2,1)S(1)}) custom-call(s32[1]{0:T(128)} %bitcast.2.me_ref, bf16[208,2048]{1,0:T(8,128)(2,1)S(1)} %get-tuple-element.56.refs_4_.x_ref, ...), custom_call_target="tpu_custom_call" | custom-call | tf_op jit(solution)/shard_map/gate_up_208_0/pallas_call | solution.py:33
  51.4 1.0 collective-permute-done.12.refs_1_
  52.9 6.9 %gate_up_208_1.2 = (bf16[208,896]{1,0:T(8,128)(2,1)S(1)}, bf16[208,896]{1,0:T(8,128)(2,1)S(1)}, bf16[208,1792]{1,0:T(8,128)(2,1)S(1)}) custom-call(s32[1]{0:T(128)} %bitcast.2.me_ref, bf16[208,2048]{1,0:T(8,128)(2,1)S(1)} %get-tuple-element.58.x_ref, f32[8,256]{1,0:T(8,128)S(1)} %get-tuple-element.59.s_ref, bf16[2048,3584]{1,0:T(8,128)(2,1)} %g_ref.7, ...), custom_call_target="tpu_custom_call" | custom-call | tf_op jit(solution)/shard_map/gate_up_208_1/pallas_call | solution.py:33
  60.8 0.7 collective-permute-done.15.g_ref
  61.6 0.5 collective-permute-done.16.u_ref
  62.1 0.8 silu.2
  62.9 6.7 %gate_up_208_1.3 = (bf16[208,896]{1,0:T(8,128)(2,1)S(1)}, bf16[208,896]{1,0:T(8,128)(2,1)S(1)}, bf16[208,1792]{1,0:T(8,128)(2,1)S(1)}) custom-call(s32[1]{0:T(128)} %bitcast.2.me_ref, bf16[208,2048]{1,0:T(8,128)(2,1)S(1)} %get-tuple-element.56.refs_4_.x_ref, f32[8,256]{1,0:T(8,128)S(1)} %get-tuple-element.57.s_ref, bf16[2048,3584]{1,0:T(8,128)(2,1)} %g_ref.7, ...), custom_call_target="tpu_custom_call" | custom-call | tf_op jit(solution)/shard_map/gate_up_208_1/pallas_call | solution.py:33
  70.7 1.7 %collective-permute-done.22.refs_2_ = bf16[208,384]{1,0:T(8,128)(2,1)S(1)} collective-permute-done((bf16[208,384]{1,0:T(8,128)(2,1)S(1)}, bf16[208,384]{1,0:T(8,128)(2,1)S(1)}, u32[]{:S(2)}, u32[]{:S(2)}) %collective-permute-start.22) | collective-permute-done | bytes 159776 | tf_op jit(solution)/shard_map/ppermute | solution.py:29
  72.4 5.3 %down_208_0.2 = (f32[208,2048]{1,0:T(8,128)S(1)}, bf16[4,512,2048]{2,1,0:T(8,128)(2,1)S(1)}) custom-call(s32[1]{0:T(128)} %bitcast.2.me_ref, f32[8,256]{1,0:T(8,128)S(1)} %get-tuple-element.81.extras_ref, bf16[3584,2048]{1,0:T(8,128)(2,1)} %w_ref.3, bf16[208,896]{1,0:T(8,128)(2,1)S(1)} %get-tuple-element.76.refs_0_, ...), custom_call_target="tpu_custom_call" | custom-call | tf_op jit(solution)/shard_map/down_208_0/pallas_call | solution.py:33
  77.7 1.4 %collective-permute-done.20.c_ref = bf16[208,1792]{1,0:T(8,128)(2,1)S(1)} collective-permute-done((bf16[208,1792]{1,0:T(8,128)(2,1)S(1)}, bf16[208,1792]{1,0:T(8,128)(2,1)S(1)}, u32[]{:S(2)}, u32[]{:S(2)}) %collective-permute-start.20) | collective-permute-done | bytes 745504 | tf_op jit(solution)/shard_map/ppermute | solution.py:29
  79.2 0.8 silu.3
  80.0 0.5 collective-permute-start.25
  80.5 0.5 collective-permute-start.24
  81.0 1.6 %collective-permute-start.31 = (bf16[208,896]{1,0:T(8,128)(2,1)S(1)}, bf16[208,896]{1,0:T(8,128)(2,1)S(1)}, u32[]{:S(2)}, u32[]{:S(2)}) collective-permute-start(bf16[208,896]{1,0:T(8,128)(2,1)S(1)} %get-tuple-element.76.refs_0_), channel_id=1, source_target_pairs={{0,2},{1,3},{2,0},{3,1},{4,6},{5,7},{6,4},{7,5},{8,10},{9,11},{10,... | collective-permute-start | bytes 1118216 | tf_op jit(solution)/shard_map/ppermute | solution.py:29
  82.6 5.3 %down_208_0.3 = (f32[208,2048]{1,0:T(8,128)S(1)}, bf16[4,512,2048]{2,1,0:T(8,128)(2,1)S(1)}) custom-call(s32[1]{0:T(128)} %bitcast.2.me_ref, f32[8,256]{1,0:T(8,128)S(1)} %get-tuple-element.55.extras_ref, bf16[3584,2048]{1,0:T(8,128)(2,1)} %w_ref.3, bf16[208,896]{1,0:T(8,128)(2,1)S(1)} %get-tuple-element.85.refs_0_, ...), custom_call_target="tpu_custom_call" | custom-call | tf_op jit(solution)/shard_map/down_208_0/pallas_call | solution.py:33
  87.9 3.8 %collective-permute-done.25.in_ref = bf16[208,896]{1,0:T(8,128)(2,1)S(1)} collective-permute-done((bf16[208,896]{1,0:T(8,128)(2,1)S(1)}, bf16[208,896]{1,0:T(8,128)(2,1)S(1)}, u32[]{:S(2)}, u32[]{:S(2)}) %collective-permute-start.25) | collective-permute-done | bytes 372768 | tf_op jit(solution)/shard_map/ppermute | solution.py:29
  92.3 1.2 collective-permute-done.27.refs_2_
  93.5 2.8 %down_208_1.2 = (bf16[72,2048]{1,0:T(8,128)(2,1)S(1)}, bf16[72,2048]{1,0:T(8,128)(2,1)S(1)}, bf16[72,2048]{1,0:T(8,128)(2,1)S(1)}, bf16[72,2048]{1,0:T(8,128)(2,1)S(1)}) custom-call(s32[1]{0:T(128)} %bitcast.2.me_ref, f32[8,256]{1,0:T(8,128)S(1)} %get-tuple-element.55.extras_ref, bf16[4,512,2048]{2,1,0:T(8,128)(2,1)S(1)} %get-tuple-element.88.w_ref, ...), custom_call_target="tpu_custom_call" | custom-call | tf_op jit(solution)/shard_map/down_208_1/pallas_call | solution.py:33
  96.3 0.6 collective-permute-start.28
  96.9 1.5 %collective-permute-start.29 = (bf16[72,2048]{1,0:T(8,128)(2,1)S(1)}, bf16[72,2048]{1,0:T(8,128)(2,1)S(1)}, u32[]{:S(2)}, u32[]{:S(2)}) collective-permute-start(bf16[72,2048]{1,0:T(8,128)(2,1)S(1)} %get-tuple-element.95), channel_id=1, source_target_pairs={{0,8},{4,12},{8,0},{12,4},{16,24},{20,28},{24,16},{28,20},{1,9},{5... | collective-permute-start | bytes 884744 | tf_op jit(solution)/shard_map/ppermute | solution.py:29
  98.4 1.5 %collective-permute-start.30 = (bf16[72,2048]{1,0:T(8,128)(2,1)S(1)}, bf16[72,2048]{1,0:T(8,128)(2,1)S(1)}, u32[]{:S(2)}, u32[]{:S(2)}) collective-permute-start(bf16[72,2048]{1,0:T(8,128)(2,1)S(1)} %get-tuple-element.96), channel_id=1, source_target_pairs={{0,12},{4,8},{8,4},{12,0},{16,28},{20,24},{24,20},{28,16},{1,13},{... | collective-permute-start | bytes 884744 | tf_op jit(solution)/shard_map/ppermute | solution.py:29
  100.5 1.2 collective-permute-done.33.refs_2_
  101.7 2.5 %down_208_1.3 = (bf16[72,2048]{1,0:T(8,128)(2,1)S(1)}, bf16[72,2048]{1,0:T(8,128)(2,1)S(1)}, bf16[72,2048]{1,0:T(8,128)(2,1)S(1)}, bf16[72,2048]{1,0:T(8,128)(2,1)S(1)}) custom-call(s32[1]{0:T(128)} %bitcast.2.me_ref, f32[8,256]{1,0:T(8,128)S(1)} %get-tuple-element.81.extras_ref, bf16[4,512,2048]{2,1,0:T(8,128)(2,1)S(1)} %get-tuple-element.97.w_ref, ...), custom_call_target="tpu_custom_call" | custom-call | tf_op jit(solution)/shard_map/down_208_1/pallas_call | solution.py:33
  104.3 0.6 collective-permute-start.35
  104.9 1.5 %collective-permute-start.36 = (bf16[72,2048]{1,0:T(8,128)(2,1)S(1)}, bf16[72,2048]{1,0:T(8,128)(2,1)S(1)}, u32[]{:S(2)}, u32[]{:S(2)}) collective-permute-start(bf16[72,2048]{1,0:T(8,128)(2,1)S(1)} %get-tuple-element.103), channel_id=1, source_target_pairs={{0,8},{4,12},{8,0},{12,4},{16,24},{20,28},{24,16},{28,20},{1,9},{5... | collective-permute-start | bytes 884744 | tf_op jit(solution)/shard_map/ppermute | solution.py:29
  106.3 1.5 %collective-permute-start.37 = (bf16[72,2048]{1,0:T(8,128)(2,1)S(1)}, bf16[72,2048]{1,0:T(8,128)(2,1)S(1)}, u32[]{:S(2)}, u32[]{:S(2)}) collective-permute-start(bf16[72,2048]{1,0:T(8,128)(2,1)S(1)} %get-tuple-element.104), channel_id=1, source_target_pairs={{0,12},{4,8},{8,4},{12,0},{16,28},{20,24},{24,20},{28,16},{1,13},{... | collective-permute-start | bytes 884744 | tf_op jit(solution)/shard_map/ppermute | solution.py:29
  107.8 6.3 %collective-permute-done.30.d_ref = bf16[72,2048]{1,0:T(8,128)(2,1)S(1)} collective-permute-done((bf16[72,2048]{1,0:T(8,128)(2,1)S(1)}, bf16[72,2048]{1,0:T(8,128)(2,1)S(1)}, u32[]{:S(2)}, u32[]{:S(2)}) %collective-permute-start.30) | collective-permute-done | bytes 294944 | tf_op jit(solution)/shard_map/ppermute | solution.py:29
  114.3 1.0 collective-permute-start.34
  115.3 3.7 %collective-permute-done.35 = bf16[72,2048]{1,0:T(8,128)(2,1)S(1)} collective-permute-done((bf16[72,2048]{1,0:T(8,128)(2,1)S(1)}, bf16[72,2048]{1,0:T(8,128)(2,1)S(1)}, u32[]{:S(2)}, u32[]{:S(2)}) %collective-permute-start.35) | collective-permute-done | bytes 294944 | tf_op jit(solution)/shard_map/ppermute | solution.py:29
  119.0 6.8 %collective-permute-done.36 = bf16[72,2048]{1,0:T(8,128)(2,1)S(1)} collective-permute-done((bf16[72,2048]{1,0:T(8,128)(2,1)S(1)}, bf16[72,2048]{1,0:T(8,128)(2,1)S(1)}, u32[]{:S(2)}, u32[]{:S(2)}) %collective-permute-start.36) | collective-permute-done | bytes 294944 | tf_op jit(solution)/shard_map/ppermute | solution.py:29
  125.8 6.2 %collective-permute-done.37 = bf16[72,2048]{1,0:T(8,128)(2,1)S(1)} collective-permute-done((bf16[72,2048]{1,0:T(8,128)(2,1)S(1)}, bf16[72,2048]{1,0:T(8,128)(2,1)S(1)}, u32[]{:S(2)}, u32[]{:S(2)}) %collective-permute-start.37) | collective-permute-done | bytes 294944 | tf_op jit(solution)/shard_map/ppermute | solution.py:29
  132.0 1.1 fusion.1
  (62 shorter events, 7.1 us)
Async XLA Ops:
  0.7 1.0 copy-start
  1.7 0.7 copy-start.4
  2.6 17.5 %collective-permute-start = (bf16[72,2048]{1,0:T(8,128)(2,1)S(1)}, bf16[72,2048]{1,0:T(8,128)(2,1)S(1)}, u32[]{:S(2)}, u32[]{:S(2)}) collective-permute-start(bf16[72,2048]{1,0:T(8,128)(2,1)S(1)} %pick.1.refs_0_), channel_id=1, source_target_pairs={{0,16},{4,20},{8,24},{12,28},{16,0},{20,4},{24,8},{28,12},{1,17},{... | collective-permute-start | bytes 884744 | tf_op jit(solution)/shard_map/ppermute | solution.py:29
  6.7 16.4 %collective-permute-start.6 = (bf16[72,2048]{1,0:T(8,128)(2,1)S(1)}, bf16[72,2048]{1,0:T(8,128)(2,1)S(1)}, u32[]{:S(2)}, u32[]{:S(2)}) collective-permute-start(bf16[72,2048]{1,0:T(8,128)(2,1)S(1)} %pick.1.refs_0_), channel_id=1, source_target_pairs={{0,12},{4,8},{8,4},{12,0},{16,28},{20,24},{24,20},{28,16},{1,13},{... | collective-permute-start | bytes 884744 | tf_op jit(solution)/shard_map/ppermute | solution.py:29
  9.2 19.9 %collective-permute-start.5 = (bf16[72,2048]{1,0:T(8,128)(2,1)S(1)}, bf16[72,2048]{1,0:T(8,128)(2,1)S(1)}, u32[]{:S(2)}, u32[]{:S(2)}) collective-permute-start(bf16[72,2048]{1,0:T(8,128)(2,1)S(1)} %pick.1.refs_0_), channel_id=1, source_target_pairs={{0,8},{4,12},{8,0},{12,4},{16,24},{20,28},{24,16},{28,20},{1,9},{5... | collective-permute-start | bytes 884744 | tf_op jit(solution)/shard_map/ppermute | solution.py:29
  9.6 19.4 %collective-permute-start.4 = (bf16[72,2048]{1,0:T(8,128)(2,1)S(1)}, bf16[72,2048]{1,0:T(8,128)(2,1)S(1)}, u32[]{:S(2)}, u32[]{:S(2)}) collective-permute-start(bf16[72,2048]{1,0:T(8,128)(2,1)S(1)} %pick.1.refs_0_), channel_id=1, source_target_pairs={{0,4},{4,0},{8,12},{12,8},{16,20},{20,16},{24,28},{28,24},{1,5},{5... | collective-permute-start | bytes 884744 | tf_op jit(solution)/shard_map/ppermute | solution.py:29
  20.1 18.1 %collective-permute-start.3 = (bf16[72,2048]{1,0:T(8,128)(2,1)S(1)}, bf16[72,2048]{1,0:T(8,128)(2,1)S(1)}, u32[]{:S(2)}, u32[]{:S(2)}) collective-permute-start(bf16[72,2048]{1,0:T(8,128)(2,1)S(1)} %collective-permute-done.refs_0_), channel_id=1, source_target_pairs={{0,12},{4,8},{8,4},{12,0},{16,28},{20,24},{24,20},{28,16},{1,13},{... | collective-permute-start | bytes 884744 | tf_op jit(solution)/shard_map/ppermute | solution.py:29
  21.7 18.6 %collective-permute-start.2 = (bf16[72,2048]{1,0:T(8,128)(2,1)S(1)}, bf16[72,2048]{1,0:T(8,128)(2,1)S(1)}, u32[]{:S(2)}, u32[]{:S(2)}) collective-permute-start(bf16[72,2048]{1,0:T(8,128)(2,1)S(1)} %collective-permute-done.refs_0_), channel_id=1, source_target_pairs={{0,8},{4,12},{8,0},{12,4},{16,24},{20,28},{24,16},{28,20},{1,9},{5... | collective-permute-start | bytes 884744 | tf_op jit(solution)/shard_map/ppermute | solution.py:29
  23.1 17.2 %collective-permute-start.1 = (bf16[72,2048]{1,0:T(8,128)(2,1)S(1)}, bf16[72,2048]{1,0:T(8,128)(2,1)S(1)}, u32[]{:S(2)}, u32[]{:S(2)}) collective-permute-start(bf16[72,2048]{1,0:T(8,128)(2,1)S(1)} %collective-permute-done.refs_0_), channel_id=1, source_target_pairs={{0,4},{4,0},{8,12},{12,8},{16,20},{20,16},{24,28},{28,24},{1,5},{5... | collective-permute-start | bytes 884744 | tf_op jit(solution)/shard_map/ppermute | solution.py:29
  29.1 0.7 copy-start.2
  30.9 9.4 %copy-start.3 = (f32[2048]{0:T(1024)S(1)}, f32[2048]{0:T(1024)}, u32[]{:S(2)}) copy-start(f32[2048]{0:T(1024)} %param.12) | copy-start | bytes 24580
  37.6 4.1 %collective-permute-start.7 = (bf16[208,512]{1,0:T(8,128)(2,1)S(1)}, bf16[208,512]{1,0:T(8,128)(2,1)S(1)}, u32[]{:S(2)}, u32[]{:S(2)}) collective-permute-start(bf16[208,512]{1,0:T(8,128)(2,1)S(1)} %get-tuple-element.61), channel_id=1, source_target_pairs={{0,1},{1,0},{2,3},{3,2},{4,5},{5,4},{6,7},{7,6},{8,9},{9,8},{10,11... | collective-permute-start | bytes 638984 | tf_op jit(solution)/shard_map/ppermute | solution.py:29
  37.7 4.0 %collective-permute-start.9 = (bf16[208,512]{1,0:T(8,128)(2,1)S(1)}, bf16[208,512]{1,0:T(8,128)(2,1)S(1)}, u32[]{:S(2)}, u32[]{:S(2)}) collective-permute-start(bf16[208,512]{1,0:T(8,128)(2,1)S(1)} %get-tuple-element.63), channel_id=1, source_target_pairs={{0,1},{1,0},{2,3},{3,2},{4,5},{5,4},{6,7},{7,6},{8,9},{9,8},{10,11... | collective-permute-start | bytes 638984 | tf_op jit(solution)/shard_map/ppermute | solution.py:29
  38.2 3.3 %collective-permute-start.8 = (bf16[208,384]{1,0:T(8,128)(2,1)S(1)}, bf16[208,384]{1,0:T(8,128)(2,1)S(1)}, u32[]{:S(2)}, u32[]{:S(2)}) collective-permute-start(bf16[208,384]{1,0:T(8,128)(2,1)S(1)} %get-tuple-element.62), channel_id=1, source_target_pairs={{0,1},{1,0},{2,3},{3,2},{4,5},{5,4},{6,7},{7,6},{8,9},{9,8},{10,11... | collective-permute-start | bytes 479240 | tf_op jit(solution)/shard_map/ppermute | solution.py:29
  40.3 1.4 %collective-permute-start.10 = (bf16[208,384]{1,0:T(8,128)(2,1)S(1)}, bf16[208,384]{1,0:T(8,128)(2,1)S(1)}, u32[]{:S(2)}, u32[]{:S(2)}) collective-permute-start(bf16[208,384]{1,0:T(8,128)(2,1)S(1)} %get-tuple-element.64), channel_id=1, source_target_pairs={{0,1},{1,0},{2,3},{3,2},{4,5},{5,4},{6,7},{7,6},{8,9},{9,8},{10,11... | collective-permute-start | bytes 479240 | tf_op jit(solution)/shard_map/ppermute | solution.py:29
  42.0 20.1 %collective-permute-start.17 = (bf16[208,1792]{1,0:T(8,128)(2,1)S(1)}, bf16[208,1792]{1,0:T(8,128)(2,1)S(1)}, u32[]{:S(2)}, u32[]{:S(2)}) collective-permute-start(bf16[208,1792]{1,0:T(8,128)(2,1)S(1)} %get-tuple-element.65.refs_0_), channel_id=1, source_target_pairs={{0,2},{1,3},{2,0},{3,1},{4,6},{5,7},{6,4},{7,5},{8,10},{9,11},{10,... | collective-permute-start | bytes 2236424 | tf_op jit(solution)/shard_map/ppermute | solution.py:29
  50.3 2.3 %collective-permute-start.11 = (bf16[208,512]{1,0:T(8,128)(2,1)S(1)}, bf16[208,512]{1,0:T(8,128)(2,1)S(1)}, u32[]{:S(2)}, u32[]{:S(2)}) collective-permute-start(bf16[208,512]{1,0:T(8,128)(2,1)S(1)} %get-tuple-element.67), channel_id=1, source_target_pairs={{0,1},{1,0},{2,3},{3,2},{4,5},{5,4},{6,7},{7,6},{8,9},{9,8},{10,11... | collective-permute-start | bytes 638984 | tf_op jit(solution)/shard_map/ppermute | solution.py:29
  50.4 2.2 %collective-permute-start.13 = (bf16[208,512]{1,0:T(8,128)(2,1)S(1)}, bf16[208,512]{1,0:T(8,128)(2,1)S(1)}, u32[]{:S(2)}, u32[]{:S(2)}) collective-permute-start(bf16[208,512]{1,0:T(8,128)(2,1)S(1)} %get-tuple-element.69), channel_id=1, source_target_pairs={{0,1},{1,0},{2,3},{3,2},{4,5},{5,4},{6,7},{7,6},{8,9},{9,8},{10,11... | collective-permute-start | bytes 638984 | tf_op jit(solution)/shard_map/ppermute | solution.py:29
  50.9 1.5 %collective-permute-start.12 = (bf16[208,384]{1,0:T(8,128)(2,1)S(1)}, bf16[208,384]{1,0:T(8,128)(2,1)S(1)}, u32[]{:S(2)}, u32[]{:S(2)}) collective-permute-start(bf16[208,384]{1,0:T(8,128)(2,1)S(1)} %get-tuple-element.68), channel_id=1, source_target_pairs={{0,1},{1,0},{2,3},{3,2},{4,5},{5,4},{6,7},{7,6},{8,9},{9,8},{10,11... | collective-permute-start | bytes 479240 | tf_op jit(solution)/shard_map/ppermute | solution.py:29
  51.0 1.6 %collective-permute-start.14 = (bf16[208,384]{1,0:T(8,128)(2,1)S(1)}, bf16[208,384]{1,0:T(8,128)(2,1)S(1)}, u32[]{:S(2)}, u32[]{:S(2)}) collective-permute-start(bf16[208,384]{1,0:T(8,128)(2,1)S(1)} %get-tuple-element.70), channel_id=1, source_target_pairs={{0,1},{1,0},{2,3},{3,2},{4,5},{5,4},{6,7},{7,6},{8,9},{9,8},{10,11... | collective-permute-start | bytes 479240 | tf_op jit(solution)/shard_map/ppermute | solution.py:29
  59.8 1.8 %collective-permute-start.15 = (bf16[208,896]{1,0:T(8,128)(2,1)S(1)}, bf16[208,896]{1,0:T(8,128)(2,1)S(1)}, u32[]{:S(2)}, u32[]{:S(2)}) collective-permute-start(bf16[208,896]{1,0:T(8,128)(2,1)S(1)} %get-tuple-element.73), channel_id=1, source_target_pairs={{0,1},{1,0},{2,3},{3,2},{4,5},{5,4},{6,7},{7,6},{8,9},{9,8},{10,11... | collective-permute-start | bytes 1118216 | tf_op jit(solution)/shard_map/ppermute | solution.py:29
  60.1 2.0 %collective-permute-start.16 = (bf16[208,896]{1,0:T(8,128)(2,1)S(1)}, bf16[208,896]{1,0:T(8,128)(2,1)S(1)}, u32[]{:S(2)}, u32[]{:S(2)}) collective-permute-start(bf16[208,896]{1,0:T(8,128)(2,1)S(1)} %get-tuple-element.74), channel_id=1, source_target_pairs={{0,1},{1,0},{2,3},{3,2},{4,5},{5,4},{6,7},{7,6},{8,9},{9,8},{10,11... | collective-permute-start | bytes 1118216 | tf_op jit(solution)/shard_map/ppermute | solution.py:29
  60.4 18.8 %collective-permute-start.20 = (bf16[208,1792]{1,0:T(8,128)(2,1)S(1)}, bf16[208,1792]{1,0:T(8,128)(2,1)S(1)}, u32[]{:S(2)}, u32[]{:S(2)}) collective-permute-start(bf16[208,1792]{1,0:T(8,128)(2,1)S(1)} %get-tuple-element.71.refs_0_), channel_id=1, source_target_pairs={{0,2},{1,3},{2,0},{3,1},{4,6},{5,7},{6,4},{7,5},{8,10},{9,11},{10,... | collective-permute-start | bytes 2236424 | tf_op jit(solution)/shard_map/ppermute | solution.py:29
  69.6 9.6 %collective-permute-start.18 = (bf16[208,896]{1,0:T(8,128)(2,1)S(1)}, bf16[208,896]{1,0:T(8,128)(2,1)S(1)}, u32[]{:S(2)}, u32[]{:S(2)}) collective-permute-start(bf16[208,896]{1,0:T(8,128)(2,1)S(1)} %get-tuple-element.78), channel_id=1, source_target_pairs={{0,1},{1,0},{2,3},{3,2},{4,5},{5,4},{6,7},{7,6},{8,9},{9,8},{10,11... | collective-permute-start | bytes 1118216 | tf_op jit(solution)/shard_map/ppermute | solution.py:29
  69.9 9.3 %collective-permute-start.19 = (bf16[208,896]{1,0:T(8,128)(2,1)S(1)}, bf16[208,896]{1,0:T(8,128)(2,1)S(1)}, u32[]{:S(2)}, u32[]{:S(2)}) collective-permute-start(bf16[208,896]{1,0:T(8,128)(2,1)S(1)} %get-tuple-element.79), channel_id=1, source_target_pairs={{0,1},{1,0},{2,3},{3,2},{4,5},{5,4},{6,7},{7,6},{8,9},{9,8},{10,11... | collective-permute-start | bytes 1118216 | tf_op jit(solution)/shard_map/ppermute | solution.py:29
  70.2 2.3 %collective-permute-start.21 = (bf16[208,512]{1,0:T(8,128)(2,1)S(1)}, bf16[208,512]{1,0:T(8,128)(2,1)S(1)}, u32[]{:S(2)}, u32[]{:S(2)}) collective-permute-start(bf16[208,512]{1,0:T(8,128)(2,1)S(1)} %get-tuple-element.82), channel_id=1, source_target_pairs={{0,1},{1,0},{2,3},{3,2},{4,5},{5,4},{6,7},{7,6},{8,9},{9,8},{10,11... | collective-permute-start | bytes 638984 | tf_op jit(solution)/shard_map/ppermute | solution.py:29
  70.4 2.1 %collective-permute-start.22 = (bf16[208,384]{1,0:T(8,128)(2,1)S(1)}, bf16[208,384]{1,0:T(8,128)(2,1)S(1)}, u32[]{:S(2)}, u32[]{:S(2)}) collective-permute-start(bf16[208,384]{1,0:T(8,128)(2,1)S(1)} %get-tuple-element.83), channel_id=1, source_target_pairs={{0,1},{1,0},{2,3},{3,2},{4,5},{5,4},{6,7},{7,6},{8,9},{9,8},{10,11... | collective-permute-start | bytes 479240 | tf_op jit(solution)/shard_map/ppermute | solution.py:29
  80.0 11.7 %collective-permute-start.25 = (bf16[208,896]{1,0:T(8,128)(2,1)S(1)}, bf16[208,896]{1,0:T(8,128)(2,1)S(1)}, u32[]{:S(2)}, u32[]{:S(2)}) collective-permute-start(bf16[208,896]{1,0:T(8,128)(2,1)S(1)} %get-tuple-element.85.refs_0_), channel_id=1, source_target_pairs={{0,2},{1,3},{2,0},{3,1},{4,6},{5,7},{6,4},{7,5},{8,10},{9,11},{10,... | collective-permute-start | bytes 1118216 | tf_op jit(solution)/shard_map/ppermute | solution.py:29
  80.5 2.1 %collective-permute-start.23 = (bf16[208,512]{1,0:T(8,128)(2,1)S(1)}, bf16[208,512]{1,0:T(8,128)(2,1)S(1)}, u32[]{:S(2)}, u32[]{:S(2)}) collective-permute-start(bf16[208,512]{1,0:T(8,128)(2,1)S(1)} %get-tuple-element.86), channel_id=1, source_target_pairs={{0,1},{1,0},{2,3},{3,2},{4,5},{5,4},{6,7},{7,6},{8,9},{9,8},{10,11... | collective-permute-start | bytes 638984 | tf_op jit(solution)/shard_map/ppermute | solution.py:29
  80.5 2.1 %collective-permute-start.24 = (bf16[208,384]{1,0:T(8,128)(2,1)S(1)}, bf16[208,384]{1,0:T(8,128)(2,1)S(1)}, u32[]{:S(2)}, u32[]{:S(2)}) collective-permute-start(bf16[208,384]{1,0:T(8,128)(2,1)S(1)} %get-tuple-element.87), channel_id=1, source_target_pairs={{0,1},{1,0},{2,3},{3,2},{4,5},{5,4},{6,7},{7,6},{8,9},{9,8},{10,11... | collective-permute-start | bytes 479240 | tf_op jit(solution)/shard_map/ppermute | solution.py:29
  81.0 18.9 %collective-permute-start.31 = (bf16[208,896]{1,0:T(8,128)(2,1)S(1)}, bf16[208,896]{1,0:T(8,128)(2,1)S(1)}, u32[]{:S(2)}, u32[]{:S(2)}) collective-permute-start(bf16[208,896]{1,0:T(8,128)(2,1)S(1)} %get-tuple-element.76.refs_0_), channel_id=1, source_target_pairs={{0,2},{1,3},{2,0},{3,1},{4,6},{5,7},{6,4},{7,5},{8,10},{9,11},{10,... | collective-permute-start | bytes 1118216 | tf_op jit(solution)/shard_map/ppermute | solution.py:29
  91.7 1.8 %collective-permute-start.26 = (bf16[208,512]{1,0:T(8,128)(2,1)S(1)}, bf16[208,512]{1,0:T(8,128)(2,1)S(1)}, u32[]{:S(2)}, u32[]{:S(2)}) collective-permute-start(bf16[208,512]{1,0:T(8,128)(2,1)S(1)} %get-tuple-element.91), channel_id=1, source_target_pairs={{0,1},{1,0},{2,3},{3,2},{4,5},{5,4},{6,7},{7,6},{8,9},{9,8},{10,11... | collective-permute-start | bytes 638984 | tf_op jit(solution)/shard_map/ppermute | solution.py:29
  91.8 1.7 %collective-permute-start.27 = (bf16[208,384]{1,0:T(8,128)(2,1)S(1)}, bf16[208,384]{1,0:T(8,128)(2,1)S(1)}, u32[]{:S(2)}, u32[]{:S(2)}) collective-permute-start(bf16[208,384]{1,0:T(8,128)(2,1)S(1)} %get-tuple-element.92), channel_id=1, source_target_pairs={{0,1},{1,0},{2,3},{3,2},{4,5},{5,4},{6,7},{7,6},{8,9},{9,8},{10,11... | collective-permute-start | bytes 479240 | tf_op jit(solution)/shard_map/ppermute | solution.py:29
  96.3 35.7 %copy-start.1 = (bf16[96,2048]{1,0:T(8,128)(2,1)S(1)}, bf16[96,2048]{1,0:T(8,128)(2,1)}, u32[]{:S(2)}) copy-start(bf16[96,2048]{1,0:T(8,128)(2,1)} %tokens_ref.1) | copy-start | bytes 1179652
  96.3 35.7 %copy-start.5 = (s32[1,72]{1,0:T(1,128)S(1)}, s32[1,72]{1,0:T(1,128)}, u32[]{:S(2)}) copy-start(s32[1,72]{1,0:T(1,128)} %chosen_ref.1) | copy-start | bytes 868
  96.3 35.7 %copy-start.6 = (f32[96]{0:T(128)S(1)}, f32[96]{0:T(128)}, u32[]{:S(2)}) copy-start(f32[96]{0:T(128)} %param.11) | copy-start | bytes 1156
  96.3 10.0 %collective-permute-start.28 = (bf16[72,2048]{1,0:T(8,128)(2,1)S(1)}, bf16[72,2048]{1,0:T(8,128)(2,1)S(1)}, u32[]{:S(2)}, u32[]{:S(2)}) collective-permute-start(bf16[72,2048]{1,0:T(8,128)(2,1)S(1)} %get-tuple-element.94), channel_id=1, source_target_pairs={{0,4},{4,0},{8,12},{12,8},{16,20},{20,16},{24,28},{28,24},{1,5},{5... | collective-permute-start | bytes 884744 | tf_op jit(solution)/shard_map/ppermute | solution.py:29
  96.9 10.9 %collective-permute-start.29 = (bf16[72,2048]{1,0:T(8,128)(2,1)S(1)}, bf16[72,2048]{1,0:T(8,128)(2,1)S(1)}, u32[]{:S(2)}, u32[]{:S(2)}) collective-permute-start(bf16[72,2048]{1,0:T(8,128)(2,1)S(1)} %get-tuple-element.95), channel_id=1, source_target_pairs={{0,8},{4,12},{8,0},{12,4},{16,24},{20,28},{24,16},{28,20},{1,9},{5... | collective-permute-start | bytes 884744 | tf_op jit(solution)/shard_map/ppermute | solution.py:29
  98.4 15.7 %collective-permute-start.30 = (bf16[72,2048]{1,0:T(8,128)(2,1)S(1)}, bf16[72,2048]{1,0:T(8,128)(2,1)S(1)}, u32[]{:S(2)}, u32[]{:S(2)}) collective-permute-start(bf16[72,2048]{1,0:T(8,128)(2,1)S(1)} %get-tuple-element.96), channel_id=1, source_target_pairs={{0,12},{4,8},{8,4},{12,0},{16,28},{20,24},{24,20},{28,16},{1,13},{... | collective-permute-start | bytes 884744 | tf_op jit(solution)/shard_map/ppermute | solution.py:29
  99.9 1.8 %collective-permute-start.32 = (bf16[208,512]{1,0:T(8,128)(2,1)S(1)}, bf16[208,512]{1,0:T(8,128)(2,1)S(1)}, u32[]{:S(2)}, u32[]{:S(2)}) collective-permute-start(bf16[208,512]{1,0:T(8,128)(2,1)S(1)} %get-tuple-element.99), channel_id=1, source_target_pairs={{0,1},{1,0},{2,3},{3,2},{4,5},{5,4},{6,7},{7,6},{8,9},{9,8},{10,11... | collective-permute-start | bytes 638984 | tf_op jit(solution)/shard_map/ppermute | solution.py:29
  100.0 1.7 %collective-permute-start.33 = (bf16[208,384]{1,0:T(8,128)(2,1)S(1)}, bf16[208,384]{1,0:T(8,128)(2,1)S(1)}, u32[]{:S(2)}, u32[]{:S(2)}) collective-permute-start(bf16[208,384]{1,0:T(8,128)(2,1)S(1)} %get-tuple-element.100), channel_id=1, source_target_pairs={{0,1},{1,0},{2,3},{3,2},{4,5},{5,4},{6,7},{7,6},{8,9},{9,8},{10,11... | collective-permute-start | bytes 479240 | tf_op jit(solution)/shard_map/ppermute | solution.py:29
  104.3 14.8 %collective-permute-start.35 = (bf16[72,2048]{1,0:T(8,128)(2,1)S(1)}, bf16[72,2048]{1,0:T(8,128)(2,1)S(1)}, u32[]{:S(2)}, u32[]{:S(2)}) collective-permute-start(bf16[72,2048]{1,0:T(8,128)(2,1)S(1)} %get-tuple-element.102), channel_id=1, source_target_pairs={{0,4},{4,0},{8,12},{12,8},{16,20},{20,16},{24,28},{28,24},{1,5},{5... | collective-permute-start | bytes 884744 | tf_op jit(solution)/shard_map/ppermute | solution.py:29
  104.9 21.0 %collective-permute-start.36 = (bf16[72,2048]{1,0:T(8,128)(2,1)S(1)}, bf16[72,2048]{1,0:T(8,128)(2,1)S(1)}, u32[]{:S(2)}, u32[]{:S(2)}) collective-permute-start(bf16[72,2048]{1,0:T(8,128)(2,1)S(1)} %get-tuple-element.103), channel_id=1, source_target_pairs={{0,8},{4,12},{8,0},{12,4},{16,24},{20,28},{24,16},{28,20},{1,9},{5... | collective-permute-start | bytes 884744 | tf_op jit(solution)/shard_map/ppermute | solution.py:29
  106.3 25.7 %collective-permute-start.37 = (bf16[72,2048]{1,0:T(8,128)(2,1)S(1)}, bf16[72,2048]{1,0:T(8,128)(2,1)S(1)}, u32[]{:S(2)}, u32[]{:S(2)}) collective-permute-start(bf16[72,2048]{1,0:T(8,128)(2,1)S(1)} %get-tuple-element.104), channel_id=1, source_target_pairs={{0,12},{4,8},{8,4},{12,0},{16,28},{20,24},{24,20},{28,16},{1,13},{... | collective-permute-start | bytes 884744 | tf_op jit(solution)/shard_map/ppermute | solution.py:29
  114.3 17.8 %collective-permute-start.34 = (bf16[72,2048]{1,0:T(8,128)(2,1)S(1)}, bf16[72,2048]{1,0:T(8,128)(2,1)S(1)}, u32[]{:S(2)}, u32[]{:S(2)}) collective-permute-start(bf16[72,2048]{1,0:T(8,128)(2,1)S(1)} %sum.1), channel_id=1, source_target_pairs={{0,16},{4,20},{8,24},{12,28},{16,0},{20,4},{24,8},{28,12},{1,17},{... | collective-permute-start | bytes 884744 | tf_op jit(solution)/shard_map/ppermute | solution.py:29

commit v4 on v3

--- a/solution.py
+++ b/solution.py
@@ -128,7 +128,9 @@
     return total[:, :LANES]
 
 
-def gate_up_kernel(me_ref, x_ref, s_ref, g_ref, u_ref, *refs, share_width, cuts, shares, count):
+def gate_up_kernel(
+    me_ref, x_ref, s_ref, g_ref, u_ref, *refs, share_width, cuts, shares, count, code
+):
     outs, (buffer, sems) = refs[-2 - count : -2], refs[-2:]
     me = me_ref[0]
     rows = x_ref.shape[0]
@@ -154,16 +156,16 @@
         if step == 1:
             place = pl.ds(array * share_width + offset, width)
             outs[-1][:, place] = term.astype(BF16)
-        elif count == 3:
+        elif count == 3 and len(cuts) > 1:
             outs[array][:, pl.ds(offset, width)] = term.astype(BF16)
-        elif tile == 0:
+        elif tile == 0 and code:
             outs[0][: rows - 16, :] = term[: rows - 16].astype(BF16)
             outs[0][rows - 16 :, :] = coded(s_ref[0:1, :], term[rows - 16 :])
         else:
             outs[tile][...] = term.astype(BF16)
 
 
-def gate_up(me, x, squares, w_gate, w_up, tp, cuts, mine, after):
+def gate_up(me, x, squares, w_gate, w_up, tp, cuts, mine, after, split=True):
     rows, feats = x.shape
     width = w_gate.shape[1] // tp
     shares = (1, 0) if mine else (3, 2)
@@ -181,11 +183,16 @@
         return [coded(squares[0:1], out[0][0]), out[0][1], joined[1]]
     whole = ((rows, 2 * width), BF16)
     pieces = [((rows, w), BF16) for _ in range(2) for _, w in cuts]
-    outs = [((rows, width), BF16)] * 2 if mine else pieces
+    outs = pieces if split else [((rows, width), BF16)] * 2
     outs = outs + [whole]
     return call(
         functools.partial(
-            gate_up_kernel, share_width=width, cuts=cuts, shares=shares, count=len(outs)
+            gate_up_kernel,
+            share_width=width,
+            cuts=cuts,
+            shares=shares,
+            count=len(outs),
+            code=not mine,
         ),
         outs,
         (me, x, squares, w_gate, w_up),
@@ -226,8 +233,8 @@
     )
 
 
-def silu_kernel(a_ref, g_ref, u_ref, c_ref, s_ref, *refs, cuts):
-    out_ref, pieces = refs[-1 - len(cuts)], refs[-len(cuts) :]
+def silu_kernel(a_ref, c_ref, s_ref, *refs, cuts, count):
+    gots, out_ref, pieces = refs[:count], refs[-1 - len(cuts)], refs[-len(cuts) :]
     rows, width = out_ref.shape
     squares = s_ref[0:1, :] + decoded(c_ref[rows - 16 :, :])
     row = lax.broadcasted_iota(jnp.int32, (rows, LANES), 0)
@@ -235,23 +242,30 @@
     column = jnp.sum(jnp.where(row == lane, squares, 0.0), axis=1, keepdims=True)
     scale = jnp.where(row[:, :1] < rows - SPARE, lax.rsqrt(column / D + EPS), 0.0)
 
-    def total(got, part):
-        return (a_ref[:, part].astype(F32) + got[...].astype(F32) + c_ref[:, part].astype(F32)) * scale
-
-    gate, up = total(g_ref, slice(0, width)), total(u_ref, slice(width, 2 * width))
-    hidden = (gate / (1.0 + jnp.exp(-gate)) * up).astype(BF16)
-    out_ref[...] = hidden
-    for piece, (offset, part) in zip(pieces, cuts):
-        piece[...] = hidden[:, offset : offset + part]
-
-
-def silu(a, gate, up, c, squares, cuts, after):
+    def total(array, cut):
+        offset, part = cuts[cut]
+        begin = array * width + offset
+        if count == 2:
+            got = gots[array][:, offset : offset + part]
+        else:
+            got = gots[array * len(cuts) + cut][...]
+        a, c = a_ref[:, begin : begin + part], c_ref[:, begin : begin + part]
+        return (a.astype(F32) + got.astype(F32) + c.astype(F32)) * scale
+
+    for cut, (offset, part) in enumerate(cuts):
+        gate, up = total(0, cut), total(1, cut)
+        hidden = (gate / (1.0 + jnp.exp(-gate)) * up).astype(BF16)
+        out_ref[:, offset : offset + part] = hidden
+        pieces[cut][...] = hidden
+
+
+def silu(a, gots, c, squares, cuts, after):
     rows, width = a.shape
     return call(
-        functools.partial(silu_kernel, cuts=cuts),
+        functools.partial(silu_kernel, cuts=cuts, count=len(gots)),
         [((rows, width // 2), BF16)] + [((rows, part), BF16) for _, part in cuts],
-        (a, gate, up, c, squares),
-        [VMEM] * 5,
+        (a, c, squares, *gots),
+        [VMEM] * (3 + len(gots)),
         "silu",
         16,
         after=after,
@@ -259,7 +273,7 @@
 
 
 def relay_kernel(in_ref, *refs, cuts):
-    whole, pieces = refs[-1 - len(cuts)], refs[-len(cuts) :]
+    whole, *pieces = refs[-1 - len(cuts) :]
     whole[...] = in_ref[...]
     for piece, (offset, width) in zip(pieces, cuts):
         piece[...] = in_ref[:, offset : offset + width]
@@ -408,23 +422,27 @@
         after = [outgoing]
     owns, cores, parts = [], [], []
     for (x, squares, extras), (across, two) in zip(chunks, begun):
-        *sends, keep = gate_up(me, x, squares, *weights, True, after)
+        *sends, keep = gate_up(me, x, squares, *weights, True, after, not owns)
         gots = [swap(piece, "tp", tp, 1) for piece in sends]
-        own, *pieces = silu(keep, *gots, across, two, cuts, parts[0][:1] if parts else [])
+        own, *pieces = silu(keep, gots, across, two, cuts, [])
         after = [own]
         owns.append(own)
         cores.append([swap(piece, "tp", tp, 1) for piece in pieces])
-        if not parts:
-            parts.append(down(me, extras, w_down, (own, *cores[0]), cuts, None, window, []))
+        if len(owns) == 2:
+            extras = chunks[0][2]
+            parts.append(down(me, extras, w_down, (owns[0], *cores[0]), cuts, None, window, [own]))
 
     blocks, behind = [], []
     for number in [*range(1, len(chunks)), 0]:
         extras = chunks[number][2]
-        other_y = swap(owns[number], "tp", tp, 2)
+        own = owns[number]
         if number:
-            hidden = (owns[number], *cores[number])
+            other_y = swap(own, "tp", tp, 2)
+            hidden = (own, *cores[number])
             part = down(me, extras, w_down, hidden, cuts, None, window, behind)
+            first = part[:1]
         else:
+            other_y = swap(relay(own, [], first)[0], "tp", tp, 2)
             part = parts[0]
         other_y, *pieces = relay(other_y, cuts, part[:1] + behind)
         both = [swap(piece, "tp", tp, 1) for piece in pieces]

time: 133 us -> 128 us (0.962)
  waiting for transfers between devices: 51.9 us -> 46.2 us
    ppermute x38 -> x40, waiting for transfers between devices: 51.9 us -> 46.2 us  [swap(): return lax.ppermute(value, axis, [(i, i ^ bit) for i in range(size)])]
    pallas_call x18 -> x19, Pallas kernels: 47.9 us -> 47.4 us  [call(): pl.pallas_call(kernel, out_shape=[jax.ShapeDtypeStruct(*out) if isinstanc...]
    ppermute x38 -> x40, starting transfers between devices: 29 us -> 29.4 us  [swap(): return lax.ppermute(value, axis, [(i, i ^ bit) for i in range(size)])]
  transfers between devices with their start and end apart: 38 -> 40, of which waited for: 17 -> 14; matrix products, arithmetic and copies ran while one was open for 0% -> 0% of each run, Pallas kernels for 35% -> 36%
where the time goes in v4:
time: 128 us; the launch traced here: 127 us
  Pallas kernels  47.4 us (37%)
  waiting for transfers between devices  46.2 us (36%)
  starting transfers between devices  29.4 us (23%)
  local copies, waits for them, and re-layouts  2.37 us (2%)
    pallas_call x19, Pallas kernels, call(): pl.pallas_call(kernel, out_shape=[jax.ShapeDtypeStruct(*out) if isinstanc...  47.4 us
    ppermute x40, waiting for transfers between devices, swap(): return lax.ppermute(value, axis, [(i, i ^ bit) for i in range(size)])  46.2 us
    ppermute x40, starting transfers between devices, swap(): return lax.ppermute(value, axis, [(i, i ^ bit) for i in range(size)])  29.4 us
  transfers between devices with their start and end apart: 40, of which 14 were waited for; matrix products, arithmetic and copies ran while one was open for 0% of the time, Pallas kernels for 36%

profile of v4, /device:TPU:0, one launch (start us, length us, event | category | flops | bytes accessed | tf_op | source)
XLA Modules:
  0.0 127.4 jit_solution(8838462942554536626)
XLA Ops:
  0.7 1.0 copy-done
  1.7 0.7 copy-done.4
  2.6 4.1 %collective-permute-start = (bf16[72,2048]{1,0:T(8,128)(2,1)S(1)}, bf16[72,2048]{1,0:T(8,128)(2,1)S(1)}, u32[]{:S(2)}, u32[]{:S(2)}) collective-permute-start(bf16[72,2048]{1,0:T(8,128)(2,1)S(1)} %pick.1.refs_0_), channel_id=1, source_target_pairs={{0,16},{4,20},{8,24},{12,28},{16,0},{20,4},{24,8},{28,12},{1,17},{... | collective-permute-start | bytes 884744 | tf_op jit(solution)/shard_map/ppermute | solution.py:29
  6.7 1.5 %collective-permute-start.4 = (bf16[72,2048]{1,0:T(8,128)(2,1)S(1)}, bf16[72,2048]{1,0:T(8,128)(2,1)S(1)}, u32[]{:S(2)}, u32[]{:S(2)}) collective-permute-start(bf16[72,2048]{1,0:T(8,128)(2,1)S(1)} %pick.1.refs_0_), channel_id=1, source_target_pairs={{0,4},{4,0},{8,12},{12,8},{16,20},{20,16},{24,28},{28,24},{1,5},{5... | collective-permute-start | bytes 884744 | tf_op jit(solution)/shard_map/ppermute | solution.py:29
  8.2 1.6 %collective-permute-start.5 = (bf16[72,2048]{1,0:T(8,128)(2,1)S(1)}, bf16[72,2048]{1,0:T(8,128)(2,1)S(1)}, u32[]{:S(2)}, u32[]{:S(2)}) collective-permute-start(bf16[72,2048]{1,0:T(8,128)(2,1)S(1)} %pick.1.refs_0_), channel_id=1, source_target_pairs={{0,8},{4,12},{8,0},{12,4},{16,24},{20,28},{24,16},{28,20},{1,9},{5... | collective-permute-start | bytes 884744 | tf_op jit(solution)/shard_map/ppermute | solution.py:29
  10.2 9.9 %collective-permute-done.refs_0_ = bf16[72,2048]{1,0:T(8,128)(2,1)S(1)} collective-permute-done((bf16[72,2048]{1,0:T(8,128)(2,1)S(1)}, bf16[72,2048]{1,0:T(8,128)(2,1)S(1)}, u32[]{:S(2)}, u32[]{:S(2)}) %collective-permute-start) | collective-permute-done | bytes 294944 | tf_op jit(solution)/shard_map/ppermute | solution.py:29
  20.1 1.5 %collective-permute-start.1 = (bf16[72,2048]{1,0:T(8,128)(2,1)S(1)}, bf16[72,2048]{1,0:T(8,128)(2,1)S(1)}, u32[]{:S(2)}, u32[]{:S(2)}) collective-permute-start(bf16[72,2048]{1,0:T(8,128)(2,1)S(1)} %collective-permute-done.refs_0_), channel_id=1, source_target_pairs={{0,4},{4,0},{8,12},{12,8},{16,20},{20,16},{24,28},{28,24},{1,5},{5... | collective-permute-start | bytes 884744 | tf_op jit(solution)/shard_map/ppermute | solution.py:29
  21.7 0.6 collective-permute-start.2
  22.3 1.3 %collective-permute-start.3 = (bf16[72,2048]{1,0:T(8,128)(2,1)S(1)}, bf16[72,2048]{1,0:T(8,128)(2,1)S(1)}, u32[]{:S(2)}, u32[]{:S(2)}) collective-permute-start(bf16[72,2048]{1,0:T(8,128)(2,1)S(1)} %collective-permute-done.refs_0_), channel_id=1, source_target_pairs={{0,12},{4,8},{8,4},{12,0},{16,28},{20,24},{24,20},{28,16},{1,13},{... | collective-permute-start | bytes 884744 | tf_op jit(solution)/shard_map/ppermute | solution.py:29
  23.6 6.1 %collective-permute-done.6.refs_3_ = bf16[72,2048]{1,0:T(8,128)(2,1)S(1)} collective-permute-done((bf16[72,2048]{1,0:T(8,128)(2,1)S(1)}, bf16[72,2048]{1,0:T(8,128)(2,1)S(1)}, u32[]{:S(2)}, u32[]{:S(2)}) %collective-permute-start.6) | collective-permute-done | bytes 294944 | tf_op jit(solution)/shard_map/ppermute | solution.py:29
  29.7 0.7 copy-done.2
  30.4 1.1 assemble_208.3
  31.5 6.7 %gate_up_208_0.2 = (bf16[208,512]{1,0:T(8,128)(2,1)S(1)}, bf16[208,384]{1,0:T(8,128)(2,1)S(1)}, bf16[208,512]{1,0:T(8,128)(2,1)S(1)}, bf16[208,384]{1,0:T(8,128)(2,1)S(1)}, bf16[208,1792]{1,0:T(8,128)(2,1)S(1)}) custom-call(s32[1]{0:T(128)} %bitcast.2.me_ref, bf16[208,2048]{1,0:T(8,128)(2,1)S(1)} %get-tuple-element.60.x_ref, ...), custom_call_target="tpu_custom_call" | custom-call | tf_op jit(solution)/shard_map/gate_up_208_0/pallas_call | solution.py:33
  38.3 0.5 collective-permute-start.9
  39.3 1.3 collective-permute-done.3.refs_3_
  40.6 1.1 assemble_208.2
  42.0 1.6 %collective-permute-start.15 = (bf16[208,1792]{1,0:T(8,128)(2,1)S(1)}, bf16[208,1792]{1,0:T(8,128)(2,1)S(1)}, u32[]{:S(2)}, u32[]{:S(2)}) collective-permute-start(bf16[208,1792]{1,0:T(8,128)(2,1)S(1)} %get-tuple-element.67.refs_0_), channel_id=1, source_target_pairs={{0,2},{1,3},{2,0},{3,1},{4,6},{5,7},{6,4},{7,5},{8,10},{9,11},{10,... | collective-permute-start | bytes 2236424 | tf_op jit(solution)/shard_map/ppermute | solution.py:29
  43.6 6.7 %gate_up_208_0.3 = (bf16[208,512]{1,0:T(8,128)(2,1)S(1)}, bf16[208,384]{1,0:T(8,128)(2,1)S(1)}, bf16[208,512]{1,0:T(8,128)(2,1)S(1)}, bf16[208,384]{1,0:T(8,128)(2,1)S(1)}, bf16[208,1792]{1,0:T(8,128)(2,1)S(1)}) custom-call(s32[1]{0:T(128)} %bitcast.2.me_ref, bf16[208,2048]{1,0:T(8,128)(2,1)S(1)} %get-tuple-element.58.refs_4_.x_ref, ...), custom_call_target="tpu_custom_call" | custom-call | tf_op jit(solution)/shard_map/gate_up_208_0/pallas_call | solution.py:33
  50.4 0.5 collective-permute-start.13
  51.4 1.0 collective-permute-done.12.refs_1_
  52.9 0.6 collective-permute-start.20
  53.5 6.8 %gate_up_208_1.2 = (bf16[208,512]{1,0:T(8,128)(2,1)S(1)}, bf16[208,384]{1,0:T(8,128)(2,1)S(1)}, bf16[208,512]{1,0:T(8,128)(2,1)S(1)}, bf16[208,384]{1,0:T(8,128)(2,1)S(1)}, bf16[208,1792]{1,0:T(8,128)(2,1)S(1)}) custom-call(s32[1]{0:T(128)} %bitcast.2.me_ref, bf16[208,2048]{1,0:T(8,128)(2,1)S(1)} %get-tuple-element.60.x_ref, ...), custom_call_target="tpu_custom_call" | custom-call | tf_op jit(solution)/shard_map/gate_up_208_1/pallas_call | solution.py:33
  60.4 0.5 collective-permute-start.16
  61.0 0.8 collective-permute-done.17.refs_1_
  61.9 1.2 collective-permute-done.19.refs_3_
  63.2 0.7 silu.2
  63.9 6.7 %gate_up_208_1.3 = (bf16[208,896]{1,0:T(8,128)(2,1)S(1)}, bf16[208,896]{1,0:T(8,128)(2,1)S(1)}, bf16[208,1792]{1,0:T(8,128)(2,1)S(1)}) custom-call(s32[1]{0:T(128)} %bitcast.2.me_ref, bf16[208,2048]{1,0:T(8,128)(2,1)S(1)} %get-tuple-element.58.refs_4_.x_ref, f32[8,256]{1,0:T(8,128)S(1)} %get-tuple-element.59.s_ref, bf16[2048,3584]{1,0:T(8,128)(2,1)} %g_ref.7, ...), custom_call_target="tpu_custom_call" | custom-call | tf_op jit(solution)/shard_map/gate_up_208_1/pallas_call | solution.py:33
  71.1 4.5 %collective-permute-done.20.c_ref = bf16[208,1792]{1,0:T(8,128)(2,1)S(1)} collective-permute-done((bf16[208,1792]{1,0:T(8,128)(2,1)S(1)}, bf16[208,1792]{1,0:T(8,128)(2,1)S(1)}, u32[]{:S(2)}, u32[]{:S(2)}) %collective-permute-start.20) | collective-permute-done | bytes 745504 | tf_op jit(solution)/shard_map/ppermute | solution.py:29
  75.6 0.7 silu.3
  76.3 1.6 %collective-permute-start.25 = (bf16[208,896]{1,0:T(8,128)(2,1)S(1)}, bf16[208,896]{1,0:T(8,128)(2,1)S(1)}, u32[]{:S(2)}, u32[]{:S(2)}) collective-permute-start(bf16[208,896]{1,0:T(8,128)(2,1)S(1)} %get-tuple-element.85.refs_0_.refs_3_), channel_id=1, source_target_pairs={{0,2},{1,3},{2,0},{3,1},{4,6},{5,7},{6,4},{7,5},{8,10},{9,11},{10,... | collective-permute-start | bytes 1118216 | tf_op jit(solution)/shard_map/ppermute | solution.py:29
  77.9 0.5 collective-permute-start.24
  78.4 1.2 collective-permute-done.24.refs_2_
  79.6 5.3 %down_208_0.2 = (f32[208,2048]{1,0:T(8,128)S(1)}, bf16[4,512,2048]{2,1,0:T(8,128)(2,1)S(1)}) custom-call(s32[1]{0:T(128)} %bitcast.2.me_ref, f32[8,256]{1,0:T(8,128)S(1)} %get-tuple-element.57.extras_ref, bf16[3584,2048]{1,0:T(8,128)(2,1)} %w_ref.3, bf16[208,896]{1,0:T(8,128)(2,1)S(1)} %get-tuple-element.85.refs_0_.refs_3_, ...), custom_call_target="tpu_custom_call" | custom-call | tf_op jit(solution)/shard_map/down_208_0/pallas_call | solution.py:33
  84.9 0.6 collective-permute-start.33
  86.6 0.7 collective-permute-done.27.refs_2_
  87.3 2.5 %down_208_1.2 = (bf16[72,2048]{1,0:T(8,128)(2,1)S(1)}, bf16[72,2048]{1,0:T(8,128)(2,1)S(1)}, bf16[72,2048]{1,0:T(8,128)(2,1)S(1)}, bf16[72,2048]{1,0:T(8,128)(2,1)S(1)}) custom-call(s32[1]{0:T(128)} %bitcast.2.me_ref, f32[8,256]{1,0:T(8,128)S(1)} %get-tuple-element.57.extras_ref, bf16[4,512,2048]{2,1,0:T(8,128)(2,1)S(1)} %get-tuple-element.88.w_ref, ...), custom_call_target="tpu_custom_call" | custom-call | tf_op jit(solution)/shard_map/down_208_1/pallas_call | solution.py:33
  89.9 1.5 %collective-permute-start.28 = (bf16[72,2048]{1,0:T(8,128)(2,1)S(1)}, bf16[72,2048]{1,0:T(8,128)(2,1)S(1)}, u32[]{:S(2)}, u32[]{:S(2)}) collective-permute-start(bf16[72,2048]{1,0:T(8,128)(2,1)S(1)} %get-tuple-element.94), channel_id=1, source_target_pairs={{0,4},{4,0},{8,12},{12,8},{16,20},{20,16},{24,28},{28,24},{1,5},{5... | collective-permute-start | bytes 884744 | tf_op jit(solution)/shard_map/ppermute | solution.py:29
  91.7 1.8 %collective-permute-start.30 = (bf16[72,2048]{1,0:T(8,128)(2,1)S(1)}, bf16[72,2048]{1,0:T(8,128)(2,1)S(1)}, u32[]{:S(2)}, u32[]{:S(2)}) collective-permute-start(bf16[72,2048]{1,0:T(8,128)(2,1)S(1)} %get-tuple-element.96), channel_id=1, source_target_pairs={{0,12},{4,8},{8,4},{12,0},{16,28},{20,24},{24,20},{28,16},{1,13},{... | collective-permute-start | bytes 884744 | tf_op jit(solution)/shard_map/ppermute | solution.py:29
  93.4 5.3 %down_208_0.3 = (f32[208,2048]{1,0:T(8,128)S(1)}, bf16[4,512,2048]{2,1,0:T(8,128)(2,1)S(1)}) custom-call(s32[1]{0:T(128)} %bitcast.2.me_ref, f32[8,256]{1,0:T(8,128)S(1)} %get-tuple-element.97.extras_ref, bf16[3584,2048]{1,0:T(8,128)(2,1)} %w_ref.3, bf16[208,896]{1,0:T(8,128)(2,1)S(1)} %get-tuple-element.80.refs_0_.in_ref, ...), custom_call_target="tpu_custom_call" | custom-call | tf_op jit(solution)/shard_map/down_208_0/pallas_call | solution.py:33
  99.4 1.2 collective-permute-done.35.refs_2_
  100.6 2.6 %down_208_1.3 = (bf16[72,2048]{1,0:T(8,128)(2,1)S(1)}, bf16[72,2048]{1,0:T(8,128)(2,1)S(1)}, bf16[72,2048]{1,0:T(8,128)(2,1)S(1)}, bf16[72,2048]{1,0:T(8,128)(2,1)S(1)}) custom-call(s32[1]{0:T(128)} %bitcast.2.me_ref, f32[8,256]{1,0:T(8,128)S(1)} %get-tuple-element.97.extras_ref, bf16[4,512,2048]{2,1,0:T(8,128)(2,1)S(1)} %get-tuple-element.100.w_ref, ...), custom_call_target="tpu_custom_call" | custom-call | tf_op jit(solution)/shard_map/down_208_1/pallas_call | solution.py:33
  103.2 1.5 %collective-permute-start.37 = (bf16[72,2048]{1,0:T(8,128)(2,1)S(1)}, bf16[72,2048]{1,0:T(8,128)(2,1)S(1)}, u32[]{:S(2)}, u32[]{:S(2)}) collective-permute-start(bf16[72,2048]{1,0:T(8,128)(2,1)S(1)} %get-tuple-element.106), channel_id=1, source_target_pairs={{0,4},{4,0},{8,12},{12,8},{16,20},{20,16},{24,28},{28,24},{1,5},{5... | collective-permute-start | bytes 884744 | tf_op jit(solution)/shard_map/ppermute | solution.py:29
  105.0 1.8 %collective-permute-start.39 = (bf16[72,2048]{1,0:T(8,128)(2,1)S(1)}, bf16[72,2048]{1,0:T(8,128)(2,1)S(1)}, u32[]{:S(2)}, u32[]{:S(2)}) collective-permute-start(bf16[72,2048]{1,0:T(8,128)(2,1)S(1)} %get-tuple-element.108), channel_id=1, source_target_pairs={{0,12},{4,8},{8,4},{12,0},{16,28},{20,24},{24,20},{28,16},{1,13},{... | collective-permute-start | bytes 884744 | tf_op jit(solution)/shard_map/ppermute | solution.py:29
  106.9 1.2 collective-permute-start.36
  108.1 4.8 %collective-permute-done.37 = bf16[72,2048]{1,0:T(8,128)(2,1)S(1)} collective-permute-done((bf16[72,2048]{1,0:T(8,128)(2,1)S(1)}, bf16[72,2048]{1,0:T(8,128)(2,1)S(1)}, u32[]{:S(2)}, u32[]{:S(2)}) %collective-permute-start.37) | collective-permute-done | bytes 294944 | tf_op jit(solution)/shard_map/ppermute | solution.py:29
  112.9 8.0 %collective-permute-done.38 = bf16[72,2048]{1,0:T(8,128)(2,1)S(1)} collective-permute-done((bf16[72,2048]{1,0:T(8,128)(2,1)S(1)}, bf16[72,2048]{1,0:T(8,128)(2,1)S(1)}, u32[]{:S(2)}, u32[]{:S(2)}) %collective-permute-start.38) | collective-permute-done | bytes 294944 | tf_op jit(solution)/shard_map/ppermute | solution.py:29
  120.9 5.3 %collective-permute-done.39 = bf16[72,2048]{1,0:T(8,128)(2,1)S(1)} collective-permute-done((bf16[72,2048]{1,0:T(8,128)(2,1)S(1)}, bf16[72,2048]{1,0:T(8,128)(2,1)S(1)}, u32[]{:S(2)}, u32[]{:S(2)}) %collective-permute-start.39) | collective-permute-done | bytes 294944 | tf_op jit(solution)/shard_map/ppermute | solution.py:29
  126.2 1.1 fusion.1
  (67 shorter events, 6.2 us)
Async XLA Ops:
  0.7 1.0 copy-start
  1.7 0.7 copy-start.4
  2.6 17.5 %collective-permute-start = (bf16[72,2048]{1,0:T(8,128)(2,1)S(1)}, bf16[72,2048]{1,0:T(8,128)(2,1)S(1)}, u32[]{:S(2)}, u32[]{:S(2)}) collective-permute-start(bf16[72,2048]{1,0:T(8,128)(2,1)S(1)} %pick.1.refs_0_), channel_id=1, source_target_pairs={{0,16},{4,20},{8,24},{12,28},{16,0},{20,4},{24,8},{28,12},{1,17},{... | collective-permute-start | bytes 884744 | tf_op jit(solution)/shard_map/ppermute | solution.py:29
  6.7 15.6 %collective-permute-start.4 = (bf16[72,2048]{1,0:T(8,128)(2,1)S(1)}, bf16[72,2048]{1,0:T(8,128)(2,1)S(1)}, u32[]{:S(2)}, u32[]{:S(2)}) collective-permute-start(bf16[72,2048]{1,0:T(8,128)(2,1)S(1)} %pick.1.refs_0_), channel_id=1, source_target_pairs={{0,4},{4,0},{8,12},{12,8},{16,20},{20,16},{24,28},{28,24},{1,5},{5... | collective-permute-start | bytes 884744 | tf_op jit(solution)/shard_map/ppermute | solution.py:29
  8.2 15.4 %collective-permute-start.5 = (bf16[72,2048]{1,0:T(8,128)(2,1)S(1)}, bf16[72,2048]{1,0:T(8,128)(2,1)S(1)}, u32[]{:S(2)}, u32[]{:S(2)}) collective-permute-start(bf16[72,2048]{1,0:T(8,128)(2,1)S(1)} %pick.1.refs_0_), channel_id=1, source_target_pairs={{0,8},{4,12},{8,0},{12,4},{16,24},{20,28},{24,16},{28,20},{1,9},{5... | collective-permute-start | bytes 884744 | tf_op jit(solution)/shard_map/ppermute | solution.py:29
  9.8 19.9 %collective-permute-start.6 = (bf16[72,2048]{1,0:T(8,128)(2,1)S(1)}, bf16[72,2048]{1,0:T(8,128)(2,1)S(1)}, u32[]{:S(2)}, u32[]{:S(2)}) collective-permute-start(bf16[72,2048]{1,0:T(8,128)(2,1)S(1)} %pick.1.refs_0_), channel_id=1, source_target_pairs={{0,12},{4,8},{8,4},{12,0},{16,28},{20,24},{24,20},{28,16},{1,13},{... | collective-permute-start | bytes 884744 | tf_op jit(solution)/shard_map/ppermute | solution.py:29
  20.1 18.7 %collective-permute-start.1 = (bf16[72,2048]{1,0:T(8,128)(2,1)S(1)}, bf16[72,2048]{1,0:T(8,128)(2,1)S(1)}, u32[]{:S(2)}, u32[]{:S(2)}) collective-permute-start(bf16[72,2048]{1,0:T(8,128)(2,1)S(1)} %collective-permute-done.refs_0_), channel_id=1, source_target_pairs={{0,4},{4,0},{8,12},{12,8},{16,20},{20,16},{24,28},{28,24},{1,5},{5... | collective-permute-start | bytes 884744 | tf_op jit(solution)/shard_map/ppermute | solution.py:29
  21.7 17.2 %collective-permute-start.2 = (bf16[72,2048]{1,0:T(8,128)(2,1)S(1)}, bf16[72,2048]{1,0:T(8,128)(2,1)S(1)}, u32[]{:S(2)}, u32[]{:S(2)}) collective-permute-start(bf16[72,2048]{1,0:T(8,128)(2,1)S(1)} %collective-permute-done.refs_0_), channel_id=1, source_target_pairs={{0,8},{4,12},{8,0},{12,4},{16,24},{20,28},{24,16},{28,20},{1,9},{5... | collective-permute-start | bytes 884744 | tf_op jit(solution)/shard_map/ppermute | solution.py:29
  22.3 18.3 %collective-permute-start.3 = (bf16[72,2048]{1,0:T(8,128)(2,1)S(1)}, bf16[72,2048]{1,0:T(8,128)(2,1)S(1)}, u32[]{:S(2)}, u32[]{:S(2)}) collective-permute-start(bf16[72,2048]{1,0:T(8,128)(2,1)S(1)} %collective-permute-done.refs_0_), channel_id=1, source_target_pairs={{0,12},{4,8},{8,4},{12,0},{16,28},{20,24},{24,20},{28,16},{1,13},{... | collective-permute-start | bytes 884744 | tf_op jit(solution)/shard_map/ppermute | solution.py:29
  29.7 0.7 copy-start.2
  31.5 9.0 %copy-start.3 = (f32[2048]{0:T(1024)S(1)}, f32[2048]{0:T(1024)}, u32[]{:S(2)}) copy-start(f32[2048]{0:T(1024)} %param.12) | copy-start | bytes 24580
  38.2 3.5 %collective-permute-start.7 = (bf16[208,512]{1,0:T(8,128)(2,1)S(1)}, bf16[208,512]{1,0:T(8,128)(2,1)S(1)}, u32[]{:S(2)}, u32[]{:S(2)}) collective-permute-start(bf16[208,512]{1,0:T(8,128)(2,1)S(1)} %get-tuple-element.63), channel_id=1, source_target_pairs={{0,1},{1,0},{2,3},{3,2},{4,5},{5,4},{6,7},{7,6},{8,9},{9,8},{10,11... | collective-permute-start | bytes 638984 | tf_op jit(solution)/shard_map/ppermute | solution.py:29
  38.3 3.4 %collective-permute-start.9 = (bf16[208,512]{1,0:T(8,128)(2,1)S(1)}, bf16[208,512]{1,0:T(8,128)(2,1)S(1)}, u32[]{:S(2)}, u32[]{:S(2)}) collective-permute-start(bf16[208,512]{1,0:T(8,128)(2,1)S(1)} %get-tuple-element.65), channel_id=1, source_target_pairs={{0,1},{1,0},{2,3},{3,2},{4,5},{5,4},{6,7},{7,6},{8,9},{9,8},{10,11... | collective-permute-start | bytes 638984 | tf_op jit(solution)/shard_map/ppermute | solution.py:29
  38.8 2.9 %collective-permute-start.10 = (bf16[208,384]{1,0:T(8,128)(2,1)S(1)}, bf16[208,384]{1,0:T(8,128)(2,1)S(1)}, u32[]{:S(2)}, u32[]{:S(2)}) collective-permute-start(bf16[208,384]{1,0:T(8,128)(2,1)S(1)} %get-tuple-element.66), channel_id=1, source_target_pairs={{0,1},{1,0},{2,3},{3,2},{4,5},{5,4},{6,7},{7,6},{8,9},{9,8},{10,11... | collective-permute-start | bytes 479240 | tf_op jit(solution)/shard_map/ppermute | solution.py:29
  38.9 2.8 %collective-permute-start.8 = (bf16[208,384]{1,0:T(8,128)(2,1)S(1)}, bf16[208,384]{1,0:T(8,128)(2,1)S(1)}, u32[]{:S(2)}, u32[]{:S(2)}) collective-permute-start(bf16[208,384]{1,0:T(8,128)(2,1)S(1)} %get-tuple-element.64), channel_id=1, source_target_pairs={{0,1},{1,0},{2,3},{3,2},{4,5},{5,4},{6,7},{7,6},{8,9},{9,8},{10,11... | collective-permute-start | bytes 479240 | tf_op jit(solution)/shard_map/ppermute | solution.py:29
  42.0 21.1 %collective-permute-start.15 = (bf16[208,1792]{1,0:T(8,128)(2,1)S(1)}, bf16[208,1792]{1,0:T(8,128)(2,1)S(1)}, u32[]{:S(2)}, u32[]{:S(2)}) collective-permute-start(bf16[208,1792]{1,0:T(8,128)(2,1)S(1)} %get-tuple-element.67.refs_0_), channel_id=1, source_target_pairs={{0,2},{1,3},{2,0},{3,1},{4,6},{5,7},{6,4},{7,5},{8,10},{9,11},{10,... | collective-permute-start | bytes 2236424 | tf_op jit(solution)/shard_map/ppermute | solution.py:29
  50.3 2.3 %collective-permute-start.11 = (bf16[208,512]{1,0:T(8,128)(2,1)S(1)}, bf16[208,512]{1,0:T(8,128)(2,1)S(1)}, u32[]{:S(2)}, u32[]{:S(2)}) collective-permute-start(bf16[208,512]{1,0:T(8,128)(2,1)S(1)} %get-tuple-element.69), channel_id=1, source_target_pairs={{0,1},{1,0},{2,3},{3,2},{4,5},{5,4},{6,7},{7,6},{8,9},{9,8},{10,11... | collective-permute-start | bytes 638984 | tf_op jit(solution)/shard_map/ppermute | solution.py:29
  50.4 2.2 %collective-permute-start.13 = (bf16[208,512]{1,0:T(8,128)(2,1)S(1)}, bf16[208,512]{1,0:T(8,128)(2,1)S(1)}, u32[]{:S(2)}, u32[]{:S(2)}) collective-permute-start(bf16[208,512]{1,0:T(8,128)(2,1)S(1)} %get-tuple-element.71), channel_id=1, source_target_pairs={{0,1},{1,0},{2,3},{3,2},{4,5},{5,4},{6,7},{7,6},{8,9},{9,8},{10,11... | collective-permute-start | bytes 638984 | tf_op jit(solution)/shard_map/ppermute | solution.py:29
  50.9 1.5 %collective-permute-start.12 = (bf16[208,384]{1,0:T(8,128)(2,1)S(1)}, bf16[208,384]{1,0:T(8,128)(2,1)S(1)}, u32[]{:S(2)}, u32[]{:S(2)}) collective-permute-start(bf16[208,384]{1,0:T(8,128)(2,1)S(1)} %get-tuple-element.70), channel_id=1, source_target_pairs={{0,1},{1,0},{2,3},{3,2},{4,5},{5,4},{6,7},{7,6},{8,9},{9,8},{10,11... | collective-permute-start | bytes 479240 | tf_op jit(solution)/shard_map/ppermute | solution.py:29
  51.0 1.6 %collective-permute-start.14 = (bf16[208,384]{1,0:T(8,128)(2,1)S(1)}, bf16[208,384]{1,0:T(8,128)(2,1)S(1)}, u32[]{:S(2)}, u32[]{:S(2)}) collective-permute-start(bf16[208,384]{1,0:T(8,128)(2,1)S(1)} %get-tuple-element.72), channel_id=1, source_target_pairs={{0,1},{1,0},{2,3},{3,2},{4,5},{5,4},{6,7},{7,6},{8,9},{9,8},{10,11... | collective-permute-start | bytes 479240 | tf_op jit(solution)/shard_map/ppermute | solution.py:29
  52.9 22.7 %collective-permute-start.20 = (bf16[208,1792]{1,0:T(8,128)(2,1)S(1)}, bf16[208,1792]{1,0:T(8,128)(2,1)S(1)}, u32[]{:S(2)}, u32[]{:S(2)}) collective-permute-start(bf16[208,1792]{1,0:T(8,128)(2,1)S(1)} %get-tuple-element.73.refs_0_), channel_id=1, source_target_pairs={{0,2},{1,3},{2,0},{3,1},{4,6},{5,7},{6,4},{7,5},{8,10},{9,11},{10,... | collective-permute-start | bytes 2236424 | tf_op jit(solution)/shard_map/ppermute | solution.py:29
  60.3 1.5 %collective-permute-start.17 = (bf16[208,384]{1,0:T(8,128)(2,1)S(1)}, bf16[208,384]{1,0:T(8,128)(2,1)S(1)}, u32[]{:S(2)}, u32[]{:S(2)}) collective-permute-start(bf16[208,384]{1,0:T(8,128)(2,1)S(1)} %get-tuple-element.77), channel_id=1, source_target_pairs={{0,1},{1,0},{2,3},{3,2},{4,5},{5,4},{6,7},{7,6},{8,9},{9,8},{10,11... | collective-permute-start | bytes 479240 | tf_op jit(solution)/shard_map/ppermute | solution.py:29
  60.4 2.8 %collective-permute-start.16 = (bf16[208,512]{1,0:T(8,128)(2,1)S(1)}, bf16[208,512]{1,0:T(8,128)(2,1)S(1)}, u32[]{:S(2)}, u32[]{:S(2)}) collective-permute-start(bf16[208,512]{1,0:T(8,128)(2,1)S(1)} %get-tuple-element.76), channel_id=1, source_target_pairs={{0,1},{1,0},{2,3},{3,2},{4,5},{5,4},{6,7},{7,6},{8,9},{9,8},{10,11... | collective-permute-start | bytes 638984 | tf_op jit(solution)/shard_map/ppermute | solution.py:29
  60.9 2.3 %collective-permute-start.18 = (bf16[208,512]{1,0:T(8,128)(2,1)S(1)}, bf16[208,512]{1,0:T(8,128)(2,1)S(1)}, u32[]{:S(2)}, u32[]{:S(2)}) collective-permute-start(bf16[208,512]{1,0:T(8,128)(2,1)S(1)} %get-tuple-element.78), channel_id=1, source_target_pairs={{0,1},{1,0},{2,3},{3,2},{4,5},{5,4},{6,7},{7,6},{8,9},{9,8},{10,11... | collective-permute-start | bytes 638984 | tf_op jit(solution)/shard_map/ppermute | solution.py:29
  61.8 1.4 %collective-permute-start.19 = (bf16[208,384]{1,0:T(8,128)(2,1)S(1)}, bf16[208,384]{1,0:T(8,128)(2,1)S(1)}, u32[]{:S(2)}, u32[]{:S(2)}) collective-permute-start(bf16[208,384]{1,0:T(8,128)(2,1)S(1)} %get-tuple-element.79), channel_id=1, source_target_pairs={{0,1},{1,0},{2,3},{3,2},{4,5},{5,4},{6,7},{7,6},{8,9},{9,8},{10,11... | collective-permute-start | bytes 479240 | tf_op jit(solution)/shard_map/ppermute | solution.py:29
  70.6 5.1 %collective-permute-start.21 = (bf16[208,896]{1,0:T(8,128)(2,1)S(1)}, bf16[208,896]{1,0:T(8,128)(2,1)S(1)}, u32[]{:S(2)}, u32[]{:S(2)}) collective-permute-start(bf16[208,896]{1,0:T(8,128)(2,1)S(1)} %get-tuple-element.83), channel_id=1, source_target_pairs={{0,1},{1,0},{2,3},{3,2},{4,5},{5,4},{6,7},{7,6},{8,9},{9,8},{10,11... | collective-permute-start | bytes 1118216 | tf_op jit(solution)/shard_map/ppermute | solution.py:29
  70.8 4.8 %collective-permute-start.22 = (bf16[208,896]{1,0:T(8,128)(2,1)S(1)}, bf16[208,896]{1,0:T(8,128)(2,1)S(1)}, u32[]{:S(2)}, u32[]{:S(2)}) collective-permute-start(bf16[208,896]{1,0:T(8,128)(2,1)S(1)} %get-tuple-element.84), channel_id=1, source_target_pairs={{0,1},{1,0},{2,3},{3,2},{4,5},{5,4},{6,7},{7,6},{8,9},{9,8},{10,11... | collective-permute-start | bytes 1118216 | tf_op jit(solution)/shard_map/ppermute | solution.py:29
  76.3 9.2 %collective-permute-start.25 = (bf16[208,896]{1,0:T(8,128)(2,1)S(1)}, bf16[208,896]{1,0:T(8,128)(2,1)S(1)}, u32[]{:S(2)}, u32[]{:S(2)}) collective-permute-start(bf16[208,896]{1,0:T(8,128)(2,1)S(1)} %get-tuple-element.85.refs_0_.refs_3_), channel_id=1, source_target_pairs={{0,2},{1,3},{2,0},{3,1},{4,6},{5,7},{6,4},{7,5},{8,10},{9,11},{10,... | collective-permute-start | bytes 1118216 | tf_op jit(solution)/shard_map/ppermute | solution.py:29
  77.9 1.7 %collective-permute-start.23 = (bf16[208,512]{1,0:T(8,128)(2,1)S(1)}, bf16[208,512]{1,0:T(8,128)(2,1)S(1)}, u32[]{:S(2)}, u32[]{:S(2)}) collective-permute-start(bf16[208,512]{1,0:T(8,128)(2,1)S(1)} %get-tuple-element.86), channel_id=1, source_target_pairs={{0,1},{1,0},{2,3},{3,2},{4,5},{5,4},{6,7},{7,6},{8,9},{9,8},{10,11... | collective-permute-start | bytes 638984 | tf_op jit(solution)/shard_map/ppermute | solution.py:29
  77.9 1.7 %collective-permute-start.24 = (bf16[208,384]{1,0:T(8,128)(2,1)S(1)}, bf16[208,384]{1,0:T(8,128)(2,1)S(1)}, u32[]{:S(2)}, u32[]{:S(2)}) collective-permute-start(bf16[208,384]{1,0:T(8,128)(2,1)S(1)} %get-tuple-element.87), channel_id=1, source_target_pairs={{0,1},{1,0},{2,3},{3,2},{4,5},{5,4},{6,7},{7,6},{8,9},{9,8},{10,11... | collective-permute-start | bytes 479240 | tf_op jit(solution)/shard_map/ppermute | solution.py:29
  84.9 13.8 %collective-permute-start.33 = (bf16[208,896]{1,0:T(8,128)(2,1)S(1)}, bf16[208,896]{1,0:T(8,128)(2,1)S(1)}, u32[]{:S(2)}, u32[]{:S(2)}) collective-permute-start(bf16[208,896]{1,0:T(8,128)(2,1)S(1)} %relay.4), channel_id=1, source_target_pairs={{0,2},{1,3},{2,0},{3,1},{4,6},{5,7},{6,4},{7,5},{8,10},{9,11},{10,... | collective-permute-start | bytes 1118216 | tf_op jit(solution)/shard_map/ppermute | solution.py:29
  85.6 1.8 %collective-permute-start.26 = (bf16[208,512]{1,0:T(8,128)(2,1)S(1)}, bf16[208,512]{1,0:T(8,128)(2,1)S(1)}, u32[]{:S(2)}, u32[]{:S(2)}) collective-permute-start(bf16[208,512]{1,0:T(8,128)(2,1)S(1)} %get-tuple-element.91), channel_id=1, source_target_pairs={{0,1},{1,0},{2,3},{3,2},{4,5},{5,4},{6,7},{7,6},{8,9},{9,8},{10,11... | collective-permute-start | bytes 638984 | tf_op jit(solution)/shard_map/ppermute | solution.py:29
  85.6 1.7 %collective-permute-start.27 = (bf16[208,384]{1,0:T(8,128)(2,1)S(1)}, bf16[208,384]{1,0:T(8,128)(2,1)S(1)}, u32[]{:S(2)}, u32[]{:S(2)}) collective-permute-start(bf16[208,384]{1,0:T(8,128)(2,1)S(1)} %get-tuple-element.92), channel_id=1, source_target_pairs={{0,1},{1,0},{2,3},{3,2},{4,5},{5,4},{6,7},{7,6},{8,9},{9,8},{10,11... | collective-permute-start | bytes 479240 | tf_op jit(solution)/shard_map/ppermute | solution.py:29
  86.1 5.5 %collective-permute-start.32 = (bf16[208,384]{1,0:T(8,128)(2,1)S(1)}, bf16[208,384]{1,0:T(8,128)(2,1)S(1)}, u32[]{:S(2)}, u32[]{:S(2)}) collective-permute-start(bf16[208,384]{1,0:T(8,128)(2,1)S(1)} %get-tuple-element.99), channel_id=1, source_target_pairs={{0,1},{1,0},{2,3},{3,2},{4,5},{5,4},{6,7},{7,6},{8,9},{9,8},{10,11... | collective-permute-start | bytes 479240 | tf_op jit(solution)/shard_map/ppermute | solution.py:29
  86.2 7.2 %collective-permute-start.31 = (bf16[208,512]{1,0:T(8,128)(2,1)S(1)}, bf16[208,512]{1,0:T(8,128)(2,1)S(1)}, u32[]{:S(2)}, u32[]{:S(2)}) collective-permute-start(bf16[208,512]{1,0:T(8,128)(2,1)S(1)} %get-tuple-element.98), channel_id=1, source_target_pairs={{0,1},{1,0},{2,3},{3,2},{4,5},{5,4},{6,7},{7,6},{8,9},{9,8},{10,11... | collective-permute-start | bytes 638984 | tf_op jit(solution)/shard_map/ppermute | solution.py:29
  89.9 15.1 %collective-permute-start.28 = (bf16[72,2048]{1,0:T(8,128)(2,1)S(1)}, bf16[72,2048]{1,0:T(8,128)(2,1)S(1)}, u32[]{:S(2)}, u32[]{:S(2)}) collective-permute-start(bf16[72,2048]{1,0:T(8,128)(2,1)S(1)} %get-tuple-element.94), channel_id=1, source_target_pairs={{0,4},{4,0},{8,12},{12,8},{16,20},{20,16},{24,28},{28,24},{1,5},{5... | collective-permute-start | bytes 884744 | tf_op jit(solution)/shard_map/ppermute | solution.py:29
  91.4 15.4 %collective-permute-start.29 = (bf16[72,2048]{1,0:T(8,128)(2,1)S(1)}, bf16[72,2048]{1,0:T(8,128)(2,1)S(1)}, u32[]{:S(2)}, u32[]{:S(2)}) collective-permute-start(bf16[72,2048]{1,0:T(8,128)(2,1)S(1)} %get-tuple-element.95), channel_id=1, source_target_pairs={{0,8},{4,12},{8,0},{12,4},{16,24},{20,28},{24,16},{28,20},{1,9},{5... | collective-permute-start | bytes 884744 | tf_op jit(solution)/shard_map/ppermute | solution.py:29
  91.7 15.1 %collective-permute-start.30 = (bf16[72,2048]{1,0:T(8,128)(2,1)S(1)}, bf16[72,2048]{1,0:T(8,128)(2,1)S(1)}, u32[]{:S(2)}, u32[]{:S(2)}) collective-permute-start(bf16[72,2048]{1,0:T(8,128)(2,1)S(1)} %get-tuple-element.96), channel_id=1, source_target_pairs={{0,12},{4,8},{8,4},{12,0},{16,28},{20,24},{24,20},{28,16},{1,13},{... | collective-permute-start | bytes 884744 | tf_op jit(solution)/shard_map/ppermute | solution.py:29
  98.7 27.5 %copy-start.1 = (bf16[96,2048]{1,0:T(8,128)(2,1)S(1)}, bf16[96,2048]{1,0:T(8,128)(2,1)}, u32[]{:S(2)}) copy-start(bf16[96,2048]{1,0:T(8,128)(2,1)} %tokens_ref.1) | copy-start | bytes 1179652
  98.7 27.5 %copy-start.5 = (s32[1,72]{1,0:T(1,128)S(1)}, s32[1,72]{1,0:T(1,128)}, u32[]{:S(2)}) copy-start(s32[1,72]{1,0:T(1,128)} %chosen_ref.1) | copy-start | bytes 868
  98.7 27.5 %copy-start.6 = (f32[96]{0:T(128)S(1)}, f32[96]{0:T(128)}, u32[]{:S(2)}) copy-start(f32[96]{0:T(128)} %param.11) | copy-start | bytes 1156
  98.8 1.8 %collective-permute-start.34 = (bf16[208,512]{1,0:T(8,128)(2,1)S(1)}, bf16[208,512]{1,0:T(8,128)(2,1)S(1)}, u32[]{:S(2)}, u32[]{:S(2)}) collective-permute-start(bf16[208,512]{1,0:T(8,128)(2,1)S(1)} %get-tuple-element.103), channel_id=1, source_target_pairs={{0,1},{1,0},{2,3},{3,2},{4,5},{5,4},{6,7},{7,6},{8,9},{9,8},{10,11... | collective-permute-start | bytes 638984 | tf_op jit(solution)/shard_map/ppermute | solution.py:29
  98.9 1.7 %collective-permute-start.35 = (bf16[208,384]{1,0:T(8,128)(2,1)S(1)}, bf16[208,384]{1,0:T(8,128)(2,1)S(1)}, u32[]{:S(2)}, u32[]{:S(2)}) collective-permute-start(bf16[208,384]{1,0:T(8,128)(2,1)S(1)} %get-tuple-element.104), channel_id=1, source_target_pairs={{0,1},{1,0},{2,3},{3,2},{4,5},{5,4},{6,7},{7,6},{8,9},{9,8},{10,11... | collective-permute-start | bytes 479240 | tf_op jit(solution)/shard_map/ppermute | solution.py:29
  103.2 9.7 %collective-permute-start.37 = (bf16[72,2048]{1,0:T(8,128)(2,1)S(1)}, bf16[72,2048]{1,0:T(8,128)(2,1)S(1)}, u32[]{:S(2)}, u32[]{:S(2)}) collective-permute-start(bf16[72,2048]{1,0:T(8,128)(2,1)S(1)} %get-tuple-element.106), channel_id=1, source_target_pairs={{0,4},{4,0},{8,12},{12,8},{16,20},{20,16},{24,28},{28,24},{1,5},{5... | collective-permute-start | bytes 884744 | tf_op jit(solution)/shard_map/ppermute | solution.py:29
  104.7 16.2 %collective-permute-start.38 = (bf16[72,2048]{1,0:T(8,128)(2,1)S(1)}, bf16[72,2048]{1,0:T(8,128)(2,1)S(1)}, u32[]{:S(2)}, u32[]{:S(2)}) collective-permute-start(bf16[72,2048]{1,0:T(8,128)(2,1)S(1)} %get-tuple-element.107), channel_id=1, source_target_pairs={{0,8},{4,12},{8,0},{12,4},{16,24},{20,28},{24,16},{28,20},{1,9},{5... | collective-permute-start | bytes 884744 | tf_op jit(solution)/shard_map/ppermute | solution.py:29
  105.0 21.2 %collective-permute-start.39 = (bf16[72,2048]{1,0:T(8,128)(2,1)S(1)}, bf16[72,2048]{1,0:T(8,128)(2,1)S(1)}, u32[]{:S(2)}, u32[]{:S(2)}) collective-permute-start(bf16[72,2048]{1,0:T(8,128)(2,1)S(1)} %get-tuple-element.108), channel_id=1, source_target_pairs={{0,12},{4,8},{8,4},{12,0},{16,28},{20,24},{24,20},{28,16},{1,13},{... | collective-permute-start | bytes 884744 | tf_op jit(solution)/shard_map/ppermute | solution.py:29
  106.9 19.3 %collective-permute-start.36 = (bf16[72,2048]{1,0:T(8,128)(2,1)S(1)}, bf16[72,2048]{1,0:T(8,128)(2,1)S(1)}, u32[]{:S(2)}, u32[]{:S(2)}) collective-permute-start(bf16[72,2048]{1,0:T(8,128)(2,1)S(1)} %sum.1), channel_id=1, source_target_pairs={{0,16},{4,20},{8,24},{12,28},{16,0},{20,4},{24,8},{28,12},{1,17},{... | collective-permute-start | bytes 884744 | tf_op jit(solution)/shard_map/ppermute | solution.py:29

commit v5 on v4

--- a/solution.py
+++ b/solution.py
@@ -12,6 +12,7 @@
 SURE = SEL // 2
 SLACK = SEL // 4
 GROUP = 4
+ORDER = (2, 3, 1)
 EPS = 1e-05
 NONE = 1024.0
 MIB = 1 << 20
@@ -377,7 +378,7 @@
 
 
 def reduce_group(blocks, n_ctx, after):
-    got = [blocks[0]] + [swap(blocks[j], "ctx", n_ctx, j) for j in range(1, GROUP)]
+    got = [blocks[0]] + [swap(blocks[j], "ctx", n_ctx, j) for j in ORDER]
     return call(
         sum_kernel, [(blocks[0].shape, BF16)], got, [VMEM] * GROUP, "sum", 16, after=after
     )[0]
@@ -451,10 +452,11 @@
 
     total = 0.0
     for number, parts in enumerate(blocks[:-1]):
-        summed = reduce_group(parts, n_ctx, blocks[-1][:1])
+        summed = reduce_group(parts, n_ctx, [])
         total = total + swap(summed, "ctx", n_ctx, GROUP * (number + 1)).astype(F32)
-    for number, part in enumerate(blocks[-1]):
-        total = total + (swap(part, "ctx", n_ctx, number) if number else part).astype(F32)
+    total = total + blocks[-1][0].astype(F32)
+    for j in ORDER:
+        total = total + swap(blocks[-1][j], "ctx", n_ctx, j).astype(F32)
 
     ffn = total.astype(BF16)
     active = jnp.arange(most, dtype=jnp.int32) < counts[0]

time: 128 us -> 127 us (level)
  no operation moved by 1% of the time
where the time goes in v5:
time: 127 us
  Pallas kernels  47.4 us (37%)
  waiting for transfers between devices  45.7 us (36%)
  starting transfers between devices  29.6 us (23%)
  local copies, waits for them, and re-layouts  2.37 us (2%)
    pallas_call x19, Pallas kernels, call(): pl.pallas_call(kernel, out_shape=[jax.ShapeDtypeStruct(*out) if isinstanc...  47.4 us
    ppermute x40, waiting for transfers between devices, swap(): return lax.ppermute(value, axis, [(i, i ^ bit) for i in range(size)])  45.7 us
    ppermute x40, starting transfers between devices, swap(): return lax.ppermute(value, axis, [(i, i ^ bit) for i in range(size)])  29.6 us
  transfers between devices with their start and end apart: 40, of which 14 were waited for; matrix products, arithmetic and copies ran while one was open for 0% of the time, Pallas kernels for 36%

profile of v5, /device:TPU:0, one launch (start us, length us, event | category | flops | bytes accessed | tf_op | source)
XLA Modules:
  0.0 127.1 jit_solution(4619066318237075500)
XLA Ops:
  0.7 1.0 copy-done
  1.7 0.7 copy-done.4
  2.6 4.1 %collective-permute-start = (bf16[72,2048]{1,0:T(8,128)(2,1)S(1)}, bf16[72,2048]{1,0:T(8,128)(2,1)S(1)}, u32[]{:S(2)}, u32[]{:S(2)}) collective-permute-start(bf16[72,2048]{1,0:T(8,128)(2,1)S(1)} %pick.1.refs_0_), channel_id=1, source_target_pairs={{0,16},{4,20},{8,24},{12,28},{16,0},{20,4},{24,8},{28,12},{1,17},{... | collective-permute-start | bytes 884744 | tf_op jit(solution)/shard_map/ppermute | solution.py:30
  6.7 1.5 %collective-permute-start.4 = (bf16[72,2048]{1,0:T(8,128)(2,1)S(1)}, bf16[72,2048]{1,0:T(8,128)(2,1)S(1)}, u32[]{:S(2)}, u32[]{:S(2)}) collective-permute-start(bf16[72,2048]{1,0:T(8,128)(2,1)S(1)} %pick.1.refs_0_), channel_id=1, source_target_pairs={{0,4},{4,0},{8,12},{12,8},{16,20},{20,16},{24,28},{28,24},{1,5},{5... | collective-permute-start | bytes 884744 | tf_op jit(solution)/shard_map/ppermute | solution.py:30
  8.2 1.6 %collective-permute-start.5 = (bf16[72,2048]{1,0:T(8,128)(2,1)S(1)}, bf16[72,2048]{1,0:T(8,128)(2,1)S(1)}, u32[]{:S(2)}, u32[]{:S(2)}) collective-permute-start(bf16[72,2048]{1,0:T(8,128)(2,1)S(1)} %pick.1.refs_0_), channel_id=1, source_target_pairs={{0,8},{4,12},{8,0},{12,4},{16,24},{20,28},{24,16},{28,20},{1,9},{5... | collective-permute-start | bytes 884744 | tf_op jit(solution)/shard_map/ppermute | solution.py:30
  10.2 9.9 %collective-permute-done.refs_0_ = bf16[72,2048]{1,0:T(8,128)(2,1)S(1)} collective-permute-done((bf16[72,2048]{1,0:T(8,128)(2,1)S(1)}, bf16[72,2048]{1,0:T(8,128)(2,1)S(1)}, u32[]{:S(2)}, u32[]{:S(2)}) %collective-permute-start) | collective-permute-done | bytes 294944 | tf_op jit(solution)/shard_map/ppermute | solution.py:30
  20.1 1.5 %collective-permute-start.1 = (bf16[72,2048]{1,0:T(8,128)(2,1)S(1)}, bf16[72,2048]{1,0:T(8,128)(2,1)S(1)}, u32[]{:S(2)}, u32[]{:S(2)}) collective-permute-start(bf16[72,2048]{1,0:T(8,128)(2,1)S(1)} %collective-permute-done.refs_0_), channel_id=1, source_target_pairs={{0,4},{4,0},{8,12},{12,8},{16,20},{20,16},{24,28},{28,24},{1,5},{5... | collective-permute-start | bytes 884744 | tf_op jit(solution)/shard_map/ppermute | solution.py:30
  21.7 0.6 collective-permute-start.2
  22.3 1.3 %collective-permute-start.3 = (bf16[72,2048]{1,0:T(8,128)(2,1)S(1)}, bf16[72,2048]{1,0:T(8,128)(2,1)S(1)}, u32[]{:S(2)}, u32[]{:S(2)}) collective-permute-start(bf16[72,2048]{1,0:T(8,128)(2,1)S(1)} %collective-permute-done.refs_0_), channel_id=1, source_target_pairs={{0,12},{4,8},{8,4},{12,0},{16,28},{20,24},{24,20},{28,16},{1,13},{... | collective-permute-start | bytes 884744 | tf_op jit(solution)/shard_map/ppermute | solution.py:30
  23.6 6.1 %collective-permute-done.6.refs_3_ = bf16[72,2048]{1,0:T(8,128)(2,1)S(1)} collective-permute-done((bf16[72,2048]{1,0:T(8,128)(2,1)S(1)}, bf16[72,2048]{1,0:T(8,128)(2,1)S(1)}, u32[]{:S(2)}, u32[]{:S(2)}) %collective-permute-start.6) | collective-permute-done | bytes 294944 | tf_op jit(solution)/shard_map/ppermute | solution.py:30
  29.7 0.7 copy-done.2
  30.4 1.1 assemble_208.3
  31.5 6.7 %gate_up_208_0.2 = (bf16[208,512]{1,0:T(8,128)(2,1)S(1)}, bf16[208,384]{1,0:T(8,128)(2,1)S(1)}, bf16[208,512]{1,0:T(8,128)(2,1)S(1)}, bf16[208,384]{1,0:T(8,128)(2,1)S(1)}, bf16[208,1792]{1,0:T(8,128)(2,1)S(1)}) custom-call(s32[1]{0:T(128)} %bitcast.2.me_ref, bf16[208,2048]{1,0:T(8,128)(2,1)S(1)} %get-tuple-element.60.x_ref, ...), custom_call_target="tpu_custom_call" | custom-call | tf_op jit(solution)/shard_map/gate_up_208_0/pallas_call | solution.py:34
  38.3 0.5 collective-permute-start.9
  39.3 1.3 collective-permute-done.3.refs_3_
  40.6 1.1 assemble_208.2
  42.0 1.6 %collective-permute-start.15 = (bf16[208,1792]{1,0:T(8,128)(2,1)S(1)}, bf16[208,1792]{1,0:T(8,128)(2,1)S(1)}, u32[]{:S(2)}, u32[]{:S(2)}) collective-permute-start(bf16[208,1792]{1,0:T(8,128)(2,1)S(1)} %get-tuple-element.67.refs_0_), channel_id=1, source_target_pairs={{0,2},{1,3},{2,0},{3,1},{4,6},{5,7},{6,4},{7,5},{8,10},{9,11},{10,... | collective-permute-start | bytes 2236424 | tf_op jit(solution)/shard_map/ppermute | solution.py:30
  43.6 6.7 %gate_up_208_0.3 = (bf16[208,512]{1,0:T(8,128)(2,1)S(1)}, bf16[208,384]{1,0:T(8,128)(2,1)S(1)}, bf16[208,512]{1,0:T(8,128)(2,1)S(1)}, bf16[208,384]{1,0:T(8,128)(2,1)S(1)}, bf16[208,1792]{1,0:T(8,128)(2,1)S(1)}) custom-call(s32[1]{0:T(128)} %bitcast.2.me_ref, bf16[208,2048]{1,0:T(8,128)(2,1)S(1)} %get-tuple-element.58.refs_4_.x_ref, ...), custom_call_target="tpu_custom_call" | custom-call | tf_op jit(solution)/shard_map/gate_up_208_0/pallas_call | solution.py:34
  51.4 1.0 collective-permute-done.12.refs_1_
  52.9 0.6 collective-permute-start.20
  53.5 6.8 %gate_up_208_1.2 = (bf16[208,512]{1,0:T(8,128)(2,1)S(1)}, bf16[208,384]{1,0:T(8,128)(2,1)S(1)}, bf16[208,512]{1,0:T(8,128)(2,1)S(1)}, bf16[208,384]{1,0:T(8,128)(2,1)S(1)}, bf16[208,1792]{1,0:T(8,128)(2,1)S(1)}) custom-call(s32[1]{0:T(128)} %bitcast.2.me_ref, bf16[208,2048]{1,0:T(8,128)(2,1)S(1)} %get-tuple-element.60.x_ref, ...), custom_call_target="tpu_custom_call" | custom-call | tf_op jit(solution)/shard_map/gate_up_208_1/pallas_call | solution.py:34
  61.0 0.8 collective-permute-done.17.refs_1_
  61.9 1.2 collective-permute-done.19.refs_3_
  63.2 0.7 silu.2
  63.9 6.7 %gate_up_208_1.3 = (bf16[208,896]{1,0:T(8,128)(2,1)S(1)}, bf16[208,896]{1,0:T(8,128)(2,1)S(1)}, bf16[208,1792]{1,0:T(8,128)(2,1)S(1)}) custom-call(s32[1]{0:T(128)} %bitcast.2.me_ref, bf16[208,2048]{1,0:T(8,128)(2,1)S(1)} %get-tuple-element.58.refs_4_.x_ref, f32[8,256]{1,0:T(8,128)S(1)} %get-tuple-element.59.s_ref, bf16[2048,3584]{1,0:T(8,128)(2,1)} %g_ref.7, ...), custom_call_target="tpu_custom_call" | custom-call | tf_op jit(solution)/shard_map/gate_up_208_1/pallas_call | solution.py:34
  71.1 4.5 %collective-permute-done.20.c_ref = bf16[208,1792]{1,0:T(8,128)(2,1)S(1)} collective-permute-done((bf16[208,1792]{1,0:T(8,128)(2,1)S(1)}, bf16[208,1792]{1,0:T(8,128)(2,1)S(1)}, u32[]{:S(2)}, u32[]{:S(2)}) %collective-permute-start.20) | collective-permute-done | bytes 745504 | tf_op jit(solution)/shard_map/ppermute | solution.py:30
  75.6 0.7 silu.3
  76.3 1.6 %collective-permute-start.25 = (bf16[208,896]{1,0:T(8,128)(2,1)S(1)}, bf16[208,896]{1,0:T(8,128)(2,1)S(1)}, u32[]{:S(2)}, u32[]{:S(2)}) collective-permute-start(bf16[208,896]{1,0:T(8,128)(2,1)S(1)} %get-tuple-element.85.refs_0_.refs_3_), channel_id=1, source_target_pairs={{0,2},{1,3},{2,0},{3,1},{4,6},{5,7},{6,4},{7,5},{8,10},{9,11},{10,... | collective-permute-start | bytes 1118216 | tf_op jit(solution)/shard_map/ppermute | solution.py:30
  77.9 0.5 collective-permute-start.24
  78.4 1.2 collective-permute-done.24.refs_2_
  79.6 5.3 %down_208_0.2 = (f32[208,2048]{1,0:T(8,128)S(1)}, bf16[4,512,2048]{2,1,0:T(8,128)(2,1)S(1)}) custom-call(s32[1]{0:T(128)} %bitcast.2.me_ref, f32[8,256]{1,0:T(8,128)S(1)} %get-tuple-element.57.extras_ref, bf16[3584,2048]{1,0:T(8,128)(2,1)} %w_ref.3, bf16[208,896]{1,0:T(8,128)(2,1)S(1)} %get-tuple-element.85.refs_0_.refs_3_, ...), custom_call_target="tpu_custom_call" | custom-call | tf_op jit(solution)/shard_map/down_208_0/pallas_call | solution.py:34
  84.9 0.6 collective-permute-start.34
  86.6 0.7 collective-permute-done.27.refs_2_
  87.3 2.5 %down_208_1.2 = (bf16[72,2048]{1,0:T(8,128)(2,1)S(1)}, bf16[72,2048]{1,0:T(8,128)(2,1)S(1)}, bf16[72,2048]{1,0:T(8,128)(2,1)S(1)}, bf16[72,2048]{1,0:T(8,128)(2,1)S(1)}) custom-call(s32[1]{0:T(128)} %bitcast.2.me_ref, f32[8,256]{1,0:T(8,128)S(1)} %get-tuple-element.57.extras_ref, bf16[4,512,2048]{2,1,0:T(8,128)(2,1)S(1)} %get-tuple-element.88.w_ref, ...), custom_call_target="tpu_custom_call" | custom-call | tf_op jit(solution)/shard_map/down_208_1/pallas_call | solution.py:34
  89.9 1.3 collective-permute-start.28
  91.1 1.7 %collective-permute-start.29 = (bf16[72,2048]{1,0:T(8,128)(2,1)S(1)}, bf16[72,2048]{1,0:T(8,128)(2,1)S(1)}, u32[]{:S(2)}, u32[]{:S(2)}) collective-permute-start(bf16[72,2048]{1,0:T(8,128)(2,1)S(1)} %get-tuple-element.95), channel_id=1, source_target_pairs={{0,12},{4,8},{8,4},{12,0},{16,28},{20,24},{24,20},{28,16},{1,13},{... | collective-permute-start | bytes 884744 | tf_op jit(solution)/shard_map/ppermute | solution.py:30
  92.8 0.6 collective-permute-start.30
  93.4 5.3 %down_208_0.3 = (f32[208,2048]{1,0:T(8,128)S(1)}, bf16[4,512,2048]{2,1,0:T(8,128)(2,1)S(1)}) custom-call(s32[1]{0:T(128)} %bitcast.2.me_ref, f32[8,256]{1,0:T(8,128)S(1)} %get-tuple-element.97.extras_ref, bf16[3584,2048]{1,0:T(8,128)(2,1)} %w_ref.3, bf16[208,896]{1,0:T(8,128)(2,1)S(1)} %get-tuple-element.80.refs_0_.in_ref, ...), custom_call_target="tpu_custom_call" | custom-call | tf_op jit(solution)/shard_map/down_208_0/pallas_call | solution.py:34
  99.4 1.2 collective-permute-done.36.refs_2_
  100.6 2.6 %down_208_1.3 = (bf16[72,2048]{1,0:T(8,128)(2,1)S(1)}, bf16[72,2048]{1,0:T(8,128)(2,1)S(1)}, bf16[72,2048]{1,0:T(8,128)(2,1)S(1)}, bf16[72,2048]{1,0:T(8,128)(2,1)S(1)}) custom-call(s32[1]{0:T(128)} %bitcast.2.me_ref, f32[8,256]{1,0:T(8,128)S(1)} %get-tuple-element.97.extras_ref, bf16[4,512,2048]{2,1,0:T(8,128)(2,1)S(1)} %get-tuple-element.100.w_ref, ...), custom_call_target="tpu_custom_call" | custom-call | tf_op jit(solution)/shard_map/down_208_1/pallas_call | solution.py:34
  103.2 1.2 collective-permute-start.37
  104.4 1.7 %collective-permute-start.38 = (bf16[72,2048]{1,0:T(8,128)(2,1)S(1)}, bf16[72,2048]{1,0:T(8,128)(2,1)S(1)}, u32[]{:S(2)}, u32[]{:S(2)}) collective-permute-start(bf16[72,2048]{1,0:T(8,128)(2,1)S(1)} %get-tuple-element.107), channel_id=1, source_target_pairs={{0,12},{4,8},{8,4},{12,0},{16,28},{20,24},{24,20},{28,16},{1,13},{... | collective-permute-start | bytes 884744 | tf_op jit(solution)/shard_map/ppermute | solution.py:30
  106.2 0.6 collective-permute-start.39
  106.7 1.0 collective-permute-done.30.d_ref
  107.9 1.4 %collective-permute-start.31 = (bf16[72,2048]{1,0:T(8,128)(2,1)S(1)}, bf16[72,2048]{1,0:T(8,128)(2,1)S(1)}, u32[]{:S(2)}, u32[]{:S(2)}) collective-permute-start(bf16[72,2048]{1,0:T(8,128)(2,1)S(1)} %sum.1), channel_id=1, source_target_pairs={{0,16},{4,20},{8,24},{12,28},{16,0},{20,4},{24,8},{28,12},{1,17},{... | collective-permute-start | bytes 884744 | tf_op jit(solution)/shard_map/ppermute | solution.py:30
  109.3 10.1 %collective-permute-done.37 = bf16[72,2048]{1,0:T(8,128)(2,1)S(1)} collective-permute-done((bf16[72,2048]{1,0:T(8,128)(2,1)S(1)}, bf16[72,2048]{1,0:T(8,128)(2,1)S(1)}, u32[]{:S(2)}, u32[]{:S(2)}) %collective-permute-start.37) | collective-permute-done | bytes 294944 | tf_op jit(solution)/shard_map/ppermute | solution.py:30
  119.4 6.5 %collective-permute-done.38 = bf16[72,2048]{1,0:T(8,128)(2,1)S(1)} collective-permute-done((bf16[72,2048]{1,0:T(8,128)(2,1)S(1)}, bf16[72,2048]{1,0:T(8,128)(2,1)S(1)}, u32[]{:S(2)}, u32[]{:S(2)}) %collective-permute-start.38) | collective-permute-done | bytes 294944 | tf_op jit(solution)/shard_map/ppermute | solution.py:30
  125.9 1.1 fusion.1
  (67 shorter events, 6.6 us)
Async XLA Ops:
  0.7 1.0 copy-start
  1.7 0.7 copy-start.4
  2.6 17.5 %collective-permute-start = (bf16[72,2048]{1,0:T(8,128)(2,1)S(1)}, bf16[72,2048]{1,0:T(8,128)(2,1)S(1)}, u32[]{:S(2)}, u32[]{:S(2)}) collective-permute-start(bf16[72,2048]{1,0:T(8,128)(2,1)S(1)} %pick.1.refs_0_), channel_id=1, source_target_pairs={{0,16},{4,20},{8,24},{12,28},{16,0},{20,4},{24,8},{28,12},{1,17},{... | collective-permute-start | bytes 884744 | tf_op jit(solution)/shard_map/ppermute | solution.py:30
  6.7 15.6 %collective-permute-start.4 = (bf16[72,2048]{1,0:T(8,128)(2,1)S(1)}, bf16[72,2048]{1,0:T(8,128)(2,1)S(1)}, u32[]{:S(2)}, u32[]{:S(2)}) collective-permute-start(bf16[72,2048]{1,0:T(8,128)(2,1)S(1)} %pick.1.refs_0_), channel_id=1, source_target_pairs={{0,4},{4,0},{8,12},{12,8},{16,20},{20,16},{24,28},{28,24},{1,5},{5... | collective-permute-start | bytes 884744 | tf_op jit(solution)/shard_map/ppermute | solution.py:30
  8.2 15.4 %collective-permute-start.5 = (bf16[72,2048]{1,0:T(8,128)(2,1)S(1)}, bf16[72,2048]{1,0:T(8,128)(2,1)S(1)}, u32[]{:S(2)}, u32[]{:S(2)}) collective-permute-start(bf16[72,2048]{1,0:T(8,128)(2,1)S(1)} %pick.1.refs_0_), channel_id=1, source_target_pairs={{0,8},{4,12},{8,0},{12,4},{16,24},{20,28},{24,16},{28,20},{1,9},{5... | collective-permute-start | bytes 884744 | tf_op jit(solution)/shard_map/ppermute | solution.py:30
  9.8 19.9 %collective-permute-start.6 = (bf16[72,2048]{1,0:T(8,128)(2,1)S(1)}, bf16[72,2048]{1,0:T(8,128)(2,1)S(1)}, u32[]{:S(2)}, u32[]{:S(2)}) collective-permute-start(bf16[72,2048]{1,0:T(8,128)(2,1)S(1)} %pick.1.refs_0_), channel_id=1, source_target_pairs={{0,12},{4,8},{8,4},{12,0},{16,28},{20,24},{24,20},{28,16},{1,13},{... | collective-permute-start | bytes 884744 | tf_op jit(solution)/shard_map/ppermute | solution.py:30
  20.1 18.7 %collective-permute-start.1 = (bf16[72,2048]{1,0:T(8,128)(2,1)S(1)}, bf16[72,2048]{1,0:T(8,128)(2,1)S(1)}, u32[]{:S(2)}, u32[]{:S(2)}) collective-permute-start(bf16[72,2048]{1,0:T(8,128)(2,1)S(1)} %collective-permute-done.refs_0_), channel_id=1, source_target_pairs={{0,4},{4,0},{8,12},{12,8},{16,20},{20,16},{24,28},{28,24},{1,5},{5... | collective-permute-start | bytes 884744 | tf_op jit(solution)/shard_map/ppermute | solution.py:30
  21.7 17.2 %collective-permute-start.2 = (bf16[72,2048]{1,0:T(8,128)(2,1)S(1)}, bf16[72,2048]{1,0:T(8,128)(2,1)S(1)}, u32[]{:S(2)}, u32[]{:S(2)}) collective-permute-start(bf16[72,2048]{1,0:T(8,128)(2,1)S(1)} %collective-permute-done.refs_0_), channel_id=1, source_target_pairs={{0,8},{4,12},{8,0},{12,4},{16,24},{20,28},{24,16},{28,20},{1,9},{5... | collective-permute-start | bytes 884744 | tf_op jit(solution)/shard_map/ppermute | solution.py:30
  22.3 18.3 %collective-permute-start.3 = (bf16[72,2048]{1,0:T(8,128)(2,1)S(1)}, bf16[72,2048]{1,0:T(8,128)(2,1)S(1)}, u32[]{:S(2)}, u32[]{:S(2)}) collective-permute-start(bf16[72,2048]{1,0:T(8,128)(2,1)S(1)} %collective-permute-done.refs_0_), channel_id=1, source_target_pairs={{0,12},{4,8},{8,4},{12,0},{16,28},{20,24},{24,20},{28,16},{1,13},{... | collective-permute-start | bytes 884744 | tf_op jit(solution)/shard_map/ppermute | solution.py:30
  29.7 0.7 copy-start.2
  31.5 9.0 %copy-start.3 = (f32[2048]{0:T(1024)S(1)}, f32[2048]{0:T(1024)}, u32[]{:S(2)}) copy-start(f32[2048]{0:T(1024)} %param.12) | copy-start | bytes 24580
  38.2 3.5 %collective-permute-start.7 = (bf16[208,512]{1,0:T(8,128)(2,1)S(1)}, bf16[208,512]{1,0:T(8,128)(2,1)S(1)}, u32[]{:S(2)}, u32[]{:S(2)}) collective-permute-start(bf16[208,512]{1,0:T(8,128)(2,1)S(1)} %get-tuple-element.63), channel_id=1, source_target_pairs={{0,1},{1,0},{2,3},{3,2},{4,5},{5,4},{6,7},{7,6},{8,9},{9,8},{10,11... | collective-permute-start | bytes 638984 | tf_op jit(solution)/shard_map/ppermute | solution.py:30
  38.3 3.4 %collective-permute-start.9 = (bf16[208,512]{1,0:T(8,128)(2,1)S(1)}, bf16[208,512]{1,0:T(8,128)(2,1)S(1)}, u32[]{:S(2)}, u32[]{:S(2)}) collective-permute-start(bf16[208,512]{1,0:T(8,128)(2,1)S(1)} %get-tuple-element.65), channel_id=1, source_target_pairs={{0,1},{1,0},{2,3},{3,2},{4,5},{5,4},{6,7},{7,6},{8,9},{9,8},{10,11... | collective-permute-start | bytes 638984 | tf_op jit(solution)/shard_map/ppermute | solution.py:30
  38.8 2.9 %collective-permute-start.10 = (bf16[208,384]{1,0:T(8,128)(2,1)S(1)}, bf16[208,384]{1,0:T(8,128)(2,1)S(1)}, u32[]{:S(2)}, u32[]{:S(2)}) collective-permute-start(bf16[208,384]{1,0:T(8,128)(2,1)S(1)} %get-tuple-element.66), channel_id=1, source_target_pairs={{0,1},{1,0},{2,3},{3,2},{4,5},{5,4},{6,7},{7,6},{8,9},{9,8},{10,11... | collective-permute-start | bytes 479240 | tf_op jit(solution)/shard_map/ppermute | solution.py:30
  38.9 2.8 %collective-permute-start.8 = (bf16[208,384]{1,0:T(8,128)(2,1)S(1)}, bf16[208,384]{1,0:T(8,128)(2,1)S(1)}, u32[]{:S(2)}, u32[]{:S(2)}) collective-permute-start(bf16[208,384]{1,0:T(8,128)(2,1)S(1)} %get-tuple-element.64), channel_id=1, source_target_pairs={{0,1},{1,0},{2,3},{3,2},{4,5},{5,4},{6,7},{7,6},{8,9},{9,8},{10,11... | collective-permute-start | bytes 479240 | tf_op jit(solution)/shard_map/ppermute | solution.py:30
  42.0 21.1 %collective-permute-start.15 = (bf16[208,1792]{1,0:T(8,128)(2,1)S(1)}, bf16[208,1792]{1,0:T(8,128)(2,1)S(1)}, u32[]{:S(2)}, u32[]{:S(2)}) collective-permute-start(bf16[208,1792]{1,0:T(8,128)(2,1)S(1)} %get-tuple-element.67.refs_0_), channel_id=1, source_target_pairs={{0,2},{1,3},{2,0},{3,1},{4,6},{5,7},{6,4},{7,5},{8,10},{9,11},{10,... | collective-permute-start | bytes 2236424 | tf_op jit(solution)/shard_map/ppermute | solution.py:30
  50.3 2.3 %collective-permute-start.11 = (bf16[208,512]{1,0:T(8,128)(2,1)S(1)}, bf16[208,512]{1,0:T(8,128)(2,1)S(1)}, u32[]{:S(2)}, u32[]{:S(2)}) collective-permute-start(bf16[208,512]{1,0:T(8,128)(2,1)S(1)} %get-tuple-element.69), channel_id=1, source_target_pairs={{0,1},{1,0},{2,3},{3,2},{4,5},{5,4},{6,7},{7,6},{8,9},{9,8},{10,11... | collective-permute-start | bytes 638984 | tf_op jit(solution)/shard_map/ppermute | solution.py:30
  50.4 2.2 %collective-permute-start.13 = (bf16[208,512]{1,0:T(8,128)(2,1)S(1)}, bf16[208,512]{1,0:T(8,128)(2,1)S(1)}, u32[]{:S(2)}, u32[]{:S(2)}) collective-permute-start(bf16[208,512]{1,0:T(8,128)(2,1)S(1)} %get-tuple-element.71), channel_id=1, source_target_pairs={{0,1},{1,0},{2,3},{3,2},{4,5},{5,4},{6,7},{7,6},{8,9},{9,8},{10,11... | collective-permute-start | bytes 638984 | tf_op jit(solution)/shard_map/ppermute | solution.py:30
  50.9 1.5 %collective-permute-start.12 = (bf16[208,384]{1,0:T(8,128)(2,1)S(1)}, bf16[208,384]{1,0:T(8,128)(2,1)S(1)}, u32[]{:S(2)}, u32[]{:S(2)}) collective-permute-start(bf16[208,384]{1,0:T(8,128)(2,1)S(1)} %get-tuple-element.70), channel_id=1, source_target_pairs={{0,1},{1,0},{2,3},{3,2},{4,5},{5,4},{6,7},{7,6},{8,9},{9,8},{10,11... | collective-permute-start | bytes 479240 | tf_op jit(solution)/shard_map/ppermute | solution.py:30
  51.0 1.6 %collective-permute-start.14 = (bf16[208,384]{1,0:T(8,128)(2,1)S(1)}, bf16[208,384]{1,0:T(8,128)(2,1)S(1)}, u32[]{:S(2)}, u32[]{:S(2)}) collective-permute-start(bf16[208,384]{1,0:T(8,128)(2,1)S(1)} %get-tuple-element.72), channel_id=1, source_target_pairs={{0,1},{1,0},{2,3},{3,2},{4,5},{5,4},{6,7},{7,6},{8,9},{9,8},{10,11... | collective-permute-start | bytes 479240 | tf_op jit(solution)/shard_map/ppermute | solution.py:30
  52.9 22.7 %collective-permute-start.20 = (bf16[208,1792]{1,0:T(8,128)(2,1)S(1)}, bf16[208,1792]{1,0:T(8,128)(2,1)S(1)}, u32[]{:S(2)}, u32[]{:S(2)}) collective-permute-start(bf16[208,1792]{1,0:T(8,128)(2,1)S(1)} %get-tuple-element.73.refs_0_), channel_id=1, source_target_pairs={{0,2},{1,3},{2,0},{3,1},{4,6},{5,7},{6,4},{7,5},{8,10},{9,11},{10,... | collective-permute-start | bytes 2236424 | tf_op jit(solution)/shard_map/ppermute | solution.py:30
  60.3 1.5 %collective-permute-start.17 = (bf16[208,384]{1,0:T(8,128)(2,1)S(1)}, bf16[208,384]{1,0:T(8,128)(2,1)S(1)}, u32[]{:S(2)}, u32[]{:S(2)}) collective-permute-start(bf16[208,384]{1,0:T(8,128)(2,1)S(1)} %get-tuple-element.77), channel_id=1, source_target_pairs={{0,1},{1,0},{2,3},{3,2},{4,5},{5,4},{6,7},{7,6},{8,9},{9,8},{10,11... | collective-permute-start | bytes 479240 | tf_op jit(solution)/shard_map/ppermute | solution.py:30
  60.4 2.8 %collective-permute-start.16 = (bf16[208,512]{1,0:T(8,128)(2,1)S(1)}, bf16[208,512]{1,0:T(8,128)(2,1)S(1)}, u32[]{:S(2)}, u32[]{:S(2)}) collective-permute-start(bf16[208,512]{1,0:T(8,128)(2,1)S(1)} %get-tuple-element.76), channel_id=1, source_target_pairs={{0,1},{1,0},{2,3},{3,2},{4,5},{5,4},{6,7},{7,6},{8,9},{9,8},{10,11... | collective-permute-start | bytes 638984 | tf_op jit(solution)/shard_map/ppermute | solution.py:30
  60.9 2.3 %collective-permute-start.18 = (bf16[208,512]{1,0:T(8,128)(2,1)S(1)}, bf16[208,512]{1,0:T(8,128)(2,1)S(1)}, u32[]{:S(2)}, u32[]{:S(2)}) collective-permute-start(bf16[208,512]{1,0:T(8,128)(2,1)S(1)} %get-tuple-element.78), channel_id=1, source_target_pairs={{0,1},{1,0},{2,3},{3,2},{4,5},{5,4},{6,7},{7,6},{8,9},{9,8},{10,11... | collective-permute-start | bytes 638984 | tf_op jit(solution)/shard_map/ppermute | solution.py:30
  61.8 1.4 %collective-permute-start.19 = (bf16[208,384]{1,0:T(8,128)(2,1)S(1)}, bf16[208,384]{1,0:T(8,128)(2,1)S(1)}, u32[]{:S(2)}, u32[]{:S(2)}) collective-permute-start(bf16[208,384]{1,0:T(8,128)(2,1)S(1)} %get-tuple-element.79), channel_id=1, source_target_pairs={{0,1},{1,0},{2,3},{3,2},{4,5},{5,4},{6,7},{7,6},{8,9},{9,8},{10,11... | collective-permute-start | bytes 479240 | tf_op jit(solution)/shard_map/ppermute | solution.py:30
  70.6 5.1 %collective-permute-start.21 = (bf16[208,896]{1,0:T(8,128)(2,1)S(1)}, bf16[208,896]{1,0:T(8,128)(2,1)S(1)}, u32[]{:S(2)}, u32[]{:S(2)}) collective-permute-start(bf16[208,896]{1,0:T(8,128)(2,1)S(1)} %get-tuple-element.83), channel_id=1, source_target_pairs={{0,1},{1,0},{2,3},{3,2},{4,5},{5,4},{6,7},{7,6},{8,9},{9,8},{10,11... | collective-permute-start | bytes 1118216 | tf_op jit(solution)/shard_map/ppermute | solution.py:30
  70.8 4.8 %collective-permute-start.22 = (bf16[208,896]{1,0:T(8,128)(2,1)S(1)}, bf16[208,896]{1,0:T(8,128)(2,1)S(1)}, u32[]{:S(2)}, u32[]{:S(2)}) collective-permute-start(bf16[208,896]{1,0:T(8,128)(2,1)S(1)} %get-tuple-element.84), channel_id=1, source_target_pairs={{0,1},{1,0},{2,3},{3,2},{4,5},{5,4},{6,7},{7,6},{8,9},{9,8},{10,11... | collective-permute-start | bytes 1118216 | tf_op jit(solution)/shard_map/ppermute | solution.py:30
  76.3 9.2 %collective-permute-start.25 = (bf16[208,896]{1,0:T(8,128)(2,1)S(1)}, bf16[208,896]{1,0:T(8,128)(2,1)S(1)}, u32[]{:S(2)}, u32[]{:S(2)}) collective-permute-start(bf16[208,896]{1,0:T(8,128)(2,1)S(1)} %get-tuple-element.85.refs_0_.refs_3_), channel_id=1, source_target_pairs={{0,2},{1,3},{2,0},{3,1},{4,6},{5,7},{6,4},{7,5},{8,10},{9,11},{10,... | collective-permute-start | bytes 1118216 | tf_op jit(solution)/shard_map/ppermute | solution.py:30
  77.9 1.7 %collective-permute-start.23 = (bf16[208,512]{1,0:T(8,128)(2,1)S(1)}, bf16[208,512]{1,0:T(8,128)(2,1)S(1)}, u32[]{:S(2)}, u32[]{:S(2)}) collective-permute-start(bf16[208,512]{1,0:T(8,128)(2,1)S(1)} %get-tuple-element.86), channel_id=1, source_target_pairs={{0,1},{1,0},{2,3},{3,2},{4,5},{5,4},{6,7},{7,6},{8,9},{9,8},{10,11... | collective-permute-start | bytes 638984 | tf_op jit(solution)/shard_map/ppermute | solution.py:30
  77.9 1.7 %collective-permute-start.24 = (bf16[208,384]{1,0:T(8,128)(2,1)S(1)}, bf16[208,384]{1,0:T(8,128)(2,1)S(1)}, u32[]{:S(2)}, u32[]{:S(2)}) collective-permute-start(bf16[208,384]{1,0:T(8,128)(2,1)S(1)} %get-tuple-element.87), channel_id=1, source_target_pairs={{0,1},{1,0},{2,3},{3,2},{4,5},{5,4},{6,7},{7,6},{8,9},{9,8},{10,11... | collective-permute-start | bytes 479240 | tf_op jit(solution)/shard_map/ppermute | solution.py:30
  84.9 13.8 %collective-permute-start.34 = (bf16[208,896]{1,0:T(8,128)(2,1)S(1)}, bf16[208,896]{1,0:T(8,128)(2,1)S(1)}, u32[]{:S(2)}, u32[]{:S(2)}) collective-permute-start(bf16[208,896]{1,0:T(8,128)(2,1)S(1)} %relay.4), channel_id=1, source_target_pairs={{0,2},{1,3},{2,0},{3,1},{4,6},{5,7},{6,4},{7,5},{8,10},{9,11},{10,... | collective-permute-start | bytes 1118216 | tf_op jit(solution)/shard_map/ppermute | solution.py:30
  85.6 1.8 %collective-permute-start.26 = (bf16[208,512]{1,0:T(8,128)(2,1)S(1)}, bf16[208,512]{1,0:T(8,128)(2,1)S(1)}, u32[]{:S(2)}, u32[]{:S(2)}) collective-permute-start(bf16[208,512]{1,0:T(8,128)(2,1)S(1)} %get-tuple-element.91), channel_id=1, source_target_pairs={{0,1},{1,0},{2,3},{3,2},{4,5},{5,4},{6,7},{7,6},{8,9},{9,8},{10,11... | collective-permute-start | bytes 638984 | tf_op jit(solution)/shard_map/ppermute | solution.py:30
  85.6 1.7 %collective-permute-start.27 = (bf16[208,384]{1,0:T(8,128)(2,1)S(1)}, bf16[208,384]{1,0:T(8,128)(2,1)S(1)}, u32[]{:S(2)}, u32[]{:S(2)}) collective-permute-start(bf16[208,384]{1,0:T(8,128)(2,1)S(1)} %get-tuple-element.92), channel_id=1, source_target_pairs={{0,1},{1,0},{2,3},{3,2},{4,5},{5,4},{6,7},{7,6},{8,9},{9,8},{10,11... | collective-permute-start | bytes 479240 | tf_op jit(solution)/shard_map/ppermute | solution.py:30
  86.1 6.7 %collective-permute-start.33 = (bf16[208,384]{1,0:T(8,128)(2,1)S(1)}, bf16[208,384]{1,0:T(8,128)(2,1)S(1)}, u32[]{:S(2)}, u32[]{:S(2)}) collective-permute-start(bf16[208,384]{1,0:T(8,128)(2,1)S(1)} %get-tuple-element.99), channel_id=1, source_target_pairs={{0,1},{1,0},{2,3},{3,2},{4,5},{5,4},{6,7},{7,6},{8,9},{9,8},{10,11... | collective-permute-start | bytes 479240 | tf_op jit(solution)/shard_map/ppermute | solution.py:30
  86.2 7.2 %collective-permute-start.32 = (bf16[208,512]{1,0:T(8,128)(2,1)S(1)}, bf16[208,512]{1,0:T(8,128)(2,1)S(1)}, u32[]{:S(2)}, u32[]{:S(2)}) collective-permute-start(bf16[208,512]{1,0:T(8,128)(2,1)S(1)} %get-tuple-element.98), channel_id=1, source_target_pairs={{0,1},{1,0},{2,3},{3,2},{4,5},{5,4},{6,7},{7,6},{8,9},{9,8},{10,11... | collective-permute-start | bytes 638984 | tf_op jit(solution)/shard_map/ppermute | solution.py:30
  89.9 16.3 %collective-permute-start.28 = (bf16[72,2048]{1,0:T(8,128)(2,1)S(1)}, bf16[72,2048]{1,0:T(8,128)(2,1)S(1)}, u32[]{:S(2)}, u32[]{:S(2)}) collective-permute-start(bf16[72,2048]{1,0:T(8,128)(2,1)S(1)} %get-tuple-element.94), channel_id=1, source_target_pairs={{0,8},{4,12},{8,0},{12,4},{16,24},{20,28},{24,16},{28,20},{1,9},{5... | collective-permute-start | bytes 884744 | tf_op jit(solution)/shard_map/ppermute | solution.py:30
  91.1 15.6 %collective-permute-start.29 = (bf16[72,2048]{1,0:T(8,128)(2,1)S(1)}, bf16[72,2048]{1,0:T(8,128)(2,1)S(1)}, u32[]{:S(2)}, u32[]{:S(2)}) collective-permute-start(bf16[72,2048]{1,0:T(8,128)(2,1)S(1)} %get-tuple-element.95), channel_id=1, source_target_pairs={{0,12},{4,8},{8,4},{12,0},{16,28},{20,24},{24,20},{28,16},{1,13},{... | collective-permute-start | bytes 884744 | tf_op jit(solution)/shard_map/ppermute | solution.py:30
  92.8 14.9 %collective-permute-start.30 = (bf16[72,2048]{1,0:T(8,128)(2,1)S(1)}, bf16[72,2048]{1,0:T(8,128)(2,1)S(1)}, u32[]{:S(2)}, u32[]{:S(2)}) collective-permute-start(bf16[72,2048]{1,0:T(8,128)(2,1)S(1)} %get-tuple-element.96), channel_id=1, source_target_pairs={{0,4},{4,0},{8,12},{12,8},{16,20},{20,16},{24,28},{28,24},{1,5},{5... | collective-permute-start | bytes 884744 | tf_op jit(solution)/shard_map/ppermute | solution.py:30
  98.7 27.2 %copy-start.1 = (bf16[96,2048]{1,0:T(8,128)(2,1)S(1)}, bf16[96,2048]{1,0:T(8,128)(2,1)}, u32[]{:S(2)}) copy-start(bf16[96,2048]{1,0:T(8,128)(2,1)} %tokens_ref.1) | copy-start | bytes 1179652
  98.7 27.2 %copy-start.5 = (s32[1,72]{1,0:T(1,128)S(1)}, s32[1,72]{1,0:T(1,128)}, u32[]{:S(2)}) copy-start(s32[1,72]{1,0:T(1,128)} %chosen_ref.1) | copy-start | bytes 868
  98.7 27.2 %copy-start.6 = (f32[96]{0:T(128)S(1)}, f32[96]{0:T(128)}, u32[]{:S(2)}) copy-start(f32[96]{0:T(128)} %param.11) | copy-start | bytes 1156
  98.8 1.8 %collective-permute-start.35 = (bf16[208,512]{1,0:T(8,128)(2,1)S(1)}, bf16[208,512]{1,0:T(8,128)(2,1)S(1)}, u32[]{:S(2)}, u32[]{:S(2)}) collective-permute-start(bf16[208,512]{1,0:T(8,128)(2,1)S(1)} %get-tuple-element.103), channel_id=1, source_target_pairs={{0,1},{1,0},{2,3},{3,2},{4,5},{5,4},{6,7},{7,6},{8,9},{9,8},{10,11... | collective-permute-start | bytes 638984 | tf_op jit(solution)/shard_map/ppermute | solution.py:30
  98.9 1.7 %collective-permute-start.36 = (bf16[208,384]{1,0:T(8,128)(2,1)S(1)}, bf16[208,384]{1,0:T(8,128)(2,1)S(1)}, u32[]{:S(2)}, u32[]{:S(2)}) collective-permute-start(bf16[208,384]{1,0:T(8,128)(2,1)S(1)} %get-tuple-element.104), channel_id=1, source_target_pairs={{0,1},{1,0},{2,3},{3,2},{4,5},{5,4},{6,7},{7,6},{8,9},{9,8},{10,11... | collective-permute-start | bytes 479240 | tf_op jit(solution)/shard_map/ppermute | solution.py:30
  103.2 16.2 %collective-permute-start.37 = (bf16[72,2048]{1,0:T(8,128)(2,1)S(1)}, bf16[72,2048]{1,0:T(8,128)(2,1)S(1)}, u32[]{:S(2)}, u32[]{:S(2)}) collective-permute-start(bf16[72,2048]{1,0:T(8,128)(2,1)S(1)} %get-tuple-element.106), channel_id=1, source_target_pairs={{0,8},{4,12},{8,0},{12,4},{16,24},{20,28},{24,16},{28,20},{1,9},{5... | collective-permute-start | bytes 884744 | tf_op jit(solution)/shard_map/ppermute | solution.py:30
  104.4 21.5 %collective-permute-start.38 = (bf16[72,2048]{1,0:T(8,128)(2,1)S(1)}, bf16[72,2048]{1,0:T(8,128)(2,1)S(1)}, u32[]{:S(2)}, u32[]{:S(2)}) collective-permute-start(bf16[72,2048]{1,0:T(8,128)(2,1)S(1)} %get-tuple-element.107), channel_id=1, source_target_pairs={{0,12},{4,8},{8,4},{12,0},{16,28},{20,24},{24,20},{28,16},{1,13},{... | collective-permute-start | bytes 884744 | tf_op jit(solution)/shard_map/ppermute | solution.py:30
  106.2 19.7 %collective-permute-start.39 = (bf16[72,2048]{1,0:T(8,128)(2,1)S(1)}, bf16[72,2048]{1,0:T(8,128)(2,1)S(1)}, u32[]{:S(2)}, u32[]{:S(2)}) collective-permute-start(bf16[72,2048]{1,0:T(8,128)(2,1)S(1)} %get-tuple-element.108), channel_id=1, source_target_pairs={{0,4},{4,0},{8,12},{12,8},{16,20},{20,16},{24,28},{28,24},{1,5},{5... | collective-permute-start | bytes 884744 | tf_op jit(solution)/shard_map/ppermute | solution.py:30
  107.9 18.0 %collective-permute-start.31 = (bf16[72,2048]{1,0:T(8,128)(2,1)S(1)}, bf16[72,2048]{1,0:T(8,128)(2,1)S(1)}, u32[]{:S(2)}, u32[]{:S(2)}) collective-permute-start(bf16[72,2048]{1,0:T(8,128)(2,1)S(1)} %sum.1), channel_id=1, source_target_pairs={{0,16},{4,20},{8,24},{12,28},{16,0},{20,4},{24,8},{28,12},{1,17},{... | collective-permute-start | bytes 884744 | tf_op jit(solution)/shard_map/ppermute | solution.py:30

commit v6 on v5

--- a/solution.py
+++ b/solution.py
@@ -12,7 +12,7 @@
 SURE = SEL // 2
 SLACK = SEL // 4
 GROUP = 4
-ORDER = (2, 3, 1)
+ORDER = (3, 2, 1)
 EPS = 1e-05
 NONE = 1024.0
 MIB = 1 << 20

time: 127 us -> 127 us (level)
  transfers between devices with their start and end apart: 40 -> 40, of which waited for: 14 -> 13; matrix products, arithmetic and copies ran while one was open for 0% -> 0% of each run, Pallas kernels for 36% -> 36%
where the time goes in v6:
time: 127 us
  Pallas kernels  47.4 us (37%)
  waiting for transfers between devices  45.9 us (36%)
  starting transfers between devices  29.4 us (23%)
  local copies, waits for them, and re-layouts  2.37 us (2%)
    pallas_call x19, Pallas kernels, call(): pl.pallas_call(kernel, out_shape=[jax.ShapeDtypeStruct(*out) if isinstanc...  47.4 us
    ppermute x40, waiting for transfers between devices, swap(): return lax.ppermute(value, axis, [(i, i ^ bit) for i in range(size)])  45.9 us
    ppermute x40, starting transfers between devices, swap(): return lax.ppermute(value, axis, [(i, i ^ bit) for i in range(size)])  29.4 us
  transfers between devices with their start and end apart: 40, of which 13 were waited for; matrix products, arithmetic and copies ran while one was open for 0% of the time, Pallas kernels for 36%

profile of v6, /device:TPU:0, one launch (start us, length us, event | category | flops | bytes accessed | tf_op | source)
XLA Modules:
  0.0 127.1 jit_solution(15672012821601883207)
XLA Ops:
  0.7 1.0 copy-done
  1.7 0.7 copy-done.4
  2.6 4.1 %collective-permute-start = (bf16[72,2048]{1,0:T(8,128)(2,1)S(1)}, bf16[72,2048]{1,0:T(8,128)(2,1)S(1)}, u32[]{:S(2)}, u32[]{:S(2)}) collective-permute-start(bf16[72,2048]{1,0:T(8,128)(2,1)S(1)} %pick.1.refs_0_), channel_id=1, source_target_pairs={{0,16},{4,20},{8,24},{12,28},{16,0},{20,4},{24,8},{28,12},{1,17},{... | collective-permute-start | bytes 884744 | tf_op jit(solution)/shard_map/ppermute | solution.py:30
  6.7 1.5 %collective-permute-start.4 = (bf16[72,2048]{1,0:T(8,128)(2,1)S(1)}, bf16[72,2048]{1,0:T(8,128)(2,1)S(1)}, u32[]{:S(2)}, u32[]{:S(2)}) collective-permute-start(bf16[72,2048]{1,0:T(8,128)(2,1)S(1)} %pick.1.refs_0_), channel_id=1, source_target_pairs={{0,4},{4,0},{8,12},{12,8},{16,20},{20,16},{24,28},{28,24},{1,5},{5... | collective-permute-start | bytes 884744 | tf_op jit(solution)/shard_map/ppermute | solution.py:30
  8.2 1.6 %collective-permute-start.5 = (bf16[72,2048]{1,0:T(8,128)(2,1)S(1)}, bf16[72,2048]{1,0:T(8,128)(2,1)S(1)}, u32[]{:S(2)}, u32[]{:S(2)}) collective-permute-start(bf16[72,2048]{1,0:T(8,128)(2,1)S(1)} %pick.1.refs_0_), channel_id=1, source_target_pairs={{0,8},{4,12},{8,0},{12,4},{16,24},{20,28},{24,16},{28,20},{1,9},{5... | collective-permute-start | bytes 884744 | tf_op jit(solution)/shard_map/ppermute | solution.py:30
  10.2 9.9 %collective-permute-done.refs_0_ = bf16[72,2048]{1,0:T(8,128)(2,1)S(1)} collective-permute-done((bf16[72,2048]{1,0:T(8,128)(2,1)S(1)}, bf16[72,2048]{1,0:T(8,128)(2,1)S(1)}, u32[]{:S(2)}, u32[]{:S(2)}) %collective-permute-start) | collective-permute-done | bytes 294944 | tf_op jit(solution)/shard_map/ppermute | solution.py:30
  20.1 1.5 %collective-permute-start.1 = (bf16[72,2048]{1,0:T(8,128)(2,1)S(1)}, bf16[72,2048]{1,0:T(8,128)(2,1)S(1)}, u32[]{:S(2)}, u32[]{:S(2)}) collective-permute-start(bf16[72,2048]{1,0:T(8,128)(2,1)S(1)} %collective-permute-done.refs_0_), channel_id=1, source_target_pairs={{0,4},{4,0},{8,12},{12,8},{16,20},{20,16},{24,28},{28,24},{1,5},{5... | collective-permute-start | bytes 884744 | tf_op jit(solution)/shard_map/ppermute | solution.py:30
  21.7 0.6 collective-permute-start.2
  22.3 1.3 %collective-permute-start.3 = (bf16[72,2048]{1,0:T(8,128)(2,1)S(1)}, bf16[72,2048]{1,0:T(8,128)(2,1)S(1)}, u32[]{:S(2)}, u32[]{:S(2)}) collective-permute-start(bf16[72,2048]{1,0:T(8,128)(2,1)S(1)} %collective-permute-done.refs_0_), channel_id=1, source_target_pairs={{0,12},{4,8},{8,4},{12,0},{16,28},{20,24},{24,20},{28,16},{1,13},{... | collective-permute-start | bytes 884744 | tf_op jit(solution)/shard_map/ppermute | solution.py:30
  23.6 6.1 %collective-permute-done.6.refs_3_ = bf16[72,2048]{1,0:T(8,128)(2,1)S(1)} collective-permute-done((bf16[72,2048]{1,0:T(8,128)(2,1)S(1)}, bf16[72,2048]{1,0:T(8,128)(2,1)S(1)}, u32[]{:S(2)}, u32[]{:S(2)}) %collective-permute-start.6) | collective-permute-done | bytes 294944 | tf_op jit(solution)/shard_map/ppermute | solution.py:30
  29.7 0.7 copy-done.2
  30.4 1.1 assemble_208.3
  31.5 6.7 %gate_up_208_0.2 = (bf16[208,512]{1,0:T(8,128)(2,1)S(1)}, bf16[208,384]{1,0:T(8,128)(2,1)S(1)}, bf16[208,512]{1,0:T(8,128)(2,1)S(1)}, bf16[208,384]{1,0:T(8,128)(2,1)S(1)}, bf16[208,1792]{1,0:T(8,128)(2,1)S(1)}) custom-call(s32[1]{0:T(128)} %bitcast.2.me_ref, bf16[208,2048]{1,0:T(8,128)(2,1)S(1)} %get-tuple-element.60.x_ref, ...), custom_call_target="tpu_custom_call" | custom-call | tf_op jit(solution)/shard_map/gate_up_208_0/pallas_call | solution.py:34
  38.3 0.5 collective-permute-start.9
  39.3 1.3 collective-permute-done.3.refs_3_
  40.6 1.1 assemble_208.2
  42.0 1.6 %collective-permute-start.15 = (bf16[208,1792]{1,0:T(8,128)(2,1)S(1)}, bf16[208,1792]{1,0:T(8,128)(2,1)S(1)}, u32[]{:S(2)}, u32[]{:S(2)}) collective-permute-start(bf16[208,1792]{1,0:T(8,128)(2,1)S(1)} %get-tuple-element.67.refs_0_), channel_id=1, source_target_pairs={{0,2},{1,3},{2,0},{3,1},{4,6},{5,7},{6,4},{7,5},{8,10},{9,11},{10,... | collective-permute-start | bytes 2236424 | tf_op jit(solution)/shard_map/ppermute | solution.py:30
  43.6 6.7 %gate_up_208_0.3 = (bf16[208,512]{1,0:T(8,128)(2,1)S(1)}, bf16[208,384]{1,0:T(8,128)(2,1)S(1)}, bf16[208,512]{1,0:T(8,128)(2,1)S(1)}, bf16[208,384]{1,0:T(8,128)(2,1)S(1)}, bf16[208,1792]{1,0:T(8,128)(2,1)S(1)}) custom-call(s32[1]{0:T(128)} %bitcast.2.me_ref, bf16[208,2048]{1,0:T(8,128)(2,1)S(1)} %get-tuple-element.58.refs_4_.x_ref, ...), custom_call_target="tpu_custom_call" | custom-call | tf_op jit(solution)/shard_map/gate_up_208_0/pallas_call | solution.py:34
  51.4 1.0 collective-permute-done.12.refs_1_
  52.9 0.6 collective-permute-start.20
  53.5 6.8 %gate_up_208_1.2 = (bf16[208,512]{1,0:T(8,128)(2,1)S(1)}, bf16[208,384]{1,0:T(8,128)(2,1)S(1)}, bf16[208,512]{1,0:T(8,128)(2,1)S(1)}, bf16[208,384]{1,0:T(8,128)(2,1)S(1)}, bf16[208,1792]{1,0:T(8,128)(2,1)S(1)}) custom-call(s32[1]{0:T(128)} %bitcast.2.me_ref, bf16[208,2048]{1,0:T(8,128)(2,1)S(1)} %get-tuple-element.60.x_ref, ...), custom_call_target="tpu_custom_call" | custom-call | tf_op jit(solution)/shard_map/gate_up_208_1/pallas_call | solution.py:34
  61.0 0.8 collective-permute-done.17.refs_1_
  61.9 1.2 collective-permute-done.19.refs_3_
  63.2 0.7 silu.2
  63.9 6.7 %gate_up_208_1.3 = (bf16[208,896]{1,0:T(8,128)(2,1)S(1)}, bf16[208,896]{1,0:T(8,128)(2,1)S(1)}, bf16[208,1792]{1,0:T(8,128)(2,1)S(1)}) custom-call(s32[1]{0:T(128)} %bitcast.2.me_ref, bf16[208,2048]{1,0:T(8,128)(2,1)S(1)} %get-tuple-element.58.refs_4_.x_ref, f32[8,256]{1,0:T(8,128)S(1)} %get-tuple-element.59.s_ref, bf16[2048,3584]{1,0:T(8,128)(2,1)} %g_ref.7, ...), custom_call_target="tpu_custom_call" | custom-call | tf_op jit(solution)/shard_map/gate_up_208_1/pallas_call | solution.py:34
  71.1 4.5 %collective-permute-done.20.c_ref = bf16[208,1792]{1,0:T(8,128)(2,1)S(1)} collective-permute-done((bf16[208,1792]{1,0:T(8,128)(2,1)S(1)}, bf16[208,1792]{1,0:T(8,128)(2,1)S(1)}, u32[]{:S(2)}, u32[]{:S(2)}) %collective-permute-start.20) | collective-permute-done | bytes 745504 | tf_op jit(solution)/shard_map/ppermute | solution.py:30
  75.6 0.7 silu.3
  76.3 1.6 %collective-permute-start.25 = (bf16[208,896]{1,0:T(8,128)(2,1)S(1)}, bf16[208,896]{1,0:T(8,128)(2,1)S(1)}, u32[]{:S(2)}, u32[]{:S(2)}) collective-permute-start(bf16[208,896]{1,0:T(8,128)(2,1)S(1)} %get-tuple-element.85.refs_0_.refs_3_), channel_id=1, source_target_pairs={{0,2},{1,3},{2,0},{3,1},{4,6},{5,7},{6,4},{7,5},{8,10},{9,11},{10,... | collective-permute-start | bytes 1118216 | tf_op jit(solution)/shard_map/ppermute | solution.py:30
  77.9 0.5 collective-permute-start.24
  78.4 1.2 collective-permute-done.24.refs_2_
  79.6 5.3 %down_208_0.2 = (f32[208,2048]{1,0:T(8,128)S(1)}, bf16[4,512,2048]{2,1,0:T(8,128)(2,1)S(1)}) custom-call(s32[1]{0:T(128)} %bitcast.2.me_ref, f32[8,256]{1,0:T(8,128)S(1)} %get-tuple-element.57.extras_ref, bf16[3584,2048]{1,0:T(8,128)(2,1)} %w_ref.3, bf16[208,896]{1,0:T(8,128)(2,1)S(1)} %get-tuple-element.85.refs_0_.refs_3_, ...), custom_call_target="tpu_custom_call" | custom-call | tf_op jit(solution)/shard_map/down_208_0/pallas_call | solution.py:34
  84.9 0.6 collective-permute-start.34
  86.6 0.7 collective-permute-done.27.refs_2_
  87.3 2.5 %down_208_1.2 = (bf16[72,2048]{1,0:T(8,128)(2,1)S(1)}, bf16[72,2048]{1,0:T(8,128)(2,1)S(1)}, bf16[72,2048]{1,0:T(8,128)(2,1)S(1)}, bf16[72,2048]{1,0:T(8,128)(2,1)S(1)}) custom-call(s32[1]{0:T(128)} %bitcast.2.me_ref, f32[8,256]{1,0:T(8,128)S(1)} %get-tuple-element.57.extras_ref, bf16[4,512,2048]{2,1,0:T(8,128)(2,1)S(1)} %get-tuple-element.88.w_ref, ...), custom_call_target="tpu_custom_call" | custom-call | tf_op jit(solution)/shard_map/down_208_1/pallas_call | solution.py:34
  89.9 1.2 collective-permute-start.28
  91.1 1.8 %collective-permute-start.29 = (bf16[72,2048]{1,0:T(8,128)(2,1)S(1)}, bf16[72,2048]{1,0:T(8,128)(2,1)S(1)}, u32[]{:S(2)}, u32[]{:S(2)}) collective-permute-start(bf16[72,2048]{1,0:T(8,128)(2,1)S(1)} %get-tuple-element.95), channel_id=1, source_target_pairs={{0,8},{4,12},{8,0},{12,4},{16,24},{20,28},{24,16},{28,20},{1,9},{5... | collective-permute-start | bytes 884744 | tf_op jit(solution)/shard_map/ppermute | solution.py:30
  92.8 0.6 collective-permute-start.30
  93.4 5.3 %down_208_0.3 = (f32[208,2048]{1,0:T(8,128)S(1)}, bf16[4,512,2048]{2,1,0:T(8,128)(2,1)S(1)}) custom-call(s32[1]{0:T(128)} %bitcast.2.me_ref, f32[8,256]{1,0:T(8,128)S(1)} %get-tuple-element.97.extras_ref, bf16[3584,2048]{1,0:T(8,128)(2,1)} %w_ref.3, bf16[208,896]{1,0:T(8,128)(2,1)S(1)} %get-tuple-element.80.refs_0_.in_ref, ...), custom_call_target="tpu_custom_call" | custom-call | tf_op jit(solution)/shard_map/down_208_0/pallas_call | solution.py:34
  98.9 0.5 collective-permute-start.36
  99.4 1.2 collective-permute-done.36.refs_2_
  100.6 2.6 %down_208_1.3 = (bf16[72,2048]{1,0:T(8,128)(2,1)S(1)}, bf16[72,2048]{1,0:T(8,128)(2,1)S(1)}, bf16[72,2048]{1,0:T(8,128)(2,1)S(1)}, bf16[72,2048]{1,0:T(8,128)(2,1)S(1)}) custom-call(s32[1]{0:T(128)} %bitcast.2.me_ref, f32[8,256]{1,0:T(8,128)S(1)} %get-tuple-element.97.extras_ref, bf16[4,512,2048]{2,1,0:T(8,128)(2,1)S(1)} %get-tuple-element.100.w_ref, ...), custom_call_target="tpu_custom_call" | custom-call | tf_op jit(solution)/shard_map/down_208_1/pallas_call | solution.py:34
  103.2 1.2 collective-permute-start.37
  104.4 1.8 %collective-permute-start.38 = (bf16[72,2048]{1,0:T(8,128)(2,1)S(1)}, bf16[72,2048]{1,0:T(8,128)(2,1)S(1)}, u32[]{:S(2)}, u32[]{:S(2)}) collective-permute-start(bf16[72,2048]{1,0:T(8,128)(2,1)S(1)} %get-tuple-element.107), channel_id=1, source_target_pairs={{0,8},{4,12},{8,0},{12,4},{16,24},{20,28},{24,16},{28,20},{1,9},{5... | collective-permute-start | bytes 884744 | tf_op jit(solution)/shard_map/ppermute | solution.py:30
  106.2 0.6 collective-permute-start.39
  106.9 1.2 collective-permute-start.31
  108.1 12.3 %collective-permute-done.37 = bf16[72,2048]{1,0:T(8,128)(2,1)S(1)} collective-permute-done((bf16[72,2048]{1,0:T(8,128)(2,1)S(1)}, bf16[72,2048]{1,0:T(8,128)(2,1)S(1)}, u32[]{:S(2)}, u32[]{:S(2)}) %collective-permute-start.37) | collective-permute-done | bytes 294944 | tf_op jit(solution)/shard_map/ppermute | solution.py:30
  120.4 5.6 %collective-permute-done.38 = bf16[72,2048]{1,0:T(8,128)(2,1)S(1)} collective-permute-done((bf16[72,2048]{1,0:T(8,128)(2,1)S(1)}, bf16[72,2048]{1,0:T(8,128)(2,1)S(1)}, u32[]{:S(2)}, u32[]{:S(2)}) %collective-permute-start.38) | collective-permute-done | bytes 294944 | tf_op jit(solution)/shard_map/ppermute | solution.py:30
  126.0 1.1 fusion.1
  (67 shorter events, 6.1 us)
Async XLA Ops:
  0.7 1.0 copy-start
  1.7 0.7 copy-start.4
  2.6 17.5 %collective-permute-start = (bf16[72,2048]{1,0:T(8,128)(2,1)S(1)}, bf16[72,2048]{1,0:T(8,128)(2,1)S(1)}, u32[]{:S(2)}, u32[]{:S(2)}) collective-permute-start(bf16[72,2048]{1,0:T(8,128)(2,1)S(1)} %pick.1.refs_0_), channel_id=1, source_target_pairs={{0,16},{4,20},{8,24},{12,28},{16,0},{20,4},{24,8},{28,12},{1,17},{... | collective-permute-start | bytes 884744 | tf_op jit(solution)/shard_map/ppermute | solution.py:30
  6.7 15.6 %collective-permute-start.4 = (bf16[72,2048]{1,0:T(8,128)(2,1)S(1)}, bf16[72,2048]{1,0:T(8,128)(2,1)S(1)}, u32[]{:S(2)}, u32[]{:S(2)}) collective-permute-start(bf16[72,2048]{1,0:T(8,128)(2,1)S(1)} %pick.1.refs_0_), channel_id=1, source_target_pairs={{0,4},{4,0},{8,12},{12,8},{16,20},{20,16},{24,28},{28,24},{1,5},{5... | collective-permute-start | bytes 884744 | tf_op jit(solution)/shard_map/ppermute | solution.py:30
  8.2 15.4 %collective-permute-start.5 = (bf16[72,2048]{1,0:T(8,128)(2,1)S(1)}, bf16[72,2048]{1,0:T(8,128)(2,1)S(1)}, u32[]{:S(2)}, u32[]{:S(2)}) collective-permute-start(bf16[72,2048]{1,0:T(8,128)(2,1)S(1)} %pick.1.refs_0_), channel_id=1, source_target_pairs={{0,8},{4,12},{8,0},{12,4},{16,24},{20,28},{24,16},{28,20},{1,9},{5... | collective-permute-start | bytes 884744 | tf_op jit(solution)/shard_map/ppermute | solution.py:30
  9.8 19.9 %collective-permute-start.6 = (bf16[72,2048]{1,0:T(8,128)(2,1)S(1)}, bf16[72,2048]{1,0:T(8,128)(2,1)S(1)}, u32[]{:S(2)}, u32[]{:S(2)}) collective-permute-start(bf16[72,2048]{1,0:T(8,128)(2,1)S(1)} %pick.1.refs_0_), channel_id=1, source_target_pairs={{0,12},{4,8},{8,4},{12,0},{16,28},{20,24},{24,20},{28,16},{1,13},{... | collective-permute-start | bytes 884744 | tf_op jit(solution)/shard_map/ppermute | solution.py:30
  20.1 18.7 %collective-permute-start.1 = (bf16[72,2048]{1,0:T(8,128)(2,1)S(1)}, bf16[72,2048]{1,0:T(8,128)(2,1)S(1)}, u32[]{:S(2)}, u32[]{:S(2)}) collective-permute-start(bf16[72,2048]{1,0:T(8,128)(2,1)S(1)} %collective-permute-done.refs_0_), channel_id=1, source_target_pairs={{0,4},{4,0},{8,12},{12,8},{16,20},{20,16},{24,28},{28,24},{1,5},{5... | collective-permute-start | bytes 884744 | tf_op jit(solution)/shard_map/ppermute | solution.py:30
  21.7 17.2 %collective-permute-start.2 = (bf16[72,2048]{1,0:T(8,128)(2,1)S(1)}, bf16[72,2048]{1,0:T(8,128)(2,1)S(1)}, u32[]{:S(2)}, u32[]{:S(2)}) collective-permute-start(bf16[72,2048]{1,0:T(8,128)(2,1)S(1)} %collective-permute-done.refs_0_), channel_id=1, source_target_pairs={{0,8},{4,12},{8,0},{12,4},{16,24},{20,28},{24,16},{28,20},{1,9},{5... | collective-permute-start | bytes 884744 | tf_op jit(solution)/shard_map/ppermute | solution.py:30
  22.3 18.3 %collective-permute-start.3 = (bf16[72,2048]{1,0:T(8,128)(2,1)S(1)}, bf16[72,2048]{1,0:T(8,128)(2,1)S(1)}, u32[]{:S(2)}, u32[]{:S(2)}) collective-permute-start(bf16[72,2048]{1,0:T(8,128)(2,1)S(1)} %collective-permute-done.refs_0_), channel_id=1, source_target_pairs={{0,12},{4,8},{8,4},{12,0},{16,28},{20,24},{24,20},{28,16},{1,13},{... | collective-permute-start | bytes 884744 | tf_op jit(solution)/shard_map/ppermute | solution.py:30
  29.7 0.7 copy-start.2
  31.5 9.0 %copy-start.3 = (f32[2048]{0:T(1024)S(1)}, f32[2048]{0:T(1024)}, u32[]{:S(2)}) copy-start(f32[2048]{0:T(1024)} %param.12) | copy-start | bytes 24580
  38.2 3.5 %collective-permute-start.7 = (bf16[208,512]{1,0:T(8,128)(2,1)S(1)}, bf16[208,512]{1,0:T(8,128)(2,1)S(1)}, u32[]{:S(2)}, u32[]{:S(2)}) collective-permute-start(bf16[208,512]{1,0:T(8,128)(2,1)S(1)} %get-tuple-element.63), channel_id=1, source_target_pairs={{0,1},{1,0},{2,3},{3,2},{4,5},{5,4},{6,7},{7,6},{8,9},{9,8},{10,11... | collective-permute-start | bytes 638984 | tf_op jit(solution)/shard_map/ppermute | solution.py:30
  38.3 3.4 %collective-permute-start.9 = (bf16[208,512]{1,0:T(8,128)(2,1)S(1)}, bf16[208,512]{1,0:T(8,128)(2,1)S(1)}, u32[]{:S(2)}, u32[]{:S(2)}) collective-permute-start(bf16[208,512]{1,0:T(8,128)(2,1)S(1)} %get-tuple-element.65), channel_id=1, source_target_pairs={{0,1},{1,0},{2,3},{3,2},{4,5},{5,4},{6,7},{7,6},{8,9},{9,8},{10,11... | collective-permute-start | bytes 638984 | tf_op jit(solution)/shard_map/ppermute | solution.py:30
  38.8 2.9 %collective-permute-start.10 = (bf16[208,384]{1,0:T(8,128)(2,1)S(1)}, bf16[208,384]{1,0:T(8,128)(2,1)S(1)}, u32[]{:S(2)}, u32[]{:S(2)}) collective-permute-start(bf16[208,384]{1,0:T(8,128)(2,1)S(1)} %get-tuple-element.66), channel_id=1, source_target_pairs={{0,1},{1,0},{2,3},{3,2},{4,5},{5,4},{6,7},{7,6},{8,9},{9,8},{10,11... | collective-permute-start | bytes 479240 | tf_op jit(solution)/shard_map/ppermute | solution.py:30
  38.9 2.8 %collective-permute-start.8 = (bf16[208,384]{1,0:T(8,128)(2,1)S(1)}, bf16[208,384]{1,0:T(8,128)(2,1)S(1)}, u32[]{:S(2)}, u32[]{:S(2)}) collective-permute-start(bf16[208,384]{1,0:T(8,128)(2,1)S(1)} %get-tuple-element.64), channel_id=1, source_target_pairs={{0,1},{1,0},{2,3},{3,2},{4,5},{5,4},{6,7},{7,6},{8,9},{9,8},{10,11... | collective-permute-start | bytes 479240 | tf_op jit(solution)/shard_map/ppermute | solution.py:30
  42.0 21.1 %collective-permute-start.15 = (bf16[208,1792]{1,0:T(8,128)(2,1)S(1)}, bf16[208,1792]{1,0:T(8,128)(2,1)S(1)}, u32[]{:S(2)}, u32[]{:S(2)}) collective-permute-start(bf16[208,1792]{1,0:T(8,128)(2,1)S(1)} %get-tuple-element.67.refs_0_), channel_id=1, source_target_pairs={{0,2},{1,3},{2,0},{3,1},{4,6},{5,7},{6,4},{7,5},{8,10},{9,11},{10,... | collective-permute-start | bytes 2236424 | tf_op jit(solution)/shard_map/ppermute | solution.py:30
  50.3 2.3 %collective-permute-start.11 = (bf16[208,512]{1,0:T(8,128)(2,1)S(1)}, bf16[208,512]{1,0:T(8,128)(2,1)S(1)}, u32[]{:S(2)}, u32[]{:S(2)}) collective-permute-start(bf16[208,512]{1,0:T(8,128)(2,1)S(1)} %get-tuple-element.69), channel_id=1, source_target_pairs={{0,1},{1,0},{2,3},{3,2},{4,5},{5,4},{6,7},{7,6},{8,9},{9,8},{10,11... | collective-permute-start | bytes 638984 | tf_op jit(solution)/shard_map/ppermute | solution.py:30
  50.4 2.2 %collective-permute-start.13 = (bf16[208,512]{1,0:T(8,128)(2,1)S(1)}, bf16[208,512]{1,0:T(8,128)(2,1)S(1)}, u32[]{:S(2)}, u32[]{:S(2)}) collective-permute-start(bf16[208,512]{1,0:T(8,128)(2,1)S(1)} %get-tuple-element.71), channel_id=1, source_target_pairs={{0,1},{1,0},{2,3},{3,2},{4,5},{5,4},{6,7},{7,6},{8,9},{9,8},{10,11... | collective-permute-start | bytes 638984 | tf_op jit(solution)/shard_map/ppermute | solution.py:30
  50.9 1.5 %collective-permute-start.12 = (bf16[208,384]{1,0:T(8,128)(2,1)S(1)}, bf16[208,384]{1,0:T(8,128)(2,1)S(1)}, u32[]{:S(2)}, u32[]{:S(2)}) collective-permute-start(bf16[208,384]{1,0:T(8,128)(2,1)S(1)} %get-tuple-element.70), channel_id=1, source_target_pairs={{0,1},{1,0},{2,3},{3,2},{4,5},{5,4},{6,7},{7,6},{8,9},{9,8},{10,11... | collective-permute-start | bytes 479240 | tf_op jit(solution)/shard_map/ppermute | solution.py:30
  51.0 1.6 %collective-permute-start.14 = (bf16[208,384]{1,0:T(8,128)(2,1)S(1)}, bf16[208,384]{1,0:T(8,128)(2,1)S(1)}, u32[]{:S(2)}, u32[]{:S(2)}) collective-permute-start(bf16[208,384]{1,0:T(8,128)(2,1)S(1)} %get-tuple-element.72), channel_id=1, source_target_pairs={{0,1},{1,0},{2,3},{3,2},{4,5},{5,4},{6,7},{7,6},{8,9},{9,8},{10,11... | collective-permute-start | bytes 479240 | tf_op jit(solution)/shard_map/ppermute | solution.py:30
  52.9 22.7 %collective-permute-start.20 = (bf16[208,1792]{1,0:T(8,128)(2,1)S(1)}, bf16[208,1792]{1,0:T(8,128)(2,1)S(1)}, u32[]{:S(2)}, u32[]{:S(2)}) collective-permute-start(bf16[208,1792]{1,0:T(8,128)(2,1)S(1)} %get-tuple-element.73.refs_0_), channel_id=1, source_target_pairs={{0,2},{1,3},{2,0},{3,1},{4,6},{5,7},{6,4},{7,5},{8,10},{9,11},{10,... | collective-permute-start | bytes 2236424 | tf_op jit(solution)/shard_map/ppermute | solution.py:30
  60.3 1.5 %collective-permute-start.17 = (bf16[208,384]{1,0:T(8,128)(2,1)S(1)}, bf16[208,384]{1,0:T(8,128)(2,1)S(1)}, u32[]{:S(2)}, u32[]{:S(2)}) collective-permute-start(bf16[208,384]{1,0:T(8,128)(2,1)S(1)} %get-tuple-element.77), channel_id=1, source_target_pairs={{0,1},{1,0},{2,3},{3,2},{4,5},{5,4},{6,7},{7,6},{8,9},{9,8},{10,11... | collective-permute-start | bytes 479240 | tf_op jit(solution)/shard_map/ppermute | solution.py:30
  60.4 2.8 %collective-permute-start.16 = (bf16[208,512]{1,0:T(8,128)(2,1)S(1)}, bf16[208,512]{1,0:T(8,128)(2,1)S(1)}, u32[]{:S(2)}, u32[]{:S(2)}) collective-permute-start(bf16[208,512]{1,0:T(8,128)(2,1)S(1)} %get-tuple-element.76), channel_id=1, source_target_pairs={{0,1},{1,0},{2,3},{3,2},{4,5},{5,4},{6,7},{7,6},{8,9},{9,8},{10,11... | collective-permute-start | bytes 638984 | tf_op jit(solution)/shard_map/ppermute | solution.py:30
  60.9 2.3 %collective-permute-start.18 = (bf16[208,512]{1,0:T(8,128)(2,1)S(1)}, bf16[208,512]{1,0:T(8,128)(2,1)S(1)}, u32[]{:S(2)}, u32[]{:S(2)}) collective-permute-start(bf16[208,512]{1,0:T(8,128)(2,1)S(1)} %get-tuple-element.78), channel_id=1, source_target_pairs={{0,1},{1,0},{2,3},{3,2},{4,5},{5,4},{6,7},{7,6},{8,9},{9,8},{10,11... | collective-permute-start | bytes 638984 | tf_op jit(solution)/shard_map/ppermute | solution.py:30
  61.8 1.4 %collective-permute-start.19 = (bf16[208,384]{1,0:T(8,128)(2,1)S(1)}, bf16[208,384]{1,0:T(8,128)(2,1)S(1)}, u32[]{:S(2)}, u32[]{:S(2)}) collective-permute-start(bf16[208,384]{1,0:T(8,128)(2,1)S(1)} %get-tuple-element.79), channel_id=1, source_target_pairs={{0,1},{1,0},{2,3},{3,2},{4,5},{5,4},{6,7},{7,6},{8,9},{9,8},{10,11... | collective-permute-start | bytes 479240 | tf_op jit(solution)/shard_map/ppermute | solution.py:30
  70.6 5.1 %collective-permute-start.21 = (bf16[208,896]{1,0:T(8,128)(2,1)S(1)}, bf16[208,896]{1,0:T(8,128)(2,1)S(1)}, u32[]{:S(2)}, u32[]{:S(2)}) collective-permute-start(bf16[208,896]{1,0:T(8,128)(2,1)S(1)} %get-tuple-element.83), channel_id=1, source_target_pairs={{0,1},{1,0},{2,3},{3,2},{4,5},{5,4},{6,7},{7,6},{8,9},{9,8},{10,11... | collective-permute-start | bytes 1118216 | tf_op jit(solution)/shard_map/ppermute | solution.py:30
  70.8 4.8 %collective-permute-start.22 = (bf16[208,896]{1,0:T(8,128)(2,1)S(1)}, bf16[208,896]{1,0:T(8,128)(2,1)S(1)}, u32[]{:S(2)}, u32[]{:S(2)}) collective-permute-start(bf16[208,896]{1,0:T(8,128)(2,1)S(1)} %get-tuple-element.84), channel_id=1, source_target_pairs={{0,1},{1,0},{2,3},{3,2},{4,5},{5,4},{6,7},{7,6},{8,9},{9,8},{10,11... | collective-permute-start | bytes 1118216 | tf_op jit(solution)/shard_map/ppermute | solution.py:30
  76.3 9.2 %collective-permute-start.25 = (bf16[208,896]{1,0:T(8,128)(2,1)S(1)}, bf16[208,896]{1,0:T(8,128)(2,1)S(1)}, u32[]{:S(2)}, u32[]{:S(2)}) collective-permute-start(bf16[208,896]{1,0:T(8,128)(2,1)S(1)} %get-tuple-element.85.refs_0_.refs_3_), channel_id=1, source_target_pairs={{0,2},{1,3},{2,0},{3,1},{4,6},{5,7},{6,4},{7,5},{8,10},{9,11},{10,... | collective-permute-start | bytes 1118216 | tf_op jit(solution)/shard_map/ppermute | solution.py:30
  77.9 1.7 %collective-permute-start.23 = (bf16[208,512]{1,0:T(8,128)(2,1)S(1)}, bf16[208,512]{1,0:T(8,128)(2,1)S(1)}, u32[]{:S(2)}, u32[]{:S(2)}) collective-permute-start(bf16[208,512]{1,0:T(8,128)(2,1)S(1)} %get-tuple-element.86), channel_id=1, source_target_pairs={{0,1},{1,0},{2,3},{3,2},{4,5},{5,4},{6,7},{7,6},{8,9},{9,8},{10,11... | collective-permute-start | bytes 638984 | tf_op jit(solution)/shard_map/ppermute | solution.py:30
  77.9 1.7 %collective-permute-start.24 = (bf16[208,384]{1,0:T(8,128)(2,1)S(1)}, bf16[208,384]{1,0:T(8,128)(2,1)S(1)}, u32[]{:S(2)}, u32[]{:S(2)}) collective-permute-start(bf16[208,384]{1,0:T(8,128)(2,1)S(1)} %get-tuple-element.87), channel_id=1, source_target_pairs={{0,1},{1,0},{2,3},{3,2},{4,5},{5,4},{6,7},{7,6},{8,9},{9,8},{10,11... | collective-permute-start | bytes 479240 | tf_op jit(solution)/shard_map/ppermute | solution.py:30
  84.9 13.8 %collective-permute-start.34 = (bf16[208,896]{1,0:T(8,128)(2,1)S(1)}, bf16[208,896]{1,0:T(8,128)(2,1)S(1)}, u32[]{:S(2)}, u32[]{:S(2)}) collective-permute-start(bf16[208,896]{1,0:T(8,128)(2,1)S(1)} %relay.4), channel_id=1, source_target_pairs={{0,2},{1,3},{2,0},{3,1},{4,6},{5,7},{6,4},{7,5},{8,10},{9,11},{10,... | collective-permute-start | bytes 1118216 | tf_op jit(solution)/shard_map/ppermute | solution.py:30
  85.6 1.8 %collective-permute-start.26 = (bf16[208,512]{1,0:T(8,128)(2,1)S(1)}, bf16[208,512]{1,0:T(8,128)(2,1)S(1)}, u32[]{:S(2)}, u32[]{:S(2)}) collective-permute-start(bf16[208,512]{1,0:T(8,128)(2,1)S(1)} %get-tuple-element.91), channel_id=1, source_target_pairs={{0,1},{1,0},{2,3},{3,2},{4,5},{5,4},{6,7},{7,6},{8,9},{9,8},{10,11... | collective-permute-start | bytes 638984 | tf_op jit(solution)/shard_map/ppermute | solution.py:30
  85.6 1.7 %collective-permute-start.27 = (bf16[208,384]{1,0:T(8,128)(2,1)S(1)}, bf16[208,384]{1,0:T(8,128)(2,1)S(1)}, u32[]{:S(2)}, u32[]{:S(2)}) collective-permute-start(bf16[208,384]{1,0:T(8,128)(2,1)S(1)} %get-tuple-element.92), channel_id=1, source_target_pairs={{0,1},{1,0},{2,3},{3,2},{4,5},{5,4},{6,7},{7,6},{8,9},{9,8},{10,11... | collective-permute-start | bytes 479240 | tf_op jit(solution)/shard_map/ppermute | solution.py:30
  86.1 6.7 %collective-permute-start.33 = (bf16[208,384]{1,0:T(8,128)(2,1)S(1)}, bf16[208,384]{1,0:T(8,128)(2,1)S(1)}, u32[]{:S(2)}, u32[]{:S(2)}) collective-permute-start(bf16[208,384]{1,0:T(8,128)(2,1)S(1)} %get-tuple-element.99), channel_id=1, source_target_pairs={{0,1},{1,0},{2,3},{3,2},{4,5},{5,4},{6,7},{7,6},{8,9},{9,8},{10,11... | collective-permute-start | bytes 479240 | tf_op jit(solution)/shard_map/ppermute | solution.py:30
  86.2 7.2 %collective-permute-start.32 = (bf16[208,512]{1,0:T(8,128)(2,1)S(1)}, bf16[208,512]{1,0:T(8,128)(2,1)S(1)}, u32[]{:S(2)}, u32[]{:S(2)}) collective-permute-start(bf16[208,512]{1,0:T(8,128)(2,1)S(1)} %get-tuple-element.98), channel_id=1, source_target_pairs={{0,1},{1,0},{2,3},{3,2},{4,5},{5,4},{6,7},{7,6},{8,9},{9,8},{10,11... | collective-permute-start | bytes 638984 | tf_op jit(solution)/shard_map/ppermute | solution.py:30
  89.9 16.3 %collective-permute-start.28 = (bf16[72,2048]{1,0:T(8,128)(2,1)S(1)}, bf16[72,2048]{1,0:T(8,128)(2,1)S(1)}, u32[]{:S(2)}, u32[]{:S(2)}) collective-permute-start(bf16[72,2048]{1,0:T(8,128)(2,1)S(1)} %get-tuple-element.94), channel_id=1, source_target_pairs={{0,12},{4,8},{8,4},{12,0},{16,28},{20,24},{24,20},{28,16},{1,13},{... | collective-permute-start | bytes 884744 | tf_op jit(solution)/shard_map/ppermute | solution.py:30
  91.1 15.7 %collective-permute-start.29 = (bf16[72,2048]{1,0:T(8,128)(2,1)S(1)}, bf16[72,2048]{1,0:T(8,128)(2,1)S(1)}, u32[]{:S(2)}, u32[]{:S(2)}) collective-permute-start(bf16[72,2048]{1,0:T(8,128)(2,1)S(1)} %get-tuple-element.95), channel_id=1, source_target_pairs={{0,8},{4,12},{8,0},{12,4},{16,24},{20,28},{24,16},{28,20},{1,9},{5... | collective-permute-start | bytes 884744 | tf_op jit(solution)/shard_map/ppermute | solution.py:30
  92.8 13.9 %collective-permute-start.30 = (bf16[72,2048]{1,0:T(8,128)(2,1)S(1)}, bf16[72,2048]{1,0:T(8,128)(2,1)S(1)}, u32[]{:S(2)}, u32[]{:S(2)}) collective-permute-start(bf16[72,2048]{1,0:T(8,128)(2,1)S(1)} %get-tuple-element.96), channel_id=1, source_target_pairs={{0,4},{4,0},{8,12},{12,8},{16,20},{20,16},{24,28},{28,24},{1,5},{5... | collective-permute-start | bytes 884744 | tf_op jit(solution)/shard_map/ppermute | solution.py:30
  98.7 27.2 %copy-start.1 = (bf16[96,2048]{1,0:T(8,128)(2,1)S(1)}, bf16[96,2048]{1,0:T(8,128)(2,1)}, u32[]{:S(2)}) copy-start(bf16[96,2048]{1,0:T(8,128)(2,1)} %tokens_ref.1) | copy-start | bytes 1179652
  98.7 27.2 %copy-start.5 = (s32[1,72]{1,0:T(1,128)S(1)}, s32[1,72]{1,0:T(1,128)}, u32[]{:S(2)}) copy-start(s32[1,72]{1,0:T(1,128)} %chosen_ref.1) | copy-start | bytes 868
  98.7 27.2 %copy-start.6 = (f32[96]{0:T(128)S(1)}, f32[96]{0:T(128)}, u32[]{:S(2)}) copy-start(f32[96]{0:T(128)} %param.11) | copy-start | bytes 1156
  98.8 1.8 %collective-permute-start.35 = (bf16[208,512]{1,0:T(8,128)(2,1)S(1)}, bf16[208,512]{1,0:T(8,128)(2,1)S(1)}, u32[]{:S(2)}, u32[]{:S(2)}) collective-permute-start(bf16[208,512]{1,0:T(8,128)(2,1)S(1)} %get-tuple-element.103), channel_id=1, source_target_pairs={{0,1},{1,0},{2,3},{3,2},{4,5},{5,4},{6,7},{7,6},{8,9},{9,8},{10,11... | collective-permute-start | bytes 638984 | tf_op jit(solution)/shard_map/ppermute | solution.py:30
  98.9 1.7 %collective-permute-start.36 = (bf16[208,384]{1,0:T(8,128)(2,1)S(1)}, bf16[208,384]{1,0:T(8,128)(2,1)S(1)}, u32[]{:S(2)}, u32[]{:S(2)}) collective-permute-start(bf16[208,384]{1,0:T(8,128)(2,1)S(1)} %get-tuple-element.104), channel_id=1, source_target_pairs={{0,1},{1,0},{2,3},{3,2},{4,5},{5,4},{6,7},{7,6},{8,9},{9,8},{10,11... | collective-permute-start | bytes 479240 | tf_op jit(solution)/shard_map/ppermute | solution.py:30
  103.2 17.2 %collective-permute-start.37 = (bf16[72,2048]{1,0:T(8,128)(2,1)S(1)}, bf16[72,2048]{1,0:T(8,128)(2,1)S(1)}, u32[]{:S(2)}, u32[]{:S(2)}) collective-permute-start(bf16[72,2048]{1,0:T(8,128)(2,1)S(1)} %get-tuple-element.106), channel_id=1, source_target_pairs={{0,12},{4,8},{8,4},{12,0},{16,28},{20,24},{24,20},{28,16},{1,13},{... | collective-permute-start | bytes 884744 | tf_op jit(solution)/shard_map/ppermute | solution.py:30
  104.4 21.5 %collective-permute-start.38 = (bf16[72,2048]{1,0:T(8,128)(2,1)S(1)}, bf16[72,2048]{1,0:T(8,128)(2,1)S(1)}, u32[]{:S(2)}, u32[]{:S(2)}) collective-permute-start(bf16[72,2048]{1,0:T(8,128)(2,1)S(1)} %get-tuple-element.107), channel_id=1, source_target_pairs={{0,8},{4,12},{8,0},{12,4},{16,24},{20,28},{24,16},{28,20},{1,9},{5... | collective-permute-start | bytes 884744 | tf_op jit(solution)/shard_map/ppermute | solution.py:30
  106.2 19.8 %collective-permute-start.39 = (bf16[72,2048]{1,0:T(8,128)(2,1)S(1)}, bf16[72,2048]{1,0:T(8,128)(2,1)S(1)}, u32[]{:S(2)}, u32[]{:S(2)}) collective-permute-start(bf16[72,2048]{1,0:T(8,128)(2,1)S(1)} %get-tuple-element.108), channel_id=1, source_target_pairs={{0,4},{4,0},{8,12},{12,8},{16,20},{20,16},{24,28},{28,24},{1,5},{5... | collective-permute-start | bytes 884744 | tf_op jit(solution)/shard_map/ppermute | solution.py:30
  106.9 19.0 %collective-permute-start.31 = (bf16[72,2048]{1,0:T(8,128)(2,1)S(1)}, bf16[72,2048]{1,0:T(8,128)(2,1)S(1)}, u32[]{:S(2)}, u32[]{:S(2)}) collective-permute-start(bf16[72,2048]{1,0:T(8,128)(2,1)S(1)} %sum.1), channel_id=1, source_target_pairs={{0,16},{4,20},{8,24},{12,28},{16,0},{20,4},{24,8},{28,12},{1,17},{... | collective-permute-start | bytes 884744 | tf_op jit(solution)/shard_map/ppermute | solution.py:30
